TPU v7x, 32 devices: a whole 2x2x4 slice. The times are simulated.
32 devices in a mesh: atoms: 8 (over y, x, core), grid: 4 (over z).
Axes of the slice: x: 2, y: 2, z: 4, core: 2. Of those that a mesh axis runs over, the one named last changes fastest.
Arguments:
- column_blocks: bfloat16 [256, 32, 256], P('atoms'), may hold values from -1 to 1
- onsite: bfloat16 [256, 256], P('atoms'), may hold values from -1 to 1
- neighbor_ids: int32 [256, 32], P('atoms'), may hold values from 0 to 255, as said below
- task_atoms: int32 [128, 32], P(('atoms', 'grid')), may hold values from 0 to 255, as said below
- chem_shift: float32 [128], P(('atoms', 'grid')), may hold values from -0.6 to 0.6
- basis_values: bfloat16 [128, 512, 1024], P(('atoms', 'grid')), may hold values from -0.59765625 to 0.59765625
- box_start: int32 [128], P(('atoms', 'grid')), may hold values from 0 to 252
- box_row: int32 [128], P(('atoms', 'grid')), may hold values from 0 to 16
- box_col: int32 [128], P(('atoms', 'grid')), may hold values from 0 to 112
Outputs:
- density_cols: bfloat16 [128, 512, 128], P(('atoms', 'grid'))
- rho: float32 [256, 32, 128], P('grid')
Inputs may be any that keep to these rules, and one draw needn't show every extreme that they name: `task_atoms`: row a of a device's block of 4 tasks, task t, names 8 atoms from each of 4 devices' columns. The atoms named by one device's tasks are all different; at most 16 of them lie in one device's columns, and some device's columns hold exactly 16 of them. `neighbor_ids`: an atom's 32 entries are different atoms, never the atom itself.
All inputs are finite; a program needn't handle non-finite values. Where the computation divides by a largest or mean magnitude, that divisor is 1e-20 or more.
Results may differ from a plain program's by a relative error of at most 0.007.
Values may be sent and summed in bfloat16 or wider, within the bound.
No kernel may reach another device: no remote copies, remote signals or barrier semaphores. Data moves between devices by JAX's collectives and lax.ppermute only.
A program may use at most 64 MiB of HBM per device.

v0:
```python
import jax
import jax.numpy as jnp
from jax import lax
from jax.sharding import PartitionSpec as P

BS = 16
KNB = 32
ITERS = 3
BOXP = 4
BOX_ROWS = 16
BOX_COLS = 16
GRID_ROWS = 32
GRID_COLS = 128
PL_SLAB = 64
CENTRAL = 128


exact_mode = lax.Precision.HIGHEST


def assemble(columns_in, onsite_in, links_in, members, offset):
    count = members.shape[0]
    matched = (links_in[None, :, :] == members[:, None, None]).astype(jnp.float32)
    blocks = columns_in.astype(jnp.float32).reshape(count, KNB, BS, BS)
    coupled = jnp.einsum("ijk,jkab->iajb", matched, blocks, precision=exact_mode)
    diagonal_part = jnp.einsum(
        "ij,jab->iajb",
        jnp.eye(count, dtype=jnp.float32),
        onsite_in.astype(jnp.float32).reshape(count, BS, BS),
        precision=exact_mode,
    )
    whole = (coupled + diagonal_part).reshape(count * BS, count * BS)
    return 0.5 * (whole + whole.T) - offset * jnp.eye(count * BS, dtype=jnp.float32)


def sign_columns(matrix):
    order_size = matrix.shape[0]
    identity = jnp.eye(order_size, dtype=jnp.float32)
    bound = jnp.max(jnp.sum(jnp.abs(matrix), axis=1)) + 1e-06
    iterate = (matrix / bound).astype(jnp.bfloat16)
    for iteration in range(ITERS - 1):
        squared = jnp.dot(iterate, iterate, preferred_element_type=jnp.float32)
        factor = (1.5 * identity - 0.5 * squared).astype(jnp.bfloat16)
        iterate = jnp.dot(iterate, factor, preferred_element_type=jnp.float32).astype(jnp.bfloat16)
    squared = jnp.dot(iterate, iterate[:, :CENTRAL], preferred_element_type=jnp.float32)
    factor = (1.5 * identity[:, :CENTRAL] - 0.5 * squared).astype(jnp.bfloat16)
    last_product = jnp.dot(iterate, factor, preferred_element_type=jnp.float32)
    return (0.5 * (identity[:, :CENTRAL] - last_product)).astype(jnp.bfloat16)


def collocate(density, basis_rows):
    weights = lax.dot_general(
        density, basis_rows, (((0,), (0,)), ((), ())), preferred_element_type=jnp.float32
    )
    values = jnp.sum(weights * basis_rows[:CENTRAL].astype(jnp.float32), axis=0)
    return values.reshape(BOXP, BOX_ROWS, BOX_COLS)


def on_device(
    column_blocks,
    onsite,
    neighbor_ids,
    task_atoms,
    chem_shift,
    basis_values,
    box_start,
    box_row,
    box_col,
):
    task_count, set_size = task_atoms.shape
    wanted_flat = task_atoms.reshape(-1)
    request_count = wanted_flat.shape[0]
    start_value = (
        jnp.zeros((request_count, KNB, BS * BS), jnp.bfloat16),
        jnp.zeros((request_count, BS * BS), jnp.bfloat16),
        jnp.zeros((request_count, KNB), jnp.int32),
    )
    blocks_piece = lax.all_gather(column_blocks, "atoms", axis=0, tiled=True)
    onsite_piece = lax.all_gather(onsite, "atoms", axis=0, tiled=True)
    links_piece = lax.all_gather(neighbor_ids, "atoms", axis=0, tiled=True)
    width_here = blocks_piece.shape[0]
    chosen = wanted_flat[:, None] == jnp.arange(width_here, dtype=jnp.int32)[None, :]
    chosen_half = chosen.astype(jnp.bfloat16)
    got_blocks = jnp.dot(
        chosen_half, blocks_piece.reshape(width_here, -1), preferred_element_type=jnp.float32
    )
    got_onsite = jnp.dot(chosen_half, onsite_piece, preferred_element_type=jnp.float32)
    got_links = jnp.dot(
        chosen.astype(jnp.float32), links_piece.astype(jnp.float32), precision=exact_mode
    )
    columns_in = got_blocks.astype(jnp.bfloat16).reshape(start_value[0].shape)
    onsite_in = got_onsite.astype(jnp.bfloat16)
    links_in = got_links.astype(jnp.int32)
    columns_in = columns_in.reshape(task_count, set_size, KNB, BS * BS)
    onsite_in = onsite_in.reshape(task_count, set_size, BS * BS)
    links_in = links_in.reshape(task_count, set_size, KNB)

    def one_task(members):
        block_cols, onsite_cols, link_cols, atom_ids, offset, basis_rows = members
        density = sign_columns(assemble(block_cols, onsite_cols, link_cols, atom_ids, offset))
        return (density, collocate(density, basis_rows))

    density_cols, boxes = lax.map(
        one_task, (columns_in, onsite_in, links_in, task_atoms, chem_shift, basis_values)
    )
    slab_count = lax.axis_size("grid")
    planes = PL_SLAB * slab_count

    def add_box(index, grid_now):
        corner = (box_start[index], box_row[index], box_col[index])
        current = lax.dynamic_slice(grid_now, corner, (BOXP, BOX_ROWS, BOX_COLS))
        return lax.dynamic_update_slice(grid_now, current + boxes[index], corner)

    partial_grid = lax.fori_loop(
        0, task_count, add_box, jnp.zeros((planes, GRID_ROWS, GRID_COLS), jnp.float32)
    )
    slab_piece = lax.psum_scatter(
        partial_grid.astype(jnp.bfloat16), "grid", scatter_dimension=0, tiled=True
    )
    slab_values = lax.psum(slab_piece, "atoms").astype(jnp.float32)
    return (density_cols, slab_values)


def solution(mesh):
    placed = (
        P("atoms", None, None),
        P("atoms", None),
        P("atoms", None),
        P(("atoms", "grid"), None),
        P(("atoms", "grid")),
        P(("atoms", "grid"), None, None),
        P(("atoms", "grid")),
        P(("atoms", "grid")),
        P(("atoms", "grid")),
    )
    return jax.shard_map(
        on_device,
        mesh=mesh,
        in_specs=placed,
        out_specs=(P(("atoms", "grid"), None, None), P("grid", None, None)),
        check_vma=False,
    )
```

profile of v0, /device:TPU:0, one launch (start us, length us, event | category | flops | bytes accessed | tf_op | source)
XLA Modules:
  0.0 350.5 jit_solution(15545532869085738837)
XLA Ops:
  8.7 10.8 %all_gather.10 = s32[256,32]{1,0:T(8,128)S(1)} all-gather(s32[32,32]{1,0:T(8,128)} %param.15), channel_id=1, replica_groups=mesh['atoms'=8,'grid'=4] {'atoms'}, dimensions={0}, use_global_device_ids=true | all-gather | bytes 36864 | tf_op jit(solution)/shard_map/all_gather | solution.py:80
  19.9 9.4 %all_gather.11 = bf16[256,256]{1,0:T(8,128)(2,1)S(1)} all-gather(bf16[32,256]{1,0:T(8,128)(2,1)} %param.14), channel_id=1, replica_groups=mesh['atoms'=8,'grid'=4] {'atoms'}, dimensions={0}, use_global_device_ids=true | all-gather | bytes 147456 | tf_op jit(solution)/shard_map/all_gather | solution.py:79
  29.5 20.4 %all-gather.2.cloned.1.call-done = bf16[256,32,256]{2,1,0:T(8,128)(2,1)} async-done(((bf16[32,32,256]{2,1,0:T(8,128)(2,1)}), bf16[256,32,256]{2,1,0:T(8,128)(2,1)}) %all-gather.2.cloned.1.call-update) | async-done | bytes 4194320 | tf_op jit(solution)/shard_map/all_gather | solution.py:78
  49.9 6.5 %copy.30 = bf16[32,8,32,256]{3,1,2,0:T(8,128)(2,1)S(1)} copy(bf16[32,8,32,256]{3,2,1,0:T(8,128)(2,1)} %bitcast.119) | data formatting | bytes 8388608
  57.7 131.3 %while.25 = (s32[]{:T(128)}, bf16[4,512,128]{2,1,0:T(8,128)(2,1)S(1)}, f32[4,4,16,16]{3,2,1,0:T(8,128)S(1)}, bf16[4,32,32,256]{3,2,1,0:T(8,128)(2,1)S(1)}, s32[4...) while((s32[]{:T(128)}, ...), condition=%wide.region_4.5_spmd, body=%wide.region_0.4_spmd.sunk | while | flops 1369342976 | bytes 36034668 | solution.py:103
  61.4 2.6 add_bitcast_fusion.2
  64.0 9.0 %copy.40 = f32[32,16,32,16]{3,2,1,0:T(8,128)} copy(f32[32,16,32,16]{0,3,1,2:T(8,128)} %add_bitcast_fusion.2) | data formatting | bytes 2097152 | tf_op jit(solution)/shard_map/while/body/eval_jaxpr/add | solution.py:32
  73.0 7.6 %reshape.41 = f32[512,512]{1,0:T(8,128)S(1)} reshape(f32[32,16,32,16]{3,2,1,0:T(8,128)} %copy.40) | data formatting | bytes 2097152 | tf_op jit(solution)/shard_map/while/body/eval_jaxpr/reshape | solution.py:32
  86.9 2.1 bitcast_dynamic-update-slice_fusion.2
  89.0 1.6 fusion.83
  94.2 2.6 add_bitcast_fusion.2
  96.8 9.0 %copy.40 = f32[32,16,32,16]{3,2,1,0:T(8,128)} copy(f32[32,16,32,16]{0,3,1,2:T(8,128)} %add_bitcast_fusion.2) | data formatting | bytes 2097152 | tf_op jit(solution)/shard_map/while/body/eval_jaxpr/add | solution.py:32
  105.8 7.6 %reshape.41 = f32[512,512]{1,0:T(8,128)S(1)} reshape(f32[32,16,32,16]{3,2,1,0:T(8,128)} %copy.40) | data formatting | bytes 2097152 | tf_op jit(solution)/shard_map/while/body/eval_jaxpr/reshape | solution.py:32
  119.6 2.1 bitcast_dynamic-update-slice_fusion.2
  126.9 2.6 add_bitcast_fusion.2
  129.6 9.0 %copy.40 = f32[32,16,32,16]{3,2,1,0:T(8,128)} copy(f32[32,16,32,16]{0,3,1,2:T(8,128)} %add_bitcast_fusion.2) | data formatting | bytes 2097152 | tf_op jit(solution)/shard_map/while/body/eval_jaxpr/add | solution.py:32
  138.6 7.6 %reshape.41 = f32[512,512]{1,0:T(8,128)S(1)} reshape(f32[32,16,32,16]{3,2,1,0:T(8,128)} %copy.40) | data formatting | bytes 2097152 | tf_op jit(solution)/shard_map/while/body/eval_jaxpr/reshape | solution.py:32
  152.4 2.1 bitcast_dynamic-update-slice_fusion.2
  159.7 2.6 add_bitcast_fusion.2
  162.3 9.0 %copy.40 = f32[32,16,32,16]{3,2,1,0:T(8,128)} copy(f32[32,16,32,16]{0,3,1,2:T(8,128)} %add_bitcast_fusion.2) | data formatting | bytes 2097152 | tf_op jit(solution)/shard_map/while/body/eval_jaxpr/add | solution.py:32
  171.3 7.6 %reshape.41 = f32[512,512]{1,0:T(8,128)S(1)} reshape(f32[32,16,32,16]{3,2,1,0:T(8,128)} %copy.40) | data formatting | bytes 2097152 | tf_op jit(solution)/shard_map/while/body/eval_jaxpr/reshape | solution.py:32
  185.2 2.1 bitcast_dynamic-update-slice_fusion.2
  189.1 2.5 broadcast_in_dim.22
  191.5 45.0 %while.26 = (s32[]{:T(128)}, f32[256,32,128]{2,1,0:T(8,128)}, s32[4]{0:T(128)S(1)}, s32[4]{0:T(128)S(1)}, s32[4]{0:T(128)S(1)}, /*index=5*/f32[4,4,16,16]{3,2,1,...) while((s32[]{:T(128)}, f32[256,32,128]{2,1,0:T(8,128)}, s32[4]{0:T(128)S(1)}, ...), condition=%wide.region_6.7_spmd, body=%wide.region_5.6_spmd.sunk | while | flops 1035 | bytes 20747 | solution.py:114
  200.0 2.7 dynamic_update_slice.22
  211.2 2.8 dynamic_update_slice.22
  222.5 2.8 dynamic_update_slice.22
  233.8 2.8 dynamic_update_slice.22
  236.5 4.0 %convert_element_type.57 = bf16[256,32,128]{2,1,0:T(8,128)(2,1)} convert(f32[256,32,128]{2,1,0:T(8,128)} %get-tuple-element.161) | non-fusion elementwise | flops 1048576 | bytes 6291456 | tf_op jit(solution)/shard_map/convert_element_type | solution.py:118
  240.6 43.9 %reduce-scatter.2.cloned.1.call-done = bf16[64,32,128]{2,1,0:T(8,128)(2,1)} async-done(((bf16[256,32,128]{2,1,0:T(8,128)(2,1)}), bf16[64,32,128]{2,1,0:T(8,128)(2,1)}) %reduce-scatter.2.cloned.1.call-update) | async-done | bytes 524304 | tf_op jit(solution)/shard_map/reduce_scatter | solution.py:117
  284.5 57.3 %all-reduce.2.cloned.1.call-done = bf16[64,32,128]{2,1,0:T(8,128)(2,1)} async-done(((bf16[64,32,128]{2,1,0:T(8,128)(2,1)}), bf16[64,32,128]{2,1,0:T(8,128)(2,1)}) %all-reduce.2.cloned.1.call-update) | async-done | bytes 524304 | tf_op jit(solution)/shard_map/psum | solution.py:120
  341.8 2.1 convert_element_type.58
  (127 shorter events, 55.4 us)
Async XLA Ops:
  7.2 42.7 %all-gather.2.cloned.1.call-start = ((), (), s32[]{:S(2)}) async-start(), calls=%async_computation.1 | async-start | bytes 4718592 | tf_op jit(solution)/shard_map/all_gather | solution.py:78
  7.9 276.6 %reduce-scatter.2.cloned.1.call-start = ((), (), s32[]{:S(2)}) async-start(), calls=%async_computation.2 | async-start | bytes 2621440 | tf_op jit(solution)/shard_map/reduce_scatter | solution.py:117
  56.4 1.4 copy-start.2
  57.9 1.3 copy-start
  85.2 5.5 %copy-start.1 = (bf16[4,32,32,256]{3,2,1,0:T(8,128)(2,1)S(1)}, bf16[4,32,32,256]{3,2,1,0:T(8,128)(2,1)}, u32[]{:S(2)}) copy-start(bf16[4,32,32,256]{3,2,1,0:T(8,128)(2,1)} %copy-done) | copy-start | bytes 6291460 | tf_op jit(solution)/shard_map/while
  90.7 1.3 copy-start
  118.0 5.5 %copy-start.1 = (bf16[4,32,32,256]{3,2,1,0:T(8,128)(2,1)S(1)}, bf16[4,32,32,256]{3,2,1,0:T(8,128)(2,1)}, u32[]{:S(2)}) copy-start(bf16[4,32,32,256]{3,2,1,0:T(8,128)(2,1)} %copy-done) | copy-start | bytes 6291460 | tf_op jit(solution)/shard_map/while
  123.5 1.3 copy-start
  150.7 5.5 %copy-start.1 = (bf16[4,32,32,256]{3,2,1,0:T(8,128)(2,1)S(1)}, bf16[4,32,32,256]{3,2,1,0:T(8,128)(2,1)}, u32[]{:S(2)}) copy-start(bf16[4,32,32,256]{3,2,1,0:T(8,128)(2,1)} %copy-done) | copy-start | bytes 6291460 | tf_op jit(solution)/shard_map/while
  156.2 1.3 copy-start
  183.5 5.5 %copy-start.1 = (bf16[4,32,32,256]{3,2,1,0:T(8,128)(2,1)S(1)}, bf16[4,32,32,256]{3,2,1,0:T(8,128)(2,1)}, u32[]{:S(2)}) copy-start(bf16[4,32,32,256]{3,2,1,0:T(8,128)(2,1)} %copy-done) | copy-start | bytes 6291460 | tf_op jit(solution)/shard_map/while
  189.0 51.5 %copy-start.6 = (bf16[4,512,128]{2,1,0:T(8,128)(2,1)}, bf16[4,512,128]{2,1,0:T(8,128)(2,1)S(1)}, u32[]{:S(2)}) copy-start(bf16[4,512,128]{2,1,0:T(8,128)(2,1)S(1)} %get-tuple-element.157) | copy-start | bytes 1572868
  189.0 2.5 copy-start.3
  189.0 2.5 copy-start.4
  189.0 2.5 copy-start.5
  240.6 101.2 %all-reduce.2.cloned.1.call-start = ((), (), s32[]{:S(2)}) async-start(), calls=%async_computation.3 | async-start | bytes 1048576 | tf_op jit(solution)/shard_map/psum | solution.py:120
Sparse Core Ops, SparseCore 0:
  9.9 39.9 all-gather.1
  240.7 43.7 reduce-scatter.1
  287.9 53.8 all-reduce.1
where the time goes:
time: 353 us; the launch traced here: 350 us
  waiting for transfers between devices  122 us (35%)
  local copies, waits for them, and re-layouts  113 us (32%)
  matrix products  39 us (11%)
  loops' own time  26.5 us (8%)
  blocking collectives  20.2 us (6%)
  other arithmetic  16.1 us (5%)
  between operations  13.8 us (4%)
    psum x1, waiting for transfers between devices, on_device(): slab_values = lax.psum(slab_piece, 'atoms').astype(jnp.float32)  57.3 us
    reduce_scatter x1, waiting for transfers between devices, on_device(): lax.psum_scatter(partial_grid.astype(jnp.bfloat16), 'grid', scatter_dimen...  43.9 us
    add x4, local copies, waits for them, and re-layouts, assemble(): whole = (coupled + diagonal_part).reshape(count * BS, count * BS)  36 us
    reshape x8, local copies, waits for them, and re-layouts, assemble(): whole = (coupled + diagonal_part).reshape(count * BS, count * BS)  31.7 us
    another operation x1, loops' own time, on_device(): lax.fori_loop(0, task_count, add_box, jnp.zeros((planes, GRID_ROWS, GRID_...  23.3 us
    all_gather x1, waiting for transfers between devices, on_device(): blocks_piece = lax.all_gather(column_blocks, 'atoms', axis=0, tiled=True)  20.4 us
    dot_general x8, matrix products, sign_columns(): jnp.dot(iterate, factor, preferred_element_type=jnp.float32)  12.3 us
    dynamic_update_slice x4, local copies, waits for them, and re-layouts, add_box(): return lax.dynamic_update_slice(grid_now, current + boxes[index], corner)  11 us
  transfers between devices with their start and end apart: 3, of which 3 were waited for; matrix products, arithmetic and copies ran while one was open for 0% of the time, Pallas kernels for 0%

commit v1 on v0

v1 whole, which is shorter than its diff:
```python
import functools

import jax
import jax.numpy as jnp
from jax import lax
from jax.experimental import pallas as pl
from jax.experimental.pallas import tpu as pltpu
from jax.sharding import PartitionSpec as P

BS = 16
ITERS = 3
BOXP = 4
BOX_ROWS = 16
BOX_COLS = 16
GRID_ROWS = 32
GRID_COLS = 128
PL_SLAB = 64
CENTRAL = 128

LOW = 8
LANES = 128


def doubled(value, axis, size, pairs):
    for step in pairs:
        other = lax.ppermute(value, axis, [(i, i ^ step) for i in range(size)])
        value = jnp.concatenate([value, other], axis=0)
    return value


def power_of_two(size):
    return size & (size - 1) == 0


def gather_everywhere(value):
    for axis in ("grid", "atoms"):
        size = lax.axis_size(axis)
        if power_of_two(size):
            steps = [1 << bit for bit in range(size.bit_length() - 1)][::-1]
            value = doubled(value, axis, size, steps)
        else:
            value = lax.all_gather(value, axis, axis=0, tiled=True)
    return value


def gather_columns(packed, holders):
    if holders < 2 or not power_of_two(holders):
        whole = lax.all_gather(packed, "atoms", axis=0)
        return [whole[i] for i in range(holders)], lambda holder: holder
    stages = holders.bit_length() - 2
    half = holders // 2

    def bit_of(device, stage):
        return 2 << (stages - 1 - stage if device & 1 else stage)

    pieces = [packed]
    for stage in range(stages):
        pairs = [(i, i ^ bit_of(i, stage)) for i in range(holders)]
        pieces = pieces + [lax.ppermute(piece, "atoms", pairs) for piece in pieces]
    swap = [(i, i ^ 1) for i in range(holders)]
    pieces = pieces + [lax.ppermute(piece, "atoms", swap) for piece in pieces]

    def slot(holder):
        apart = holder ^ lax.axis_index("atoms")
        plain = apart >> 1
        turned = sum((((plain >> bit) & 1) << (stages - 1 - bit) for bit in range(stages)), 0 * plain)
        return (apart & 1) * half + jnp.where(holder & 1 == 1, turned, plain)

    return pieces, slot


def iota(shape, axis):
    return lax.broadcasted_iota(jnp.int32, shape, axis)


def nn(left, right):
    return jnp.dot(left, right, preferred_element_type=jnp.float32)


def nt(left, right):
    return lax.dot_general(left, right, (((1,), (1,)), ((), ())), preferred_element_type=jnp.float32)


def density_kernel(
    holders,
    atoms_here,
    links,
    place_ref,
    shift_ref,
    slot_col_ref,
    member_col_ref,
    basis_ref,
    *rest,
):
    pieces = rest[:holders]
    density_ref, box_ref, cols, onsites, idents, ids_all, onsite_all, product, matrix, sems = rest[holders:]
    half = jnp.bfloat16
    task = pl.program_id(0)
    set_size = member_col_ref.shape[1]
    order = set_size * BS
    area = BS * BS
    block_rows = atoms_here * links
    groups = set_size // LOW

    @pl.when(task == 0)
    def _():
        copies = []
        for number, piece in enumerate(pieces):
            copies.append(
                pltpu.make_async_copy(
                    piece.at[pl.ds(0, block_rows)], cols.at[pl.ds(number * block_rows, block_rows)], sems.at[0, number]
                )
            )
            copies.append(
                pltpu.make_async_copy(
                    piece.at[pl.ds(block_rows, atoms_here)],
                    onsites.at[pl.ds(number * atoms_here, atoms_here)],
                    sems.at[1, number],
                )
            )
            copies.append(
                pltpu.make_async_copy(
                    piece.at[pl.ds(block_rows + atoms_here, atoms_here)],
                    idents.at[pl.ds(number * atoms_here, atoms_here)],
                    sems.at[2, number],
                )
            )
        for copy in copies:
            copy.start()
        for copy in copies:
            copy.wait()
        count = slot_col_ref.shape[0]
        chosen = (slot_col_ref[...] == iota((count, holders * atoms_here), 1)).astype(jnp.float32).astype(half)
        onsite_all[...] = nn(chosen, onsites[...])
        raw = nn(chosen, idents[...]).astype(half)
        source, target = iota((area, LOW * links), 0), iota((area, LOW * links), 1) % links
        spread = jnp.where(source == target, 1.0, jnp.where(source == links + target, 256.0, 0.0)).astype(half)
        ids_all[...] = nn(raw, spread)

    source, target = iota((area, area), 0), iota((area, area), 1)
    wanted = ((target // LANES) * LOW + target % LOW) * BS + (target % LANES) // LOW
    reorder = (source == wanted).astype(jnp.float32).astype(half)

    member = member_col_ref[0]
    lane_owner = iota((LOW, LOW * links), 1) // links
    own = lane_owner == iota((LOW, LOW * links), 0)
    owner_wide = iota((set_size, LOW * links), 1) // links
    lane = iota((set_size, LANES), 1)
    for group in range(groups):
        base = pl.multiple_of(task * set_size + group * LOW, LOW)
        ids_row = jnp.sum(jnp.where(own, ids_all[pl.ds(base, LOW), :], 0.0), axis=0, keepdims=True)
        match = (member == ids_row).astype(jnp.float32)
        spread_match = jnp.concatenate(
            [jnp.where(owner_wide == low, match, 0.0).astype(half) for low in range(LOW)], axis=0
        )
        stacked = jnp.concatenate(
            [
                cols[pl.ds(pl.multiple_of(place_ref[task, group * LOW + low] * links, links), links), :]
                for low in range(LOW)
            ],
            axis=0,
        )
        product[...] = nn(spread_match, stacked)
        for low in range(LOW):
            row = low * set_size + group * LOW + low
            product[pl.ds(row, 1), :] = onsite_all[pl.ds(base + low, 1), :]
        ordered = nn(product[...].astype(half), reorder)
        for high in range(area // LANES):
            tiles = [
                ordered[low * set_size : (low + 1) * set_size, high * LANES : (high + 1) * LANES] for low in range(LOW)
            ]
            for step in (1, 2, 4):
                keep = (lane & step) == 0
                for low in range(LOW):
                    if low & step:
                        continue
                    first, second = tiles[low], tiles[low | step]
                    tiles[low] = jnp.where(keep, first, pltpu.roll(second, step, 1))
                    tiles[low | step] = jnp.where(keep, pltpu.roll(first, LANES - step, 1), second)
            for low in range(LOW):
                for upper in range(set_size // LOW):
                    matrix[
                        pl.ds(upper * LANES + (high * LOW + low) * LOW, LOW), pl.ds(group * LANES, LANES)
                    ] = tiles[low][upper * LOW : (upper + 1) * LOW]

    on_diagonal = iota((order, order), 0) == iota((order, order), 1)
    identity = on_diagonal.astype(jnp.float32)
    mirrored = nt(identity.astype(half), matrix[...].astype(half))
    whole = 0.5 * (matrix[...] + mirrored) - shift_ref[task] * identity
    bound = jnp.max(jnp.sum(jnp.abs(whole), axis=0)) + 1e-06
    iterate = (whole / bound).astype(half)
    for _ in range(ITERS - 1):
        factor = (1.5 * identity - 0.5 * nn(iterate, iterate)).astype(half)
        iterate = nn(iterate, factor).astype(half)
    left = identity[:, :CENTRAL]
    factor = (1.5 * left - 0.5 * nn(iterate, iterate[:, :CENTRAL])).astype(half)
    turned = (0.5 * (left - nn(iterate, factor))).astype(half)

    source, target = iota((LANES, LANES), 0), iota((LANES, LANES), 1)
    back = (source == (target % BS) * LOW + target // BS).astype(jnp.float32).astype(half)
    front = (target == (source % BS) * LOW + source // BS).astype(jnp.float32).astype(half)
    mid = nn(turned, back).astype(half)
    tall = nt(front, turned).astype(half)
    wide = []
    for upper in range(order // LANES):
        part = pl.ds(upper * LANES, LANES)
        density_ref[0, part, :] = nn(front, mid[upper * LANES : (upper + 1) * LANES]).astype(half)
        wide.append(nn(tall[:, upper * LANES : (upper + 1) * LANES], back).astype(half))
    weights = nn(jnp.concatenate(wide, axis=1), basis_ref[0])
    values = jnp.sum(weights * basis_ref[0, :CENTRAL, :].astype(jnp.float32), axis=0, keepdims=True)
    rows = values.shape[1] // LANES
    box_ref[0] = jnp.concatenate(
        [values[:, row * LANES : (row + 1) * LANES] for row in range(rows)], axis=0
    ).astype(half)


def slab_kernel(start_ref, row_ref, col_ref, boxes_ref, slab_ref, work):
    planes = slab_ref.shape[0]
    work[...] = jnp.zeros_like(work)
    per_row = LANES // BOX_COLS
    lane, within = iota((per_row, LANES), 1), iota((per_row, LANES), 0)
    tiles_per_plane = BOX_ROWS // per_row

    def add(index, carry):
        first = start_ref[index]

        @pl.when(jnp.logical_and(first > -BOXP, first < planes))
        def _():
            row, col = row_ref[index], col_ref[index]
            box = pltpu.roll(boxes_ref[index].astype(jnp.float32), col, 1)
            inside = jnp.logical_and(lane >= col, lane < col + BOX_COLS)
            for plane in range(BOXP):
                for part in range(tiles_per_plane):
                    at = plane * tiles_per_plane + part
                    moved = jnp.broadcast_to(box[at : at + 1, :], (per_row, LANES))
                    step = 1
                    while step < per_row:
                        turned = pltpu.roll(moved, LANES - step * BOX_COLS, 1)
                        moved = jnp.where(within & step == 0, moved, turned)
                        step *= 2
                    moved = jnp.where(inside, moved, 0.0)
                    where = pl.ds(row + part * per_row, per_row)
                    work[first + BOXP - 1 + plane, where, :] += moved
        return carry

    lax.fori_loop(0, start_ref.shape[0], add, 0)
    slab_ref[...] = work[pl.ds(BOXP - 1, planes)]


def on_device(
    column_blocks,
    onsite,
    neighbor_ids,
    task_atoms,
    chem_shift,
    basis_values,
    box_start,
    box_row,
    box_col,
):
    half = jnp.bfloat16
    holders = lax.axis_size("atoms")
    atoms_here, links, area = column_blocks.shape
    tasks, set_size = task_atoms.shape
    order, points = basis_values.shape[1:]
    corners = gather_everywhere(jnp.stack([box_start, box_row, box_col], axis=1))
    idents = jnp.concatenate([neighbor_ids % 256, neighbor_ids // 256], axis=1).astype(half)
    idents = jnp.pad(idents, ((0, 0), (0, area - 2 * links)))
    packed = jnp.concatenate([column_blocks.reshape(atoms_here * links, area), onsite, idents], axis=0)
    pieces, slot = gather_columns(packed, holders)
    place = slot(task_atoms // atoms_here) * atoms_here + task_atoms % atoms_here
    everything = pl.BlockSpec(memory_space=pl.ANY)
    scalars = pl.BlockSpec(memory_space=pltpu.SMEM)
    density, boxes = pl.pallas_call(
        functools.partial(density_kernel, holders, atoms_here, links),
        grid=(tasks,),
        in_specs=[
            scalars,
            scalars,
            pl.BlockSpec((tasks * set_size, 1), lambda t: (0, 0)),
            pl.BlockSpec((1, set_size, 1), lambda t: (t, 0, 0)),
            pl.BlockSpec((1, order, points), lambda t: (t, 0, 0)),
        ]
        + [everything] * holders,
        out_specs=[
            pl.BlockSpec((1, order, CENTRAL), lambda t: (t, 0, 0)),
            pl.BlockSpec((1, points // LANES, LANES), lambda t: (t, 0, 0)),
        ],
        out_shape=[
            jax.ShapeDtypeStruct((tasks, order, CENTRAL), half),
            jax.ShapeDtypeStruct((tasks, points // LANES, LANES), half),
        ],
        scratch_shapes=[
            pltpu.VMEM((holders * atoms_here * links, area), half),
            pltpu.VMEM((holders * atoms_here, area), half),
            pltpu.VMEM((holders * atoms_here, area), half),
            pltpu.VMEM((tasks * set_size, LOW * links), jnp.float32),
            pltpu.VMEM((tasks * set_size, area), jnp.float32),
            pltpu.VMEM((LOW * set_size, area), jnp.float32),
            pltpu.VMEM((order, order), jnp.float32),
            pltpu.SemaphoreType.DMA((3, holders)),
        ],
        compiler_params=pltpu.CompilerParams(vmem_limit_bytes=52 * 1024 * 1024),
    )(
        place,
        chem_shift,
        place.reshape(-1, 1),
        task_atoms.astype(jnp.float32)[:, :, None],
        basis_values,
        *pieces,
    )
    all_boxes = gather_everywhere(boxes)
    starts = corners[:, 0] - lax.axis_index("grid") * PL_SLAB
    slab = pl.pallas_call(
        slab_kernel,
        in_specs=[scalars, scalars, scalars, pl.BlockSpec(memory_space=pltpu.VMEM)],
        out_specs=pl.BlockSpec(memory_space=pltpu.VMEM),
        out_shape=jax.ShapeDtypeStruct((PL_SLAB, GRID_ROWS, GRID_COLS), jnp.float32),
        scratch_shapes=[pltpu.VMEM((PL_SLAB + 2 * (BOXP - 1), GRID_ROWS, GRID_COLS), jnp.float32)],
        compiler_params=pltpu.CompilerParams(vmem_limit_bytes=32 * 1024 * 1024),
    )(starts, corners[:, 1], corners[:, 2], all_boxes)
    return density, slab


def solution(mesh):
    placed = (
        P("atoms", None, None),
        P("atoms", None),
        P("atoms", None),
        P(("atoms", "grid"), None),
        P(("atoms", "grid")),
        P(("atoms", "grid"), None, None),
        P(("atoms", "grid")),
        P(("atoms", "grid")),
        P(("atoms", "grid")),
    )
    return jax.shard_map(
        on_device,
        mesh=mesh,
        in_specs=placed,
        out_specs=(P(("atoms", "grid"), None, None), P("grid", None, None)),
        check_vma=False,
    )
```

time: 353 us -> 94.7 us (0.27)
  the two profiles are of different devices: /device:TPU:0 before, /device:TPU:11 now
where the time goes in v1:
time: 94.7 us; the launch traced here: 94.3 us
  Pallas kernels  34.9 us (37%)
  waiting for transfers between devices  30.3 us (32%)
  starting transfers between devices  24.6 us (26%)
  other arithmetic  2.22 us (2%)
  local copies, waits for them, and re-layouts  1.45 us (2%)
    pallas_call x1, Pallas kernels, on_device(): pl.pallas_call(functools.partial(density_kernel, holders, atoms_here, lin...  22 us
    ppermute x10, waiting for transfers between devices, doubled(): other = lax.ppermute(value, axis, [(i, i ^ step) for i in range(size)])  16.8 us
    ppermute x10, starting transfers between devices, doubled(): other = lax.ppermute(value, axis, [(i, i ^ step) for i in range(size)])  14.8 us
    ppermute x3, waiting for transfers between devices, gather_columns(): pieces = pieces + [lax.ppermute(piece, 'atoms', pairs) for piece in pieces]  13.5 us
    pallas_call x1, Pallas kernels, on_device(): pl.pallas_call(slab_kernel, in_specs=[scalars, scalars, scalars, pl.Block...  13 us
    ppermute x4, starting transfers between devices, gather_columns(): pieces = pieces + [lax.ppermute(piece, 'atoms', swap) for piece in pieces]  8.24 us
  transfers between devices with their start and end apart: 17, of which 11 were waited for; matrix products, arithmetic and copies ran while one was open for 1% of the time, Pallas kernels for 0%

profile of v1, /device:TPU:11, one launch (start us, length us, event | category | flops | bytes accessed | tf_op | source)
XLA Modules:
  0.0 94.3 jit_solution(14398680612937991927)
XLA Ops:
  0.7 0.8 fusion.2
  1.5 1.1 %pad_maximum_fusion.rest_0_ = bf16[1088,256]{1,0:T(8,128)(2,1)S(1)} fusion(bf16[32,256]{1,0:T(8,128)(2,1)S(1)} %fusion.4, bf16[32,256]{1,0:T(8,128)(2,1)} %param.10, bf16[1024,256]{1,0:T(8,128)(2,1)} %bitcast.12), kind=kLoop, calls=%fused_computation | loop fusion | flops 1671168 | bytes 1114112 | tf_op jit(solution)/shard_map/concatenate | solution.py:269
  2.6 1.3 %collective-permute-start = (bf16[1088,256]{1,0:T(8,128)(2,1)S(1)}, bf16[1088,256]{1,0:T(8,128)(2,1)S(1)}, u32[]{:S(2)}, u32[]{:S(2)}) collective-permute-start(bf16[1088,256]{1,0:T(8,128)(2,1)S(1)} %pad_maximum_fusion.rest_0_), channel_id=1, source_target_pairs={{0,8},{4,20},{8,0},{12,28},{16,24},{20,4},{24,16},{28,12},{1,9},{5... | collective-permute-start | bytes 1671176 | tf_op jit(solution)/shard_map/ppermute | solution.py:59
  3.9 0.3 collective-permute-start.1
  4.2 11.4 %collective-permute-done.rest_1_ = bf16[1088,256]{1,0:T(8,128)(2,1)S(1)} collective-permute-done((bf16[1088,256]{1,0:T(8,128)(2,1)S(1)}, bf16[1088,256]{1,0:T(8,128)(2,1)S(1)}, u32[]{:S(2)}, u32[]{:S(2)}) %collective-permute-start) | collective-permute-done | bytes 557088 | tf_op jit(solution)/shard_map/ppermute | solution.py:59
  15.6 3.9 %collective-permute-start.3 = (bf16[1088,256]{1,0:T(8,128)(2,1)S(1)}, bf16[1088,256]{1,0:T(8,128)(2,1)S(1)}, u32[]{:S(2)}, u32[]{:S(2)}) collective-permute-start(bf16[1088,256]{1,0:T(8,128)(2,1)S(1)} %pad_maximum_fusion.rest_0_), channel_id=1, source_target_pairs={{0,4},{4,0},{8,12},{12,8},{16,20},{20,16},{24,28},{28,24},{1,5},{5... | collective-permute-start | bytes 1671176 | tf_op jit(solution)/shard_map/ppermute | solution.py:61
  19.5 2.4 %collective-permute-start.7 = (s32[4,3]{0,1:T(4,128)S(1)}, s32[4,3]{0,1:T(4,128)S(1)}, u32[]{:S(2)}, u32[]{:S(2)}) collective-permute-start(s32[4,3]{0,1:T(4,128)S(1)} %pad_add_fusion), channel_id=1, source_target_pairs={{0,2},{1,3},{2,0},{3,1},{4,6},{5,7},{6,4},{7,5},{8,10},{9,11},{10,... | collective-permute-start | bytes 152 | tf_op jit(solution)/shard_map/ppermute | solution.py:26
  21.9 0.3 collective-permute-start.4
  22.2 0.2 collective-permute-start.5
  22.4 2.1 %collective-permute-done.2.rest_3_ = bf16[1088,256]{1,0:T(8,128)(2,1)S(1)} collective-permute-done((bf16[1088,256]{1,0:T(8,128)(2,1)S(1)}, bf16[1088,256]{1,0:T(8,128)(2,1)S(1)}, u32[]{:S(2)}, u32[]{:S(2)}) %collective-permute-start.2) | collective-permute-done | bytes 557088 | tf_op jit(solution)/shard_map/ppermute | solution.py:59
  24.5 3.8 %collective-permute-start.6 = (bf16[1088,256]{1,0:T(8,128)(2,1)S(1)}, bf16[1088,256]{1,0:T(8,128)(2,1)}, u32[]{:S(2)}, u32[]{:S(2)}) collective-permute-start(bf16[1088,256]{1,0:T(8,128)(2,1)S(1)} %collective-permute-done.2.rest_3_), channel_id=1, source_target_pairs={{0,4},{4,0},{8,12},{12,8},{16,20},{20,16},{24,28},{28,24},{1,5},{5... | collective-permute-start | bytes 1671176 | tf_op jit(solution)/shard_map/ppermute | solution.py:61
  28.4 0.2 collective-permute-start.8
  28.6 2.3 %collective-permute-done.8 = s32[8,3]{0,1:T(4,128)S(1)} collective-permute-done((s32[8,3]{0,1:T(4,128)S(1)}, s32[8,3]{0,1:T(4,128)S(1)}, u32[]{:S(2)}, u32[]{:S(2)}) %collective-permute-start.8) | collective-permute-done | bytes 128 | tf_op jit(solution)/shard_map/ppermute | solution.py:26
  30.9 0.4 collective-permute-start.9
  31.3 2.0 %collective-permute-done.9 = s32[16,3]{0,1:T(4,128)S(1)} collective-permute-done((s32[16,3]{0,1:T(4,128)S(1)}, s32[16,3]{0,1:T(4,128)S(1)}, u32[]{:S(2)}, u32[]{:S(2)}) %collective-permute-start.9) | collective-permute-done | bytes 224 | tf_op jit(solution)/shard_map/ppermute | solution.py:26
  33.4 0.3 collective-permute-start.10
  33.7 2.2 %collective-permute-done.10 = s32[32,3]{0,1:T(4,128)S(1)} collective-permute-done((s32[32,3]{0,1:T(4,128)S(1)}, s32[32,3]{0,1:T(4,128)S(1)}, u32[]{:S(2)}, u32[]{:S(2)}) %collective-permute-start.10) | collective-permute-done | bytes 416 | tf_op jit(solution)/shard_map/ppermute | solution.py:26
  35.9 3.5 %collective-permute-start.11 = (s32[64,3]{0,1:T(4,128)S(1)}, s32[64,3]{0,1:T(4,128)S(1)}, u32[]{:S(2)}, u32[]{:S(2)}) collective-permute-start(s32[64,3]{0,1:T(4,128)S(1)} %concatenate.50), channel_id=1, source_target_pairs={{0,4},{4,0},{8,12},{12,8},{16,20},{20,16},{24,28},{28,24},{1,5},{5... | collective-permute-start | bytes 2312 | tf_op jit(solution)/shard_map/ppermute | solution.py:26
  39.6 0.6 collective-permute-done.11
  40.4 0.8 copy-done.2
  41.1 0.2 copy-done.3
  41.3 22.0 %shard_map.104 = (bf16[4,512,128]{2,1,0:T(8,128)(2,1)}, bf16[4,8,128]{2,1,0:T(8,128)(2,1)S(1)}) custom-call(s32[4,32]{1,0:T(4,128)S(1)} %get-tuple-element.22.place_ref, f32[4]{0:T(128)S(1)} %copy-done, s32[128,1]{1,0:T(8,128)S(1)} %reshape.14.slot_col_ref, f32[4,32,1]{2,1,0:T(8,128)S(1)} %copy.12.member_col_ref, bf16[4,512,1024]{2,1,0:T(8,128)(2,1)} %basis_ref.1, ...), custom_call_target="tpu_custom_call" | custom-call | tf_op jit(solution)/shard_map/pallas_call | solution.py:274
  63.3 2.4 %collective-permute-start.12 = (bf16[4,8,128]{2,1,0:T(8,128)(2,1)S(1)}, bf16[4,8,128]{2,1,0:T(8,128)(2,1)S(1)}, u32[]{:S(2)}, u32[]{:S(2)}) collective-permute-start(bf16[4,8,128]{2,1,0:T(8,128)(2,1)S(1)} %get-tuple-element.5), channel_id=1, source_target_pairs={{0,2},{1,3},{2,0},{3,1},{4,6},{5,7},{6,4},{7,5},{8,10},{9,11},{10,... | collective-permute-start | bytes 24584 | tf_op jit(solution)/shard_map/ppermute | solution.py:26
  65.7 1.1 %collective-permute-done.12 = bf16[4,8,128]{2,1,0:T(8,128)(2,1)S(1)} collective-permute-done((bf16[4,8,128]{2,1,0:T(8,128)(2,1)S(1)}, bf16[4,8,128]{2,1,0:T(8,128)(2,1)S(1)}, u32[]{:S(2)}, u32[]{:S(2)}) %collective-permute-start.12) | collective-permute-done | bytes 8224 | tf_op jit(solution)/shard_map/ppermute | solution.py:26
  67.0 2.4 %collective-permute-done.13 = bf16[8,8,128]{2,1,0:T(8,128)(2,1)S(1)} collective-permute-done((bf16[8,8,128]{2,1,0:T(8,128)(2,1)S(1)}, bf16[8,8,128]{2,1,0:T(8,128)(2,1)S(1)}, u32[]{:S(2)}, u32[]{:S(2)}) %collective-permute-start.13) | collective-permute-done | bytes 16416 | tf_op jit(solution)/shard_map/ppermute | solution.py:26
  69.4 0.4 collective-permute-start.14
  69.8 2.3 %collective-permute-done.14 = bf16[16,8,128]{2,1,0:T(8,128)(2,1)S(1)} collective-permute-done((bf16[16,8,128]{2,1,0:T(8,128)(2,1)S(1)}, bf16[16,8,128]{2,1,0:T(8,128)(2,1)S(1)}, u32[]{:S(2)}, u32[]{:S(2)}) %collective-permute-start.14) | collective-permute-done | bytes 32800 | tf_op jit(solution)/shard_map/ppermute | solution.py:26
  72.2 0.3 collective-permute-start.15
  72.5 3.0 %collective-permute-done.15 = bf16[32,8,128]{2,1,0:T(8,128)(2,1)S(1)} collective-permute-done((bf16[32,8,128]{2,1,0:T(8,128)(2,1)S(1)}, bf16[32,8,128]{2,1,0:T(8,128)(2,1)S(1)}, u32[]{:S(2)}, u32[]{:S(2)}) %collective-permute-start.15) | collective-permute-done | bytes 65568 | tf_op jit(solution)/shard_map/ppermute | solution.py:26
  75.6 4.8 %collective-permute-start.16 = (bf16[64,8,128]{2,1,0:T(8,128)(2,1)S(1)}, bf16[64,8,128]{2,1,0:T(8,128)(2,1)S(1)}, u32[]{:S(2)}, u32[]{:S(2)}) collective-permute-start(bf16[64,8,128]{2,1,0:T(8,128)(2,1)S(1)} %get-tuple-element.6), channel_id=1, source_target_pairs={{0,4},{4,0},{8,12},{12,8},{16,20},{20,16},{24,28},{28,24},{1,5},{5... | collective-permute-start | bytes 393224 | tf_op jit(solution)/shard_map/ppermute | solution.py:26
  80.4 1.0 %collective-permute-done.16 = bf16[64,8,128]{2,1,0:T(8,128)(2,1)S(1)} collective-permute-done((bf16[64,8,128]{2,1,0:T(8,128)(2,1)S(1)}, bf16[64,8,128]{2,1,0:T(8,128)(2,1)S(1)}, u32[]{:S(2)}, u32[]{:S(2)}) %collective-permute-start.16) | collective-permute-done | bytes 131104 | tf_op jit(solution)/shard_map/ppermute | solution.py:26
  81.4 13.0 %shard_map.105 = f32[64,32,128]{2,1,0:T(8,128)} custom-call(s32[128]{0:T(128)S(1)} %get-tuple-element.20.start_ref, s32[128]{0:T(128)S(1)} %get-tuple-element.19.row_ref, s32[128]{0:T(128)S(1)} %get-tuple-element.18.col_ref, bf16[128,8,128]{2,1,0:T(8,128)(2,1)S(1)} %constant_dynamic-update-slice_fusion.5.boxes_ref), custom_call_target="tpu_custom_call" | custom-call | tf_op jit(solution)/shard_map/pallas_call | solution.py:314
  (42 shorter events, 1.1 us)
Async XLA Ops:
  0.6 18.9 %copy-start.6 = (s32[4]{0:T(128)S(1)}, s32[4]{0:T(128)}, u32[]{:S(2)}) copy-start(s32[4]{0:T(128)} %param.15) | copy-start | bytes 52
  0.6 18.9 %copy-start.5 = (s32[4]{0:T(128)S(1)}, s32[4]{0:T(128)}, u32[]{:S(2)}) copy-start(s32[4]{0:T(128)} %param.16) | copy-start | bytes 52
  0.7 18.8 %copy-start.4 = (s32[4]{0:T(128)S(1)}, s32[4]{0:T(128)}, u32[]{:S(2)}) copy-start(s32[4]{0:T(128)} %param.17) | copy-start | bytes 52
  0.7 38.7 %copy-start.7 = (s32[4,32]{1,0:T(4,128)S(1)}, s32[4,32]{1,0:T(4,128)}, u32[]{:S(2)}) copy-start(s32[4,32]{1,0:T(4,128)} %param.12) | copy-start | bytes 1540
  0.7 40.7 %copy-start = (f32[4]{0:T(128)S(1)}, f32[4]{0:T(128)}, u32[]{:S(2)}) copy-start(f32[4]{0:T(128)} %shift_ref.1) | copy-start | bytes 52
  2.6 13.0 %collective-permute-start = (bf16[1088,256]{1,0:T(8,128)(2,1)S(1)}, bf16[1088,256]{1,0:T(8,128)(2,1)S(1)}, u32[]{:S(2)}, u32[]{:S(2)}) collective-permute-start(bf16[1088,256]{1,0:T(8,128)(2,1)S(1)} %pad_maximum_fusion.rest_0_), channel_id=1, source_target_pairs={{0,8},{4,20},{8,0},{12,28},{16,24},{20,4},{24,16},{28,12},{1,9},{5... | collective-permute-start | bytes 1671176 | tf_op jit(solution)/shard_map/ppermute | solution.py:59
  3.9 18.2 %collective-permute-start.1 = (bf16[1088,256]{1,0:T(8,128)(2,1)S(1)}, bf16[1088,256]{1,0:T(8,128)(2,1)S(1)}, u32[]{:S(2)}, u32[]{:S(2)}) collective-permute-start(bf16[1088,256]{1,0:T(8,128)(2,1)S(1)} %pad_maximum_fusion.rest_0_), channel_id=1, source_target_pairs={{0,16},{4,12},{8,24},{12,4},{16,0},{20,28},{24,8},{28,20},{1,17},{... | collective-permute-start | bytes 1671176 | tf_op jit(solution)/shard_map/ppermute | solution.py:59
  15.6 8.8 %collective-permute-start.2 = (bf16[1088,256]{1,0:T(8,128)(2,1)S(1)}, bf16[1088,256]{1,0:T(8,128)(2,1)S(1)}, u32[]{:S(2)}, u32[]{:S(2)}) collective-permute-start(bf16[1088,256]{1,0:T(8,128)(2,1)S(1)} %collective-permute-done.rest_1_), channel_id=1, source_target_pairs={{0,16},{4,12},{8,24},{12,4},{16,0},{20,28},{24,8},{28,20},{1,17},{... | collective-permute-start | bytes 1671176 | tf_op jit(solution)/shard_map/ppermute | solution.py:59
  15.6 24.7 %collective-permute-start.3 = (bf16[1088,256]{1,0:T(8,128)(2,1)S(1)}, bf16[1088,256]{1,0:T(8,128)(2,1)S(1)}, u32[]{:S(2)}, u32[]{:S(2)}) collective-permute-start(bf16[1088,256]{1,0:T(8,128)(2,1)S(1)} %pad_maximum_fusion.rest_0_), channel_id=1, source_target_pairs={{0,4},{4,0},{8,12},{12,8},{16,20},{20,16},{24,28},{28,24},{1,5},{5... | collective-permute-start | bytes 1671176 | tf_op jit(solution)/shard_map/ppermute | solution.py:61
  19.5 8.8 %collective-permute-start.7 = (s32[4,3]{0,1:T(4,128)S(1)}, s32[4,3]{0,1:T(4,128)S(1)}, u32[]{:S(2)}, u32[]{:S(2)}) collective-permute-start(s32[4,3]{0,1:T(4,128)S(1)} %pad_add_fusion), channel_id=1, source_target_pairs={{0,2},{1,3},{2,0},{3,1},{4,6},{5,7},{6,4},{7,5},{8,10},{9,11},{10,... | collective-permute-start | bytes 152 | tf_op jit(solution)/shard_map/ppermute | solution.py:26
  21.9 18.4 %collective-permute-start.4 = (bf16[1088,256]{1,0:T(8,128)(2,1)S(1)}, bf16[1088,256]{1,0:T(8,128)(2,1)S(1)}, u32[]{:S(2)}, u32[]{:S(2)}) collective-permute-start(bf16[1088,256]{1,0:T(8,128)(2,1)S(1)} %collective-permute-done.rest_1_), channel_id=1, source_target_pairs={{0,4},{4,0},{8,12},{12,8},{16,20},{20,16},{24,28},{28,24},{1,5},{5... | collective-permute-start | bytes 1671176 | tf_op jit(solution)/shard_map/ppermute | solution.py:61
  22.2 18.2 %collective-permute-start.5 = (bf16[1088,256]{1,0:T(8,128)(2,1)S(1)}, bf16[1088,256]{1,0:T(8,128)(2,1)}, u32[]{:S(2)}, u32[]{:S(2)}) collective-permute-start(bf16[1088,256]{1,0:T(8,128)(2,1)S(1)} %collective-permute-done.1.rest_2_), channel_id=1, source_target_pairs={{0,4},{4,0},{8,12},{12,8},{16,20},{20,16},{24,28},{28,24},{1,5},{5... | collective-permute-start | bytes 1671176 | tf_op jit(solution)/shard_map/ppermute | solution.py:61
  24.4 15.9 %copy-start.1 = (bf16[1088,256]{1,0:T(8,128)(2,1)}, bf16[1088,256]{1,0:T(8,128)(2,1)S(1)}, u32[]{:S(2)}) copy-start(bf16[1088,256]{1,0:T(8,128)(2,1)S(1)} %collective-permute-done.2.rest_3_) | copy-start | bytes 1671172
  24.5 15.9 %collective-permute-start.6 = (bf16[1088,256]{1,0:T(8,128)(2,1)S(1)}, bf16[1088,256]{1,0:T(8,128)(2,1)}, u32[]{:S(2)}, u32[]{:S(2)}) collective-permute-start(bf16[1088,256]{1,0:T(8,128)(2,1)S(1)} %collective-permute-done.2.rest_3_), channel_id=1, source_target_pairs={{0,4},{4,0},{8,12},{12,8},{16,20},{20,16},{24,28},{28,24},{1,5},{5... | collective-permute-start | bytes 1671176 | tf_op jit(solution)/shard_map/ppermute | solution.py:61
  28.4 2.4 %collective-permute-start.8 = (s32[8,3]{0,1:T(4,128)S(1)}, s32[8,3]{0,1:T(4,128)S(1)}, u32[]{:S(2)}, u32[]{:S(2)}) collective-permute-start(s32[8,3]{0,1:T(4,128)S(1)} %pad_add_fusion.1), channel_id=1, source_target_pairs={{0,1},{1,0},{2,3},{3,2},{4,5},{5,4},{6,7},{7,6},{8,9},{9,8},{10,11... | collective-permute-start | bytes 296 | tf_op jit(solution)/shard_map/ppermute | solution.py:26
  30.9 2.4 %collective-permute-start.9 = (s32[16,3]{0,1:T(4,128)S(1)}, s32[16,3]{0,1:T(4,128)S(1)}, u32[]{:S(2)}, u32[]{:S(2)}) collective-permute-start(s32[16,3]{0,1:T(4,128)S(1)} %pad_add_fusion.2), channel_id=1, source_target_pairs={{0,16},{4,20},{8,24},{12,28},{16,0},{20,4},{24,8},{28,12},{1,17},{... | collective-permute-start | bytes 584 | tf_op jit(solution)/shard_map/ppermute | solution.py:26
  33.4 2.4 %collective-permute-start.10 = (s32[32,3]{0,1:T(4,128)S(1)}, s32[32,3]{0,1:T(4,128)S(1)}, u32[]{:S(2)}, u32[]{:S(2)}) collective-permute-start(s32[32,3]{0,1:T(4,128)S(1)} %pad_add_fusion.3), channel_id=1, source_target_pairs={{0,8},{4,12},{8,0},{12,4},{16,24},{20,28},{24,16},{28,20},{1,9},{5... | collective-permute-start | bytes 1160 | tf_op jit(solution)/shard_map/ppermute | solution.py:26
  35.9 4.3 %collective-permute-start.11 = (s32[64,3]{0,1:T(4,128)S(1)}, s32[64,3]{0,1:T(4,128)S(1)}, u32[]{:S(2)}, u32[]{:S(2)}) collective-permute-start(s32[64,3]{0,1:T(4,128)S(1)} %concatenate.50), channel_id=1, source_target_pairs={{0,4},{4,0},{8,12},{12,8},{16,20},{20,16},{24,28},{28,24},{1,5},{5... | collective-permute-start | bytes 2312 | tf_op jit(solution)/shard_map/ppermute | solution.py:26
  40.3 0.8 copy-start.2
  40.3 1.0 %copy-start.3 = (bf16[1088,256]{1,0:T(8,128)(2,1)}, bf16[1088,256]{1,0:T(8,128)(2,1)S(1)}, u32[]{:S(2)}) copy-start(bf16[1088,256]{1,0:T(8,128)(2,1)S(1)} %collective-permute-done.4.rest_5_) | copy-start | bytes 1671172
  63.3 3.5 %collective-permute-start.12 = (bf16[4,8,128]{2,1,0:T(8,128)(2,1)S(1)}, bf16[4,8,128]{2,1,0:T(8,128)(2,1)S(1)}, u32[]{:S(2)}, u32[]{:S(2)}) collective-permute-start(bf16[4,8,128]{2,1,0:T(8,128)(2,1)S(1)} %get-tuple-element.5), channel_id=1, source_target_pairs={{0,2},{1,3},{2,0},{3,1},{4,6},{5,7},{6,4},{7,5},{8,10},{9,11},{10,... | collective-permute-start | bytes 24584 | tf_op jit(solution)/shard_map/ppermute | solution.py:26
  66.8 2.6 %collective-permute-start.13 = (bf16[8,8,128]{2,1,0:T(8,128)(2,1)S(1)}, bf16[8,8,128]{2,1,0:T(8,128)(2,1)S(1)}, u32[]{:S(2)}, u32[]{:S(2)}) collective-permute-start(bf16[8,8,128]{2,1,0:T(8,128)(2,1)S(1)} %pad_maximum_fusion.3), channel_id=1, source_target_pairs={{0,1},{1,0},{2,3},{3,2},{4,5},{5,4},{6,7},{7,6},{8,9},{9,8},{10,11... | collective-permute-start | bytes 49160 | tf_op jit(solution)/shard_map/ppermute | solution.py:26
  69.4 2.8 %collective-permute-start.14 = (bf16[16,8,128]{2,1,0:T(8,128)(2,1)S(1)}, bf16[16,8,128]{2,1,0:T(8,128)(2,1)S(1)}, u32[]{:S(2)}, u32[]{:S(2)}) collective-permute-start(bf16[16,8,128]{2,1,0:T(8,128)(2,1)S(1)} %pad_maximum_fusion.2), channel_id=1, source_target_pairs={{0,16},{4,20},{8,24},{12,28},{16,0},{20,4},{24,8},{28,12},{1,17},{... | collective-permute-start | bytes 98312 | tf_op jit(solution)/shard_map/ppermute | solution.py:26
  72.2 3.4 %collective-permute-start.15 = (bf16[32,8,128]{2,1,0:T(8,128)(2,1)S(1)}, bf16[32,8,128]{2,1,0:T(8,128)(2,1)S(1)}, u32[]{:S(2)}, u32[]{:S(2)}) collective-permute-start(bf16[32,8,128]{2,1,0:T(8,128)(2,1)S(1)} %pad_maximum_fusion.1), channel_id=1, source_target_pairs={{0,8},{4,12},{8,0},{12,4},{16,24},{20,28},{24,16},{28,20},{1,9},{5... | collective-permute-start | bytes 196616 | tf_op jit(solution)/shard_map/ppermute | solution.py:26
  75.6 5.8 %collective-permute-start.16 = (bf16[64,8,128]{2,1,0:T(8,128)(2,1)S(1)}, bf16[64,8,128]{2,1,0:T(8,128)(2,1)S(1)}, u32[]{:S(2)}, u32[]{:S(2)}) collective-permute-start(bf16[64,8,128]{2,1,0:T(8,128)(2,1)S(1)} %get-tuple-element.6), channel_id=1, source_target_pairs={{0,4},{4,0},{8,12},{12,8},{16,20},{20,16},{24,28},{28,24},{1,5},{5... | collective-permute-start | bytes 393224 | tf_op jit(solution)/shard_map/ppermute | solution.py:26

commit v2 on v1

v2 whole, which is shorter than its diff:
```python
import functools

import jax
import jax.numpy as jnp
from jax import lax
from jax.experimental import pallas as pl
from jax.experimental.pallas import tpu as pltpu
from jax.sharding import PartitionSpec as P

BS = 16
ITERS = 3
BOXP = 4
BOX_ROWS = 16
BOX_COLS = 16
GRID_ROWS = 32
GRID_COLS = 128
PL_SLAB = 64
CENTRAL = 128

LOW = 8
LANES = 128
BATCH = 4
STAGGER = 1


def doubled(value, axis, size, pairs):
    for step in pairs:
        other = lax.ppermute(value, axis, [(i, i ^ step) for i in range(size)])
        value = jnp.concatenate([value, other], axis=0)
    return value


def power_of_two(size):
    return size & (size - 1) == 0


def gather_everywhere(value):
    for axis in ("grid", "atoms"):
        size = lax.axis_size(axis)
        if power_of_two(size):
            steps = [1 << bit for bit in range(size.bit_length() - 1)][::-1]
            value = doubled(value, axis, size, steps)
        else:
            value = lax.all_gather(value, axis, axis=0, tiled=True)
    return value


def gather_columns(packed, holders):
    if holders < 2 or not power_of_two(holders):
        whole = lax.all_gather(packed, "atoms", axis=0)
        return [whole[i] for i in range(holders)], lambda holder: holder
    stages = holders.bit_length() - 2
    half = holders // 2

    def bit_of(device, stage):
        return 2 << (stages - 1 - stage if device & 1 else stage)

    pieces = [packed]
    for stage in range(stages):
        pairs = [(i, i ^ bit_of(i, stage)) for i in range(holders)]
        pieces = pieces + [lax.ppermute(piece, "atoms", pairs) for piece in pieces]
    swap = [(i, i ^ 1) for i in range(holders)]
    pieces = pieces + [lax.ppermute(piece, "atoms", swap) for piece in pieces]

    def slot(holder):
        apart = holder ^ lax.axis_index("atoms")
        plain = apart >> 1
        turned = sum((((plain >> bit) & 1) << (stages - 1 - bit) for bit in range(stages)), 0 * plain)
        return (apart & 1) * half + jnp.where(holder & 1 == 1, turned, plain)

    return pieces, slot


def iota(shape, axis):
    return lax.broadcasted_iota(jnp.int32, shape, axis)


def nn(left, right):
    return jnp.dot(left, right, preferred_element_type=jnp.float32)


def nt(left, right):
    return lax.dot_general(left, right, (((1,), (1,)), ((), ())), preferred_element_type=jnp.float32)


def plus_diagonal(value, scale, amount):
    here = iota((LANES, LANES), 0) == iota((LANES, LANES), 1)
    diagonal = jnp.where(here, amount, 0.0)
    rows, columns = value.shape
    out = []
    for row in range(0, rows, LANES):
        part = scale * value[row : row + LANES]
        if row < columns:
            pieces = [part[:, :row], part[:, row : row + LANES] + diagonal, part[:, row + LANES :]]
            part = jnp.concatenate([piece for piece in pieces if piece.shape[1]], axis=1)
        out.append(part)
    return jnp.concatenate(out, axis=0)


def density_kernel(
    holders,
    atoms_here,
    links,
    place_ref,
    shift_ref,
    start_ref,
    row_ref,
    col_ref,
    slot_col_ref,
    member_col_ref,
    basis_hbm,
    *rest,
):
    pieces = rest[:holders]
    (
        density_hbm,
        box_ref,
        cols,
        onsites,
        idents,
        basis,
        density,
        ids_all,
        onsite_all,
        product,
        matrix,
        sems,
        basis_sems,
        density_sems,
    ) = rest[holders:]
    half = jnp.bfloat16
    tasks, set_size = member_col_ref.shape[:2]
    order = set_size * BS
    area = BS * BS
    block_rows = atoms_here * links
    groups = set_size // LOW

    copies = []
    for number, piece in enumerate(pieces):
        spots = (
            (cols, 0, block_rows),
            (onsites, block_rows, atoms_here),
            (idents, block_rows + atoms_here, atoms_here),
        )
        for kind, (target, first, count) in enumerate(spots):
            copies.append(
                pltpu.make_async_copy(
                    piece.at[pl.ds(first, count)], target.at[pl.ds(number * count, count)], sems.at[kind, number]
                )
            )
    loads = [pltpu.make_async_copy(basis_hbm.at[t], basis.at[t], basis_sems.at[t]) for t in range(tasks)]
    stores = [pltpu.make_async_copy(density.at[t], density_hbm.at[t], density_sems.at[t]) for t in range(tasks)]
    for copy in copies:
        copy.start()
    for copy in copies:
        copy.wait()
    for load in loads:
        load.start()
    count = tasks * set_size
    chosen = (slot_col_ref[...] == iota((count, holders * atoms_here), 1)).astype(jnp.float32).astype(half)
    onsite_all[...] = nn(chosen, onsites[...])
    raw = nn(chosen, idents[...]).astype(half)
    source, target = iota((area, LOW * links), 0), iota((area, LOW * links), 1) % links
    spread = jnp.where(source == target, 1.0, jnp.where(source == links + target, 256.0, 0.0)).astype(half)
    ids_all[...] = nn(raw, spread)

    source, target = iota((area, area), 0), iota((area, area), 1)
    wanted = ((target // LANES) * LOW + target % LOW) * BS + (target % LANES) // LOW
    reorder = (source == wanted).astype(jnp.float32).astype(half)
    identity = (iota((order, order), 0) == iota((order, order), 1)).astype(jnp.float32).astype(half)
    source, target = iota((LANES, LANES), 0), iota((LANES, LANES), 1)
    back = (source == (target % BS) * LOW + target // BS).astype(jnp.float32).astype(half)
    front = (target == (source % BS) * LOW + source // BS).astype(jnp.float32).astype(half)

    lane_owner = iota((LOW, LOW * links), 1) // links
    own = lane_owner == iota((LOW, LOW * links), 0)
    owner_wide = iota((set_size, LOW * links), 1) // links
    lane = iota((set_size, LANES), 1)
    boxes = {}

    def assemble(task, group):
        base = task * set_size + group * LOW
        ids_row = jnp.sum(jnp.where(own, ids_all[pl.ds(base, LOW), :], 0.0), axis=0, keepdims=True)
        match = (member_col_ref[task] == ids_row).astype(jnp.float32)
        spread_match = jnp.concatenate(
            [jnp.where(owner_wide == low, match, 0.0).astype(half) for low in range(LOW)], axis=0
        )
        stacked = jnp.concatenate(
            [
                cols[pl.ds(pl.multiple_of(place_ref[task, group * LOW + low] * links, links), links), :]
                for low in range(LOW)
            ],
            axis=0,
        )
        spot = product.at[task, group % 2]
        spot[...] = nn(spread_match, stacked)
        for low in range(LOW):
            row = low * set_size + group * LOW + low
            spot[pl.ds(row, 1), :] = onsite_all[pl.ds(base + low, 1), :]
        ordered = nn(spot[...].astype(half), reorder)
        for high in range(area // LANES):
            tiles = [
                ordered[low * set_size : (low + 1) * set_size, high * LANES : (high + 1) * LANES] for low in range(LOW)
            ]
            for step in (1, 2, 4):
                keep = (lane & step) == 0
                for low in range(LOW):
                    if low & step:
                        continue
                    first, second = tiles[low], tiles[low | step]
                    tiles[low] = jnp.where(keep, first, pltpu.roll(second, step, 1))
                    tiles[low | step] = jnp.where(keep, pltpu.roll(first, LANES - step, 1), second)
            for low in range(LOW):
                for upper in range(set_size // LOW):
                    matrix[
                        task,
                        pl.ds(upper * LANES + (high * LOW + low) * LOW, LOW),
                        pl.ds(group * LANES, LANES),
                    ] = tiles[low][upper * LOW : (upper + 1) * LOW]

    def steps_of(task):
        for group in range(groups):
            assemble(task, group)
            yield
        mirrored = nt(identity, matrix[task].astype(half))
        yield
        whole = plus_diagonal(matrix[task] + mirrored, 0.5, -shift_ref[task])
        bound = jnp.max(jnp.sum(jnp.abs(whole), axis=0, keepdims=True), axis=1, keepdims=True) + 1e-06
        iterate = (whole * (1.0 / bound)).astype(half)
        yield
        for _ in range(ITERS - 1):
            factor = plus_diagonal(nn(iterate, iterate), -0.5, 1.5).astype(half)
            yield
            iterate = nn(iterate, factor).astype(half)
            yield
        factor = plus_diagonal(nn(iterate, iterate[:, :CENTRAL]), -0.5, 1.5).astype(half)
        yield
        turned = plus_diagonal(nn(iterate, factor), -0.5, 0.5).astype(half)
        yield
        mid = nn(turned, back).astype(half)
        tall = nt(front, turned).astype(half)
        wide = []
        for upper in range(order // LANES):
            part = slice(upper * LANES, (upper + 1) * LANES)
            density[task, part, :] = nn(front, mid[part]).astype(half)
            wide.append(nn(tall[:, part], back).astype(half))
        stores[task].start()
        yield
        loads[task].wait()
        weights = nn(jnp.concatenate(wide, axis=1), basis[task])
        values = jnp.sum(weights * basis[task, :CENTRAL, :].astype(jnp.float32), axis=0, keepdims=True)
        rows = values.shape[1] // LANES
        box = jnp.concatenate([values[:, row * LANES : (row + 1) * LANES] for row in range(rows)], axis=0)
        boxes[task] = pltpu.roll(box, col_ref[task], 1)
        yield

    running = []
    waiting = [steps_of(task) for task in range(tasks)]
    tick = 0
    while running or waiting:
        if waiting and tick % STAGGER == 0:
            running.append(waiting.pop(0))
        for steps in list(running):
            if next(steps, running) is running:
                running.remove(steps)
        tick += 1

    lane = iota((1, LANES), 1)
    corner = jnp.zeros((1, LANES), jnp.float32)
    for task in range(tasks):
        numbers = (start_ref[task] // PL_SLAB, start_ref[task] % PL_SLAB, row_ref[task], col_ref[task])
        for place, number in enumerate(numbers):
            corner = jnp.where(lane == task * len(numbers) + place, number.astype(jnp.float32), corner)
    box_rows = [boxes[task] for task in range(tasks)]
    rest_rows = box_ref.shape[0] - sum(box.shape[0] for box in box_rows) - 1
    box_ref[...] = jnp.concatenate(
        box_rows + [corner, jnp.zeros((rest_rows, LANES), jnp.float32)], axis=0
    ).astype(half)
    for store in stores:
        store.wait()


def slab_kernel(tasks, slab_number_ref, boxes_ref, slab_ref, work, wide, unfolded, corner_vmem, corners, chosen, sem):
    planes = slab_ref.shape[0]
    devices = boxes_ref.shape[0]
    per_row = LANES // BOX_COLS
    box_rows = BOXP * BOX_ROWS // per_row
    corner_at = tasks * box_rows
    numbers = boxes_ref[:, corner_at : corner_at + LOW, :].astype(jnp.float32)[:, 0, :].astype(jnp.int32)
    first = (pltpu.roll(numbers, 1, 1) - slab_number_ref[0]) * planes + numbers
    corner_vmem[...] = jnp.where(iota(numbers.shape, 1) % 4 == 1, first, numbers)
    copy = pltpu.make_async_copy(corner_vmem, corners, sem)
    copy.start()
    work[...] = jnp.zeros_like(work)
    wide[...] = boxes_ref[:, :corner_at, :].astype(jnp.float32).reshape(devices * tasks, box_rows, LANES)
    lane = iota((per_row, LANES), 1)
    copy.wait()

    def look(device, count):
        for task in range(tasks):
            first = corners[device, 4 * task + 1]
            chosen[count] = device * tasks + task
            count += jnp.logical_and(first > -BOXP, first < planes).astype(jnp.int32)
        return count

    count = lax.fori_loop(0, devices, look, 0)
    for extra in range(BATCH):
        chosen[count + extra] = -1

    def add(turn, carry):
        places = []
        for part in range(BATCH):
            index = chosen[turn * BATCH + part]
            box = jnp.maximum(index, 0)
            device, task = box // tasks, box % tasks
            first = jnp.where(index < 0, planes + BOXP - 1, corners[device, 4 * task + 1])
            row, col = corners[device, 4 * task + 2], corners[device, 4 * task + 3]
            places.append((first + BOXP - 1, row))
            inside = jnp.logical_and(lane >= col, lane < col + BOX_COLS)
            rows = wide[box]
            for within in range(per_row):
                turned = rows if within == 0 else pltpu.roll(rows, LANES - within * BOX_COLS, 1)
                unfolded[part, pl.ds(within * box_rows, box_rows), :] = jnp.where(inside, turned, 0.0)
        for part, (plane, row) in enumerate(places):
            for at in range(box_rows):
                tile = unfolded[part, pl.ds(at, per_row, stride=box_rows), :]
                where = pl.ds(row + at % (BOX_ROWS // per_row) * per_row, per_row)
                work[plane + at // (BOX_ROWS // per_row), where, :] += tile
        return carry

    lax.fori_loop(0, (count + BATCH - 1) // BATCH, add, 0)
    slab_ref[...] = work[pl.ds(BOXP - 1, planes)]


def on_device(
    column_blocks,
    onsite,
    neighbor_ids,
    task_atoms,
    chem_shift,
    basis_values,
    box_start,
    box_row,
    box_col,
):
    half = jnp.bfloat16
    holders = lax.axis_size("atoms")
    atoms_here, links, area = column_blocks.shape
    tasks, set_size = task_atoms.shape
    order, points = basis_values.shape[1:]
    idents = jnp.concatenate([neighbor_ids % 256, neighbor_ids // 256], axis=1).astype(half)
    idents = jnp.pad(idents, ((0, 0), (0, area - 2 * links)))
    packed = jnp.concatenate([column_blocks.reshape(atoms_here * links, area), onsite, idents], axis=0)
    pieces, slot = gather_columns(packed, holders)
    place = slot(task_atoms // atoms_here) * atoms_here + task_atoms % atoms_here
    everything = pl.BlockSpec(memory_space=pl.ANY)
    scalars = pl.BlockSpec(memory_space=pltpu.SMEM)
    vectors = pl.BlockSpec(memory_space=pltpu.VMEM)
    box_rows = (tasks * points // LANES + 1 + 15) // 16 * 16
    column_bytes = packed.size * holders * 2
    density, boxes = pl.pallas_call(
        functools.partial(density_kernel, holders, atoms_here, links),
        in_specs=[scalars] * 5 + [vectors] * 2 + [pl.BlockSpec(memory_space=pltpu.HBM)] + [everything] * holders,
        out_specs=[everything, vectors],
        out_shape=[
            jax.ShapeDtypeStruct((tasks, order, CENTRAL), half),
            jax.ShapeDtypeStruct((box_rows, LANES), half),
        ],
        scratch_shapes=[
            pltpu.VMEM((holders * atoms_here * links, area), half),
            pltpu.VMEM((holders * atoms_here, area), half),
            pltpu.VMEM((holders * atoms_here, area), half),
            pltpu.VMEM((tasks, order, points), half),
            pltpu.VMEM((tasks, order, CENTRAL), half),
            pltpu.VMEM((tasks * set_size, LOW * links), jnp.float32),
            pltpu.VMEM((tasks * set_size, area), jnp.float32),
            pltpu.VMEM((tasks, 2, LOW * set_size, area), jnp.float32),
            pltpu.VMEM((tasks, order, order), jnp.float32),
            pltpu.SemaphoreType.DMA((3, holders)),
            pltpu.SemaphoreType.DMA((tasks,)),
            pltpu.SemaphoreType.DMA((tasks,)),
        ],
        compiler_params=pltpu.CompilerParams(vmem_limit_bytes=48 * 1024 * 1024),
    )(
        place,
        chem_shift,
        box_start,
        box_row,
        box_col,
        place.reshape(-1, 1),
        task_atoms.astype(jnp.float32)[:, :, None],
        basis_values,
        *pieces,
    )
    all_boxes = gather_everywhere(boxes[None])
    slab_number = lax.axis_index("grid").astype(jnp.int32).reshape(1)
    slab = pl.pallas_call(
        functools.partial(slab_kernel, tasks),
        in_specs=[scalars, vectors],
        out_specs=vectors,
        out_shape=jax.ShapeDtypeStruct((PL_SLAB, GRID_ROWS, GRID_COLS), jnp.float32),
        scratch_shapes=[
            pltpu.VMEM((PL_SLAB + 3 * BOXP, GRID_ROWS, GRID_COLS), jnp.float32),
            pltpu.VMEM((all_boxes.shape[0] * tasks, points // LANES, LANES), jnp.float32),
            pltpu.VMEM((BATCH, points // BOX_COLS, LANES), jnp.float32),
            pltpu.VMEM((all_boxes.shape[0], LANES), jnp.int32),
            pltpu.SMEM((all_boxes.shape[0], LANES), jnp.int32),
            pltpu.SMEM((all_boxes.shape[0] * tasks + BATCH,), jnp.int32),
            pltpu.SemaphoreType.DMA,
        ],
        compiler_params=pltpu.CompilerParams(vmem_limit_bytes=32 * 1024 * 1024),
    )(slab_number, all_boxes)
    return density, slab


def solution(mesh):
    placed = (
        P("atoms", None, None),
        P("atoms", None),
        P("atoms", None),
        P(("atoms", "grid"), None),
        P(("atoms", "grid")),
        P(("atoms", "grid"), None, None),
        P(("atoms", "grid")),
        P(("atoms", "grid")),
        P(("atoms", "grid")),
    )
    return jax.shard_map(
        on_device,
        mesh=mesh,
        in_specs=placed,
        out_specs=(P(("atoms", "grid"), None, None), P("grid", None, None)),
        check_vma=False,
    )
```

time: 94.7 us -> 68.7 us (0.73)
  the two profiles are of different devices: /device:TPU:11 before, /device:TPU:0 now
where the time goes in v2:
time: 68.7 us; the launch traced here: 68.3 us
  waiting for transfers between devices  31.6 us (46%)
  Pallas kernels  18.5 us (27%)
  starting transfers between devices  15.1 us (22%)
  other arithmetic  1.99 us (3%)
  between operations  0.77 us (1%)
    ppermute x3, waiting for transfers between devices, gather_columns(): pieces = pieces + [lax.ppermute(piece, 'atoms', pairs) for piece in pieces]  18.8 us
    pallas_call x1, Pallas kernels, on_device(): pl.pallas_call(functools.partial(density_kernel, holders, atoms_here, lin...  14.9 us
    ppermute x5, waiting for transfers between devices, doubled(): other = lax.ppermute(value, axis, [(i, i ^ step) for i in range(size)])  10.9 us
    ppermute x5, starting transfers between devices, doubled(): other = lax.ppermute(value, axis, [(i, i ^ step) for i in range(size)])  8.49 us
    ppermute x3, starting transfers between devices, gather_columns(): pieces = pieces + [lax.ppermute(piece, 'atoms', pairs) for piece in pieces]  6.09 us
    pallas_call x1, Pallas kernels, on_device(): pl.pallas_call(functools.partial(slab_kernel, tasks), in_specs=[scalars,...  3.63 us
    ppermute x4, waiting for transfers between devices, gather_columns(): pieces = pieces + [lax.ppermute(piece, 'atoms', swap) for piece in pieces]  1.82 us
  transfers between devices with their start and end apart: 12, of which 8 were waited for; matrix products, arithmetic and copies ran while one was open for 0% of the time, Pallas kernels for 0%

profile of v2, /device:TPU:0, one launch (start us, length us, event | category | flops | bytes accessed | tf_op | source)
XLA Modules:
  0.0 68.3 jit_solution(9446320924371678496)
XLA Ops:
  0.6 0.0 copy-start.4
  0.7 0.8 %fusion.2 = (bf16[32,32]{1,0:T(8,128)(2,1)S(1)}, bf16[32,32]{1,0:T(8,128)(2,1)S(1)}) fusion(s32[32,32]{1,0:T(8,128)} %param.11), kind=kLoop, calls=%fused_computation.23 | loop fusion | flops 21504 | bytes 8192 | tf_op jit(solution)/shard_map/convert
  1.5 0.1 fusion.4
  1.5 1.1 %pad_maximum_fusion.rest_0_ = bf16[1088,256]{1,0:T(8,128)(2,1)S(1)} fusion(bf16[32,256]{1,0:T(8,128)(2,1)S(1)} %fusion.4, bf16[32,256]{1,0:T(8,128)(2,1)} %param.10, bf16[1024,256]{1,0:T(8,128)(2,1)} %bitcast.11), kind=kLoop, calls=%fused_computation | loop fusion | flops 1671168 | bytes 1114112 | tf_op jit(solution)/shard_map/concatenate | solution.py:353
  2.6 3.0 %collective-permute-start = (bf16[1088,256]{1,0:T(8,128)(2,1)S(1)}, bf16[1088,256]{1,0:T(8,128)(2,1)S(1)}, u32[]{:S(2)}, u32[]{:S(2)}) collective-permute-start(bf16[1088,256]{1,0:T(8,128)(2,1)S(1)} %pad_maximum_fusion.rest_0_), channel_id=1, source_target_pairs={{0,8},{4,20},{8,0},{12,28},{16,24},{20,4},{24,16},{28,12},{1,9},{5... | collective-permute-start | bytes 1671176 | tf_op jit(solution)/shard_map/ppermute | solution.py:61
  5.6 1.5 %collective-permute-start.1 = (bf16[1088,256]{1,0:T(8,128)(2,1)S(1)}, bf16[1088,256]{1,0:T(8,128)(2,1)S(1)}, u32[]{:S(2)}, u32[]{:S(2)}) collective-permute-start(bf16[1088,256]{1,0:T(8,128)(2,1)S(1)} %pad_maximum_fusion.rest_0_), channel_id=1, source_target_pairs={{0,16},{4,12},{8,24},{12,4},{16,0},{20,28},{24,8},{28,20},{1,17},{... | collective-permute-start | bytes 1671176 | tf_op jit(solution)/shard_map/ppermute | solution.py:61
  7.2 11.4 %collective-permute-done.rest_1_ = bf16[1088,256]{1,0:T(8,128)(2,1)S(1)} collective-permute-done((bf16[1088,256]{1,0:T(8,128)(2,1)S(1)}, bf16[1088,256]{1,0:T(8,128)(2,1)S(1)}, u32[]{:S(2)}, u32[]{:S(2)}) %collective-permute-start) | collective-permute-done | bytes 557088 | tf_op jit(solution)/shard_map/ppermute | solution.py:61
  18.5 1.6 %collective-permute-start.2 = (bf16[1088,256]{1,0:T(8,128)(2,1)S(1)}, bf16[1088,256]{1,0:T(8,128)(2,1)S(1)}, u32[]{:S(2)}, u32[]{:S(2)}) collective-permute-start(bf16[1088,256]{1,0:T(8,128)(2,1)S(1)} %collective-permute-done.rest_1_), channel_id=1, source_target_pairs={{0,16},{4,12},{8,24},{12,4},{16,0},{20,28},{24,8},{28,20},{1,17},{... | collective-permute-start | bytes 1671176 | tf_op jit(solution)/shard_map/ppermute | solution.py:61
  20.1 0.0 collective-permute-start.3
  20.1 0.5 collective-permute-start.4
  20.6 0.0 collective-permute-done.1.rest_2_
  20.6 0.0 collective-permute-start.5
  20.6 7.5 %collective-permute-done.2.rest_3_ = bf16[1088,256]{1,0:T(8,128)(2,1)S(1)} collective-permute-done((bf16[1088,256]{1,0:T(8,128)(2,1)S(1)}, bf16[1088,256]{1,0:T(8,128)(2,1)S(1)}, u32[]{:S(2)}, u32[]{:S(2)}) %collective-permute-start.2) | collective-permute-done | bytes 557088 | tf_op jit(solution)/shard_map/ppermute | solution.py:61
  28.1 0.0 collective-permute-start.6
  28.1 0.1 copy.12.member_col_ref
  28.2 0.1 reshape.16.slot_col_ref
  28.3 0.0 collective-permute-done.3.rest_4_
  28.3 0.0 collective-permute-done.5.rest_6_
  28.3 0.0 collective-permute-done.4.rest_5_
  28.4 1.8 %collective-permute-done.6.rest_7_ = bf16[1088,256]{1,0:T(8,128)(2,1)} collective-permute-done((bf16[1088,256]{1,0:T(8,128)(2,1)S(1)}, bf16[1088,256]{1,0:T(8,128)(2,1)}, u32[]{:S(2)}, u32[]{:S(2)}) %collective-permute-start.6) | collective-permute-done | bytes 557088 | tf_op jit(solution)/shard_map/ppermute | solution.py:63
  30.2 14.9 %shard_map.104 = (bf16[4,512,128]{2,1,0:T(8,128)(2,1)}, bf16[48,128]{1,0:T(8,128)(2,1)S(1)}) custom-call(s32[4,32]{1,0:T(4,128)S(1)} %get-tuple-element.19.place_ref, f32[4]{0:T(128)S(1)} %copy-done, s32[4]{0:T(128)S(1)} %copy-done.1, s32[4]{0:T(128)S(1)} %copy-done.2, s32[4]{0:T(128)S(1)} %copy-done.3, s32[128,1]{1,0:T(8,128)S(1)} %reshape.16.slot_col_ref, ...), custom_call_target="tpu_custom_call" | custom-call | tf_op jit(solution)/shard_map/pallas_call | solution.py:361
  45.1 3.6 %collective-permute-start.7 = (bf16[1,48,128]{2,1,0:T(8,128)(2,1)S(1)}, bf16[1,48,128]{2,1,0:T(8,128)(2,1)S(1)}, u32[]{:S(2)}, u32[]{:S(2)}) collective-permute-start(bf16[1,48,128]{2,1,0:T(8,128)(2,1)S(1)} %bitcast.7), channel_id=1, source_target_pairs={{0,2},{1,3},{2,0},{3,1},{4,6},{5,7},{6,4},{7,5},{8,10},{9,11},{10,... | collective-permute-start | bytes 36872 | tf_op jit(solution)/shard_map/ppermute | solution.py:28
  48.7 1.7 %collective-permute-done.7 = bf16[1,48,128]{2,1,0:T(8,128)(2,1)S(1)} collective-permute-done((bf16[1,48,128]{2,1,0:T(8,128)(2,1)S(1)}, bf16[1,48,128]{2,1,0:T(8,128)(2,1)S(1)}, u32[]{:S(2)}, u32[]{:S(2)}) %collective-permute-start.7) | collective-permute-done | bytes 12320 | tf_op jit(solution)/shard_map/ppermute | solution.py:28
  50.4 1.9 %collective-permute-start.8 = (bf16[2,48,128]{2,1,0:T(8,128)(2,1)S(1)}, bf16[2,48,128]{2,1,0:T(8,128)(2,1)S(1)}, u32[]{:S(2)}, u32[]{:S(2)}) collective-permute-start(bf16[2,48,128]{2,1,0:T(8,128)(2,1)S(1)} %pad_maximum_fusion.3), channel_id=1, source_target_pairs={{0,1},{1,0},{2,3},{3,2},{4,5},{5,4},{6,7},{7,6},{8,9},{9,8},{10,11... | collective-permute-start | bytes 73736 | tf_op jit(solution)/shard_map/ppermute | solution.py:28
  52.3 1.9 %collective-permute-done.8 = bf16[2,48,128]{2,1,0:T(8,128)(2,1)S(1)} collective-permute-done((bf16[2,48,128]{2,1,0:T(8,128)(2,1)S(1)}, bf16[2,48,128]{2,1,0:T(8,128)(2,1)S(1)}, u32[]{:S(2)}, u32[]{:S(2)}) %collective-permute-start.8) | collective-permute-done | bytes 24608 | tf_op jit(solution)/shard_map/ppermute | solution.py:28
  54.3 1.0 %collective-permute-start.9 = (bf16[4,48,128]{2,1,0:T(8,128)(2,1)S(1)}, bf16[4,48,128]{2,1,0:T(8,128)(2,1)S(1)}, u32[]{:S(2)}, u32[]{:S(2)}) collective-permute-start(bf16[4,48,128]{2,1,0:T(8,128)(2,1)S(1)} %pad_maximum_fusion.2), channel_id=1, source_target_pairs={{0,16},{4,20},{8,24},{12,28},{16,0},{20,4},{24,8},{28,12},{1,17},{... | collective-permute-start | bytes 147464 | tf_op jit(solution)/shard_map/ppermute | solution.py:28
  55.2 3.2 %collective-permute-done.9 = bf16[4,48,128]{2,1,0:T(8,128)(2,1)S(1)} collective-permute-done((bf16[4,48,128]{2,1,0:T(8,128)(2,1)S(1)}, bf16[4,48,128]{2,1,0:T(8,128)(2,1)S(1)}, u32[]{:S(2)}, u32[]{:S(2)}) %collective-permute-start.9) | collective-permute-done | bytes 49184 | tf_op jit(solution)/shard_map/ppermute | solution.py:28
  58.4 1.9 %collective-permute-start.10 = (bf16[8,48,128]{2,1,0:T(8,128)(2,1)S(1)}, bf16[8,48,128]{2,1,0:T(8,128)(2,1)S(1)}, u32[]{:S(2)}, u32[]{:S(2)}) collective-permute-start(bf16[8,48,128]{2,1,0:T(8,128)(2,1)S(1)} %pad_maximum_fusion.1), channel_id=1, source_target_pairs={{0,8},{4,12},{8,0},{12,4},{16,24},{20,28},{24,16},{28,20},{1,9},{5... | collective-permute-start | bytes 294920 | tf_op jit(solution)/shard_map/ppermute | solution.py:28
  60.3 2.8 %collective-permute-done.10 = bf16[8,48,128]{2,1,0:T(8,128)(2,1)S(1)} collective-permute-done((bf16[8,48,128]{2,1,0:T(8,128)(2,1)S(1)}, bf16[8,48,128]{2,1,0:T(8,128)(2,1)S(1)}, u32[]{:S(2)}, u32[]{:S(2)}) %collective-permute-start.10) | collective-permute-done | bytes 98336 | tf_op jit(solution)/shard_map/ppermute | solution.py:28
  63.2 0.1 collective-permute-start.11
  63.2 1.4 %collective-permute-done.11 = bf16[16,48,128]{2,1,0:T(8,128)(2,1)S(1)} collective-permute-done((bf16[16,48,128]{2,1,0:T(8,128)(2,1)S(1)}, bf16[16,48,128]{2,1,0:T(8,128)(2,1)S(1)}, u32[]{:S(2)}, u32[]{:S(2)}) %collective-permute-start.11) | collective-permute-done | bytes 196640 | tf_op jit(solution)/shard_map/ppermute | solution.py:28
  64.7 3.6 %shard_map.105 = f32[64,32,128]{2,1,0:T(8,128)} custom-call(s32[1]{0:T(128)} %bitcast.2.slab_number_ref, bf16[32,48,128]{2,1,0:T(8,128)(2,1)S(1)} %constant_dynamic-update-slice_fusion.5.boxes_ref), custom_call_target="tpu_custom_call" | custom-call | tf_op jit(solution)/shard_map/pallas_call | solution.py:397
  (19 shorter events, 0.2 us)
Async XLA Ops:
  0.6 27.5 %copy-start.4 = (s32[4,32]{1,0:T(4,128)S(1)}, s32[4,32]{1,0:T(4,128)}, u32[]{:S(2)}) copy-start(s32[4,32]{1,0:T(4,128)} %param.12) | copy-start | bytes 1540
  0.6 29.5 %copy-start.3 = (s32[4]{0:T(128)S(1)}, s32[4]{0:T(128)}, u32[]{:S(2)}) copy-start(s32[4]{0:T(128)} %col_ref.1) | copy-start | bytes 52
  0.7 29.5 %copy-start.2 = (s32[4]{0:T(128)S(1)}, s32[4]{0:T(128)}, u32[]{:S(2)}) copy-start(s32[4]{0:T(128)} %row_ref.1) | copy-start | bytes 52
  0.7 29.5 %copy-start.1 = (s32[4]{0:T(128)S(1)}, s32[4]{0:T(128)}, u32[]{:S(2)}) copy-start(s32[4]{0:T(128)} %start_ref.1) | copy-start | bytes 52
  0.7 29.5 %copy-start = (f32[4]{0:T(128)S(1)}, f32[4]{0:T(128)}, u32[]{:S(2)}) copy-start(f32[4]{0:T(128)} %shift_ref.1) | copy-start | bytes 52
  2.6 15.9 %collective-permute-start = (bf16[1088,256]{1,0:T(8,128)(2,1)S(1)}, bf16[1088,256]{1,0:T(8,128)(2,1)S(1)}, u32[]{:S(2)}, u32[]{:S(2)}) collective-permute-start(bf16[1088,256]{1,0:T(8,128)(2,1)S(1)} %pad_maximum_fusion.rest_0_), channel_id=1, source_target_pairs={{0,8},{4,20},{8,0},{12,28},{16,24},{20,4},{24,16},{28,12},{1,9},{5... | collective-permute-start | bytes 1671176 | tf_op jit(solution)/shard_map/ppermute | solution.py:61
  5.6 15.0 %collective-permute-start.1 = (bf16[1088,256]{1,0:T(8,128)(2,1)S(1)}, bf16[1088,256]{1,0:T(8,128)(2,1)S(1)}, u32[]{:S(2)}, u32[]{:S(2)}) collective-permute-start(bf16[1088,256]{1,0:T(8,128)(2,1)S(1)} %pad_maximum_fusion.rest_0_), channel_id=1, source_target_pairs={{0,16},{4,12},{8,24},{12,4},{16,0},{20,28},{24,8},{28,20},{1,17},{... | collective-permute-start | bytes 1671176 | tf_op jit(solution)/shard_map/ppermute | solution.py:61
  18.5 9.5 %collective-permute-start.2 = (bf16[1088,256]{1,0:T(8,128)(2,1)S(1)}, bf16[1088,256]{1,0:T(8,128)(2,1)S(1)}, u32[]{:S(2)}, u32[]{:S(2)}) collective-permute-start(bf16[1088,256]{1,0:T(8,128)(2,1)S(1)} %collective-permute-done.rest_1_), channel_id=1, source_target_pairs={{0,16},{4,12},{8,24},{12,4},{16,0},{20,28},{24,8},{28,20},{1,17},{... | collective-permute-start | bytes 1671176 | tf_op jit(solution)/shard_map/ppermute | solution.py:61
  20.1 8.2 %collective-permute-start.3 = (bf16[1088,256]{1,0:T(8,128)(2,1)S(1)}, bf16[1088,256]{1,0:T(8,128)(2,1)S(1)}, u32[]{:S(2)}, u32[]{:S(2)}) collective-permute-start(bf16[1088,256]{1,0:T(8,128)(2,1)S(1)} %pad_maximum_fusion.rest_0_), channel_id=1, source_target_pairs={{0,4},{4,0},{8,12},{12,8},{16,20},{20,16},{24,28},{28,24},{1,5},{5... | collective-permute-start | bytes 1671176 | tf_op jit(solution)/shard_map/ppermute | solution.py:63
  20.1 8.2 %collective-permute-start.4 = (bf16[1088,256]{1,0:T(8,128)(2,1)S(1)}, bf16[1088,256]{1,0:T(8,128)(2,1)S(1)}, u32[]{:S(2)}, u32[]{:S(2)}) collective-permute-start(bf16[1088,256]{1,0:T(8,128)(2,1)S(1)} %collective-permute-done.rest_1_), channel_id=1, source_target_pairs={{0,4},{4,0},{8,12},{12,8},{16,20},{20,16},{24,28},{28,24},{1,5},{5... | collective-permute-start | bytes 1671176 | tf_op jit(solution)/shard_map/ppermute | solution.py:63
  20.6 7.7 %collective-permute-start.5 = (bf16[1088,256]{1,0:T(8,128)(2,1)S(1)}, bf16[1088,256]{1,0:T(8,128)(2,1)}, u32[]{:S(2)}, u32[]{:S(2)}) collective-permute-start(bf16[1088,256]{1,0:T(8,128)(2,1)S(1)} %collective-permute-done.1.rest_2_), channel_id=1, source_target_pairs={{0,4},{4,0},{8,12},{12,8},{16,20},{20,16},{24,28},{28,24},{1,5},{5... | collective-permute-start | bytes 1671176 | tf_op jit(solution)/shard_map/ppermute | solution.py:63
  28.1 2.1 %collective-permute-start.6 = (bf16[1088,256]{1,0:T(8,128)(2,1)S(1)}, bf16[1088,256]{1,0:T(8,128)(2,1)}, u32[]{:S(2)}, u32[]{:S(2)}) collective-permute-start(bf16[1088,256]{1,0:T(8,128)(2,1)S(1)} %collective-permute-done.2.rest_3_), channel_id=1, source_target_pairs={{0,4},{4,0},{8,12},{12,8},{16,20},{20,16},{24,28},{28,24},{1,5},{5... | collective-permute-start | bytes 1671176 | tf_op jit(solution)/shard_map/ppermute | solution.py:63
  45.1 5.3 %collective-permute-start.7 = (bf16[1,48,128]{2,1,0:T(8,128)(2,1)S(1)}, bf16[1,48,128]{2,1,0:T(8,128)(2,1)S(1)}, u32[]{:S(2)}, u32[]{:S(2)}) collective-permute-start(bf16[1,48,128]{2,1,0:T(8,128)(2,1)S(1)} %bitcast.7), channel_id=1, source_target_pairs={{0,2},{1,3},{2,0},{3,1},{4,6},{5,7},{6,4},{7,5},{8,10},{9,11},{10,... | collective-permute-start | bytes 36872 | tf_op jit(solution)/shard_map/ppermute | solution.py:28
  50.4 3.8 %collective-permute-start.8 = (bf16[2,48,128]{2,1,0:T(8,128)(2,1)S(1)}, bf16[2,48,128]{2,1,0:T(8,128)(2,1)S(1)}, u32[]{:S(2)}, u32[]{:S(2)}) collective-permute-start(bf16[2,48,128]{2,1,0:T(8,128)(2,1)S(1)} %pad_maximum_fusion.3), channel_id=1, source_target_pairs={{0,1},{1,0},{2,3},{3,2},{4,5},{5,4},{6,7},{7,6},{8,9},{9,8},{10,11... | collective-permute-start | bytes 73736 | tf_op jit(solution)/shard_map/ppermute | solution.py:28
  54.3 4.2 %collective-permute-start.9 = (bf16[4,48,128]{2,1,0:T(8,128)(2,1)S(1)}, bf16[4,48,128]{2,1,0:T(8,128)(2,1)S(1)}, u32[]{:S(2)}, u32[]{:S(2)}) collective-permute-start(bf16[4,48,128]{2,1,0:T(8,128)(2,1)S(1)} %pad_maximum_fusion.2), channel_id=1, source_target_pairs={{0,16},{4,20},{8,24},{12,28},{16,0},{20,4},{24,8},{28,12},{1,17},{... | collective-permute-start | bytes 147464 | tf_op jit(solution)/shard_map/ppermute | solution.py:28
  58.4 4.7 %collective-permute-start.10 = (bf16[8,48,128]{2,1,0:T(8,128)(2,1)S(1)}, bf16[8,48,128]{2,1,0:T(8,128)(2,1)S(1)}, u32[]{:S(2)}, u32[]{:S(2)}) collective-permute-start(bf16[8,48,128]{2,1,0:T(8,128)(2,1)S(1)} %pad_maximum_fusion.1), channel_id=1, source_target_pairs={{0,8},{4,12},{8,0},{12,4},{16,24},{20,28},{24,16},{28,20},{1,9},{5... | collective-permute-start | bytes 294920 | tf_op jit(solution)/shard_map/ppermute | solution.py:28
  63.2 1.5 %collective-permute-start.11 = (bf16[16,48,128]{2,1,0:T(8,128)(2,1)S(1)}, bf16[16,48,128]{2,1,0:T(8,128)(2,1)S(1)}, u32[]{:S(2)}, u32[]{:S(2)}) collective-permute-start(bf16[16,48,128]{2,1,0:T(8,128)(2,1)S(1)} %get-tuple-element.6), channel_id=1, source_target_pairs={{0,4},{4,0},{8,12},{12,8},{16,20},{20,16},{24,28},{28,24},{1,5},{5... | collective-permute-start | bytes 589832 | tf_op jit(solution)/shard_map/ppermute | solution.py:28

commit v3 on v2

--- a/solution.py
+++ b/solution.py
@@ -23,13 +23,6 @@
 STAGGER = 1
 
 
-def doubled(value, axis, size, pairs):
-    for step in pairs:
-        other = lax.ppermute(value, axis, [(i, i ^ step) for i in range(size)])
-        value = jnp.concatenate([value, other], axis=0)
-    return value
-
-
 def power_of_two(size):
     return size & (size - 1) == 0
 
@@ -37,38 +30,72 @@
 def gather_everywhere(value):
     for axis in ("grid", "atoms"):
         size = lax.axis_size(axis)
-        if power_of_two(size):
-            steps = [1 << bit for bit in range(size.bit_length() - 1)][::-1]
-            value = doubled(value, axis, size, steps)
-        else:
+        if not power_of_two(size):
             value = lax.all_gather(value, axis, axis=0, tiled=True)
+            continue
+        steps = [1 << bit for bit in range(size.bit_length() - 1)][::-1]
+        for stage, step in enumerate(steps):
+            pairs = [(i, i ^ step) for i in range(size)]
+            if axis == "atoms" and step > 1:
+                pairs = [(i, i ^ (steps[len(steps) - 2 - stage] if i & 1 else step)) for i in range(size)]
+            value = jnp.concatenate([value, lax.ppermute(value, axis, pairs)], axis=0)
     return value
 
 
-def gather_columns(packed, holders):
+def split(number, size):
+    if power_of_two(size):
+        return number >> (size.bit_length() - 1), number & (size - 1)
+    return number // size, number % size
+
+
+def slot_of(holder, holders):
     if holders < 2 or not power_of_two(holders):
-        whole = lax.all_gather(packed, "atoms", axis=0)
-        return [whole[i] for i in range(holders)], lambda holder: holder
+        return holder
     stages = holders.bit_length() - 2
-    half = holders // 2
+    apart = holder ^ lax.axis_index("atoms")
+    plain = apart >> 1
+    turned = sum((((plain >> bit) & 1) << (stages - 1 - bit) for bit in range(stages)), 0 * plain)
+    return (apart & 1) * (holders // 2) + jnp.where(holder & 1 == 1, turned, plain)
+
+
+def gather_columns(blocks, side, holders):
+    if holders < 2 or not power_of_two(holders):
+        gathered = [lax.all_gather(part, "atoms", axis=0) for part in (blocks, side())]
+        return [[whole[i] for i in range(holders)] for whole in gathered]
+    stages = holders.bit_length() - 2
 
     def bit_of(device, stage):
         return 2 << (stages - 1 - stage if device & 1 else stage)
 
-    pieces = [packed]
-    for stage in range(stages):
-        pairs = [(i, i ^ bit_of(i, stage)) for i in range(holders)]
-        pieces = pieces + [lax.ppermute(piece, "atoms", pairs) for piece in pieces]
+    pairs = [[(i, i ^ bit_of(i, stage)) for i in range(holders)] for stage in range(stages)]
     swap = [(i, i ^ 1) for i in range(holders)]
-    pieces = pieces + [lax.ppermute(piece, "atoms", swap) for piece in pieces]
-
-    def slot(holder):
-        apart = holder ^ lax.axis_index("atoms")
-        plain = apart >> 1
-        turned = sum((((plain >> bit) & 1) << (stages - 1 - bit) for bit in range(stages)), 0 * plain)
-        return (apart & 1) * half + jnp.where(holder & 1 == 1, turned, plain)
-
-    return pieces, slot
+
+    def send(part):
+        return [lax.ppermute(part, "atoms", pair) for pair in pairs]
+
+    def forward(part, firsts):
+        have = [part]
+        for first, pair in zip(firsts, pairs):
+            have = have + [first] + [lax.ppermute(piece, "atoms", pair) for piece in have[1:]]
+        return have
+
+    firsts = send(blocks)
+    beside = lax.ppermute(blocks, "atoms", swap)
+    beside, wanted = lax.optimization_barrier((beside, side()))
+    side_firsts = send(wanted)
+    if stages:
+        firsts[0], side_firsts = lax.optimization_barrier((firsts[0], side_firsts))
+    have, side_have = forward(blocks, firsts), forward(wanted, side_firsts)
+    swapped = [beside] + [lax.ppermute(piece, "atoms", swap) for piece in have[1:-1]]
+    side_swapped = [lax.ppermute(piece, "atoms", swap) for piece in side_have[:-1]]
+    mine = jnp.concatenate([blocks, wanted[:, : blocks.shape[1]]], axis=0)
+    have[-1], side_have[-1], swapped, side_swapped, mine = lax.optimization_barrier(
+        (have[-1], side_have[-1], swapped, side_swapped, mine)
+    )
+    if stages:
+        swapped.append(lax.ppermute(have[-1], "atoms", swap))
+    side_swapped.append(lax.ppermute(side_have[-1], "atoms", swap))
+    return [[mine] + have[1:] + swapped, side_have + side_swapped]
 
 
 def iota(shape, axis):
@@ -101,68 +128,77 @@
     holders,
     atoms_here,
     links,
-    place_ref,
     shift_ref,
     start_ref,
     row_ref,
     col_ref,
-    slot_col_ref,
-    member_col_ref,
+    members_ref,
     basis_hbm,
     *rest,
 ):
-    pieces = rest[:holders]
+    pieces, extras = rest[:holders], rest[holders : 2 * holders]
     (
         density_hbm,
         box_ref,
         cols,
-        onsites,
-        idents,
+        sides,
         basis,
         density,
         ids_all,
         onsite_all,
         product,
         matrix,
+        place_vmem,
+        place_ref,
+        place_sem,
         sems,
         basis_sems,
         density_sems,
-    ) = rest[holders:]
+    ) = rest[2 * holders :]
     half = jnp.bfloat16
-    tasks, set_size = member_col_ref.shape[:2]
+    tasks, set_size = members_ref.shape
     order = set_size * BS
     area = BS * BS
     block_rows = atoms_here * links
     groups = set_size // LOW
 
     copies = []
-    for number, piece in enumerate(pieces):
-        spots = (
-            (cols, 0, block_rows),
-            (onsites, block_rows, atoms_here),
-            (idents, block_rows + atoms_here, atoms_here),
-        )
-        for kind, (target, first, count) in enumerate(spots):
-            copies.append(
-                pltpu.make_async_copy(
-                    piece.at[pl.ds(first, count)], target.at[pl.ds(number * count, count)], sems.at[kind, number]
-                )
-            )
+    for kind, (parts, whole, count) in enumerate(((extras, sides, atoms_here), (pieces, cols, block_rows))):
+        for number, part in enumerate(parts):
+            target = whole.at[pl.ds(number * count, count)]
+            copies.append(pltpu.make_async_copy(part.at[pl.ds(0, count)], target, sems.at[kind, number]))
     loads = [pltpu.make_async_copy(basis_hbm.at[t], basis.at[t], basis_sems.at[t]) for t in range(tasks)]
     stores = [pltpu.make_async_copy(density.at[t], density_hbm.at[t], density_sems.at[t]) for t in range(tasks)]
     for copy in copies:
         copy.start()
-    for copy in copies:
+    held_by, held_at = split(members_ref[...], atoms_here)
+    slots = slot_of(held_by, holders) * atoms_here + held_at
+    place_vmem[...] = slots
+    place_copy = pltpu.make_async_copy(place_vmem, place_ref, place_sem)
+    place_copy.start()
+    for copy in copies[:holders]:
+        copy.wait()
+    atoms = iota((set_size, holders * atoms_here), 1).astype(jnp.float32)
+    diagonal = iota((set_size, set_size), 0) == iota((set_size, set_size), 1)
+
+    def column(rows, task):
+        row = rows[task : task + 1].astype(jnp.float32)
+        return jnp.sum(jnp.where(diagonal, row, 0.0), axis=1, keepdims=True)
+
+    members = [column(members_ref[...], task) for task in range(tasks)]
+    chosen = jnp.concatenate(
+        [(column(slots, task) == atoms).astype(jnp.float32) for task in range(tasks)], axis=0
+    ).astype(half)
+    onsite_all[...] = nn(chosen, sides[:, :area])
+    raw = nn(chosen, sides[:, area:]).astype(half)
+    source, target = iota((area, LOW * links), 0), iota((area, LOW * links), 1) % links
+    spread = jnp.where(source == target, 1.0, jnp.where(source == links + target, 256.0, 0.0)).astype(half)
+    ids_all[...] = nn(raw, spread)
+    place_copy.wait()
+    for copy in copies[holders:]:
         copy.wait()
     for load in loads:
         load.start()
-    count = tasks * set_size
-    chosen = (slot_col_ref[...] == iota((count, holders * atoms_here), 1)).astype(jnp.float32).astype(half)
-    onsite_all[...] = nn(chosen, onsites[...])
-    raw = nn(chosen, idents[...]).astype(half)
-    source, target = iota((area, LOW * links), 0), iota((area, LOW * links), 1) % links
-    spread = jnp.where(source == target, 1.0, jnp.where(source == links + target, 256.0, 0.0)).astype(half)
-    ids_all[...] = nn(raw, spread)
 
     source, target = iota((area, area), 0), iota((area, area), 1)
     wanted = ((target // LANES) * LOW + target % LOW) * BS + (target % LANES) // LOW
@@ -181,7 +217,7 @@
     def assemble(task, group):
         base = task * set_size + group * LOW
         ids_row = jnp.sum(jnp.where(own, ids_all[pl.ds(base, LOW), :], 0.0), axis=0, keepdims=True)
-        match = (member_col_ref[task] == ids_row).astype(jnp.float32)
+        match = (members[task] == ids_row).astype(jnp.float32)
         spread_match = jnp.concatenate(
             [jnp.where(owner_wide == low, match, 0.0).astype(half) for low in range(LOW)], axis=0
         )
@@ -348,19 +384,21 @@
     atoms_here, links, area = column_blocks.shape
     tasks, set_size = task_atoms.shape
     order, points = basis_values.shape[1:]
-    idents = jnp.concatenate([neighbor_ids % 256, neighbor_ids // 256], axis=1).astype(half)
-    idents = jnp.pad(idents, ((0, 0), (0, area - 2 * links)))
-    packed = jnp.concatenate([column_blocks.reshape(atoms_here * links, area), onsite, idents], axis=0)
-    pieces, slot = gather_columns(packed, holders)
-    place = slot(task_atoms // atoms_here) * atoms_here + task_atoms % atoms_here
+    blocks = column_blocks.reshape(atoms_here * links, area)
+
+    def side():
+        ids, diagonal = lax.optimization_barrier((neighbor_ids, onsite))
+        idents = jnp.concatenate([ids % 256, ids // 256], axis=1).astype(half)
+        return jnp.concatenate([diagonal, jnp.pad(idents, ((0, 0), (0, area - 2 * links)))], axis=1)
+
+    pieces, extras = gather_columns(blocks, side, holders)
     everything = pl.BlockSpec(memory_space=pl.ANY)
     scalars = pl.BlockSpec(memory_space=pltpu.SMEM)
     vectors = pl.BlockSpec(memory_space=pltpu.VMEM)
     box_rows = (tasks * points // LANES + 1 + 15) // 16 * 16
-    column_bytes = packed.size * holders * 2
     density, boxes = pl.pallas_call(
         functools.partial(density_kernel, holders, atoms_here, links),
-        in_specs=[scalars] * 5 + [vectors] * 2 + [pl.BlockSpec(memory_space=pltpu.HBM)] + [everything] * holders,
+        in_specs=[scalars] * 4 + [vectors, pl.BlockSpec(memory_space=pltpu.HBM)] + [everything] * (2 * holders),
         out_specs=[everything, vectors],
         out_shape=[
             jax.ShapeDtypeStruct((tasks, order, CENTRAL), half),
@@ -368,29 +406,30 @@
         ],
         scratch_shapes=[
             pltpu.VMEM((holders * atoms_here * links, area), half),
-            pltpu.VMEM((holders * atoms_here, area), half),
-            pltpu.VMEM((holders * atoms_here, area), half),
+            pltpu.VMEM((holders * atoms_here, 2 * area), half),
             pltpu.VMEM((tasks, order, points), half),
             pltpu.VMEM((tasks, order, CENTRAL), half),
             pltpu.VMEM((tasks * set_size, LOW * links), jnp.float32),
             pltpu.VMEM((tasks * set_size, area), jnp.float32),
             pltpu.VMEM((tasks, 2, LOW * set_size, area), jnp.float32),
             pltpu.VMEM((tasks, order, order), jnp.float32),
-            pltpu.SemaphoreType.DMA((3, holders)),
+            pltpu.VMEM((tasks, set_size), jnp.int32),
+            pltpu.SMEM((tasks, set_size), jnp.int32),
+            pltpu.SemaphoreType.DMA,
+            pltpu.SemaphoreType.DMA((2, holders)),
             pltpu.SemaphoreType.DMA((tasks,)),
             pltpu.SemaphoreType.DMA((tasks,)),
         ],
         compiler_params=pltpu.CompilerParams(vmem_limit_bytes=48 * 1024 * 1024),
     )(
-        place,
         chem_shift,
         box_start,
         box_row,
         box_col,
-        place.reshape(-1, 1),
-        task_atoms.astype(jnp.float32)[:, :, None],
+        task_atoms,
         basis_values,
         *pieces,
+        *extras,
     )
     all_boxes = gather_everywhere(boxes[None])
     slab_number = lax.axis_index("grid").astype(jnp.int32).reshape(1)

time: 68.7 us -> 66 us (0.961)
  waiting for transfers between devices: 31.6 us -> 26.4 us
  starting transfers between devices: 15.1 us -> 18.3 us
  Pallas kernels: 18.5 us -> 17.4 us
    ppermute x12 -> x19, waiting for transfers between devices: 31.6 us -> 26.4 us  [the longest x5 10.6 us: gather_everywhere(): value = jnp.concatenate([value, lax.ppermute(value, axis, pairs)], axis=0)]
    ppermute x12 -> x19, starting transfers between devices: 15.1 us -> 18.3 us  [the longest x5 8.58 us: gather_everywhere(): value = jnp.concatenate([value, lax.ppermute(value, axis, pairs)], axis=0)]
    pallas_call x1, Pallas kernels: 14.9 us -> 13.9 us  [on_device(): pl.pallas_call(functools.partial(density_kernel, holders, atoms_here, lin...]
    concatenate x5 -> x6, other arithmetic: 1.2 us -> 1.9 us  [the longest x1 1.08 us: gather_columns(): mine = jnp.concatenate([blocks, wanted[:, :blocks.shape[1]]], axis=0)]
  transfers between devices with their start and end apart: 12 -> 19, of which waited for: 8 -> 11; matrix products, arithmetic and copies ran while one was open for 0% -> 4% of each run, Pallas kernels for 0% -> 0%
where the time goes in v3:
time: 66 us; the launch traced here: 65.6 us
  waiting for transfers between devices  26.4 us (40%)
  starting transfers between devices  18.3 us (28%)
  Pallas kernels  17.4 us (26%)
  other arithmetic  2.64 us (4%)
  between operations  0.78 us (1%)
    pallas_call x1, Pallas kernels, on_device(): pl.pallas_call(functools.partial(density_kernel, holders, atoms_here, lin...  13.9 us
    ppermute x5, waiting for transfers between devices, gather_everywhere(): value = jnp.concatenate([value, lax.ppermute(value, axis, pairs)], axis=0)  10.6 us
    ppermute x4, waiting for transfers between devices, send(): return [lax.ppermute(part, 'atoms', pair) for pair in pairs]  9.74 us
    ppermute x5, starting transfers between devices, gather_everywhere(): value = jnp.concatenate([value, lax.ppermute(value, axis, pairs)], axis=0)  8.58 us
    ppermute x4, starting transfers between devices, send(): return [lax.ppermute(part, 'atoms', pair) for pair in pairs]  4.7 us
    pallas_call x1, Pallas kernels, on_device(): pl.pallas_call(functools.partial(slab_kernel, tasks), in_specs=[scalars,...  3.5 us
    ppermute x2, waiting for transfers between devices, forward(): lax.ppermute(piece, 'atoms', pair)  3.12 us
    ppermute x2, starting transfers between devices, forward(): lax.ppermute(piece, 'atoms', pair)  3.03 us
  transfers between devices with their start and end apart: 19, of which 11 were waited for; matrix products, arithmetic and copies ran while one was open for 4% of the time, Pallas kernels for 0%

profile of v3, /device:TPU:0, one launch (start us, length us, event | category | flops | bytes accessed | tf_op | source)
XLA Modules:
  0.0 65.6 jit_solution(7876444305882052416)
XLA Ops:
  0.7 0.5 collective-permute-start.1
  1.2 2.6 %collective-permute-start.7 = (bf16[1024,256]{1,0:T(8,128)(2,1)}, bf16[1024,256]{1,0:T(8,128)(2,1)S(1)}, u32[]{:S(2)}, u32[]{:S(2)}) collective-permute-start(bf16[1024,256]{1,0:T(8,128)(2,1)} %bitcast.10), channel_id=1, source_target_pairs={{0,16},{4,12},{8,24},{12,4},{16,0},{20,28},{24,8},{28,20},{1,17},{... | collective-permute-start | bytes 1572872 | tf_op jit(solution)/shard_map/ppermute | solution.py:74
  3.8 1.5 %collective-permute-start = (bf16[1024,256]{1,0:T(8,128)(2,1)}, bf16[1024,256]{1,0:T(8,128)(2,1)S(1)}, u32[]{:S(2)}, u32[]{:S(2)}) collective-permute-start(bf16[1024,256]{1,0:T(8,128)(2,1)} %bitcast.11), channel_id=1, source_target_pairs={{0,8},{4,20},{8,0},{12,28},{16,24},{20,4},{24,16},{28,12},{1,9},{5... | collective-permute-start | bytes 1572872 | tf_op jit(solution)/shard_map/ppermute | solution.py:74
  5.3 0.7 %fusion.2 = (bf16[32,32]{1,0:T(8,128)(2,1)S(1)}, bf16[32,32]{1,0:T(8,128)(2,1)S(1)}) fusion(s32[32,32]{1,0:T(8,128)} %param.11), kind=kLoop, calls=%fused_computation.24 | loop fusion | flops 21504 | bytes 8192 | tf_op jit(solution)/shard_map/convert
  6.0 0.1 fusion.4
  6.1 0.7 %pad_maximum_fusion.3.rest_8_ = bf16[32,512]{1,0:T(8,128)(2,1)S(1)} fusion(bf16[32,256]{1,0:T(8,128)(2,1)S(1)} %fusion.4, bf16[32,256]{1,0:T(8,128)(2,1)} %param.10), kind=kLoop, calls=%fused_computation.6 | loop fusion | flops 65536 | bytes 65536 | tf_op jit(solution)/shard_map/concatenate | solution.py:392
  6.8 0.5 collective-permute-start.2
  7.4 0.1 collective-permute-start.3
  7.4 8.4 %collective-permute-done.7.rest_2_ = bf16[1024,256]{1,0:T(8,128)(2,1)S(1)} collective-permute-done((bf16[1024,256]{1,0:T(8,128)(2,1)}, bf16[1024,256]{1,0:T(8,128)(2,1)S(1)}, u32[]{:S(2)}, u32[]{:S(2)}) %collective-permute-start.7) | collective-permute-done | bytes 524320 | tf_op jit(solution)/shard_map/ppermute | solution.py:74
  15.8 1.0 %collective-permute-done.rest_1_ = bf16[1024,256]{1,0:T(8,128)(2,1)S(1)} collective-permute-done((bf16[1024,256]{1,0:T(8,128)(2,1)}, bf16[1024,256]{1,0:T(8,128)(2,1)S(1)}, u32[]{:S(2)}, u32[]{:S(2)}) %collective-permute-start) | collective-permute-done | bytes 524320 | tf_op jit(solution)/shard_map/ppermute | solution.py:74
  16.8 0.4 collective-permute-done.2.rest_9_
  17.2 1.8 %collective-permute-start.4 = (bf16[1024,256]{1,0:T(8,128)(2,1)S(1)}, bf16[1024,256]{1,0:T(8,128)(2,1)S(1)}, u32[]{:S(2)}, u32[]{:S(2)}) collective-permute-start(bf16[1024,256]{1,0:T(8,128)(2,1)S(1)} %collective-permute-done.rest_1_), channel_id=1, source_target_pairs={{0,16},{4,12},{8,24},{12,4},{16,0},{20,28},{24,8},{28,20},{1,17},{... | collective-permute-start | bytes 1572872 | tf_op jit(solution)/shard_map/ppermute | solution.py:79
  19.0 0.5 collective-permute-start.9
  19.5 1.4 %collective-permute-done.9.rest_12_ = bf16[32,512]{1,0:T(8,128)(2,1)S(1)} collective-permute-done((bf16[32,512]{1,0:T(8,128)(2,1)S(1)}, bf16[32,512]{1,0:T(8,128)(2,1)S(1)}, u32[]{:S(2)}, u32[]{:S(2)}) %collective-permute-start.9) | collective-permute-done | bytes 32800 | tf_op jit(solution)/shard_map/ppermute | solution.py:90
  20.9 1.3 %collective-permute-start.5 = (bf16[32,512]{1,0:T(8,128)(2,1)S(1)}, bf16[32,512]{1,0:T(8,128)(2,1)S(1)}, u32[]{:S(2)}, u32[]{:S(2)}) collective-permute-start(bf16[32,512]{1,0:T(8,128)(2,1)S(1)} %collective-permute-done.2.rest_9_), channel_id=1, source_target_pairs={{0,16},{4,12},{8,24},{12,4},{16,0},{20,28},{24,8},{28,20},{1,17},{... | collective-permute-start | bytes 98312 | tf_op jit(solution)/shard_map/ppermute | solution.py:79
  22.2 0.3 collective-permute-start.11
  22.5 1.1 %pad_maximum_fusion.rest_0_ = bf16[1056,256]{1,0:T(8,128)(2,1)S(1)} fusion(bf16[32,256]{1,0:T(8,128)(2,1)S(1)} %slice.3, bf16[1024,256]{1,0:T(8,128)(2,1)} %bitcast.12), kind=kLoop, calls=%fused_computation | loop fusion | flops 1081344 | bytes 1081344 | tf_op jit(solution)/shard_map/concatenate | solution.py:91
  23.6 3.1 %collective-permute-done.5.rest_11_ = bf16[32,512]{1,0:T(8,128)(2,1)S(1)} collective-permute-done((bf16[32,512]{1,0:T(8,128)(2,1)S(1)}, bf16[32,512]{1,0:T(8,128)(2,1)S(1)}, u32[]{:S(2)}, u32[]{:S(2)}) %collective-permute-start.5) | collective-permute-done | bytes 32800 | tf_op jit(solution)/shard_map/ppermute | solution.py:79
  26.8 0.1 collective-permute-start.12
  26.8 0.5 collective-permute-start.13
  27.3 1.4 %collective-permute-done.13.rest_15_ = bf16[32,512]{1,0:T(8,128)(2,1)S(1)} collective-permute-done((bf16[32,512]{1,0:T(8,128)(2,1)S(1)}, bf16[32,512]{1,0:T(8,128)(2,1)S(1)}, u32[]{:S(2)}, u32[]{:S(2)}) %collective-permute-start.13) | collective-permute-done | bytes 32800 | tf_op jit(solution)/shard_map/ppermute | solution.py:97
  28.8 13.9 %shard_map.104 = (bf16[4,512,128]{2,1,0:T(8,128)(2,1)}, bf16[48,128]{1,0:T(8,128)(2,1)S(1)}) custom-call(f32[4]{0:T(128)S(1)} %copy-done.1, s32[4]{0:T(128)S(1)} %copy-done.2, s32[4]{0:T(128)S(1)} %copy-done.3, s32[4]{0:T(128)S(1)} %copy-done.4, s32[4,32]{1,0:T(4,128)S(1)} %copy-done, bf16[4,512,1024]{2,1,0:T(8,128)(2,1)} %basis_hbm.1, ...), custom_call_target="tpu_custom_call" | custom-call | tf_op jit(solution)/shard_map/pallas_call | solution.py:399
  42.7 2.9 %collective-permute-start.14 = (bf16[1,48,128]{2,1,0:T(8,128)(2,1)S(1)}, bf16[1,48,128]{2,1,0:T(8,128)(2,1)S(1)}, u32[]{:S(2)}, u32[]{:S(2)}) collective-permute-start(bf16[1,48,128]{2,1,0:T(8,128)(2,1)S(1)} %bitcast.5), channel_id=1, source_target_pairs={{0,2},{1,3},{2,0},{3,1},{4,6},{5,7},{6,4},{7,5},{8,10},{9,11},{10,... | collective-permute-start | bytes 36872 | tf_op jit(solution)/shard_map/ppermute | solution.py:41
  45.7 1.7 %collective-permute-done.14 = bf16[1,48,128]{2,1,0:T(8,128)(2,1)S(1)} collective-permute-done((bf16[1,48,128]{2,1,0:T(8,128)(2,1)S(1)}, bf16[1,48,128]{2,1,0:T(8,128)(2,1)S(1)}, u32[]{:S(2)}, u32[]{:S(2)}) %collective-permute-start.14) | collective-permute-done | bytes 12320 | tf_op jit(solution)/shard_map/ppermute | solution.py:41
  47.4 1.8 %collective-permute-start.15 = (bf16[2,48,128]{2,1,0:T(8,128)(2,1)S(1)}, bf16[2,48,128]{2,1,0:T(8,128)(2,1)S(1)}, u32[]{:S(2)}, u32[]{:S(2)}) collective-permute-start(bf16[2,48,128]{2,1,0:T(8,128)(2,1)S(1)} %pad_maximum_fusion.4), channel_id=1, source_target_pairs={{0,1},{1,0},{2,3},{3,2},{4,5},{5,4},{6,7},{7,6},{8,9},{9,8},{10,11... | collective-permute-start | bytes 73736 | tf_op jit(solution)/shard_map/ppermute | solution.py:41
  49.2 2.0 %collective-permute-done.15 = bf16[2,48,128]{2,1,0:T(8,128)(2,1)S(1)} collective-permute-done((bf16[2,48,128]{2,1,0:T(8,128)(2,1)S(1)}, bf16[2,48,128]{2,1,0:T(8,128)(2,1)S(1)}, u32[]{:S(2)}, u32[]{:S(2)}) %collective-permute-start.15) | collective-permute-done | bytes 24608 | tf_op jit(solution)/shard_map/ppermute | solution.py:41
  51.2 1.8 %collective-permute-start.16 = (bf16[4,48,128]{2,1,0:T(8,128)(2,1)S(1)}, bf16[4,48,128]{2,1,0:T(8,128)(2,1)S(1)}, u32[]{:S(2)}, u32[]{:S(2)}) collective-permute-start(bf16[4,48,128]{2,1,0:T(8,128)(2,1)S(1)} %pad_maximum_fusion.2), channel_id=1, source_target_pairs={{0,16},{4,12},{8,24},{12,4},{16,0},{20,28},{24,8},{28,20},{1,17},{... | collective-permute-start | bytes 147464 | tf_op jit(solution)/shard_map/ppermute | solution.py:41
  53.1 2.7 %collective-permute-done.16 = bf16[4,48,128]{2,1,0:T(8,128)(2,1)S(1)} collective-permute-done((bf16[4,48,128]{2,1,0:T(8,128)(2,1)S(1)}, bf16[4,48,128]{2,1,0:T(8,128)(2,1)S(1)}, u32[]{:S(2)}, u32[]{:S(2)}) %collective-permute-start.16) | collective-permute-done | bytes 49184 | tf_op jit(solution)/shard_map/ppermute | solution.py:41
  55.8 1.9 %collective-permute-start.17 = (bf16[8,48,128]{2,1,0:T(8,128)(2,1)S(1)}, bf16[8,48,128]{2,1,0:T(8,128)(2,1)S(1)}, u32[]{:S(2)}, u32[]{:S(2)}) collective-permute-start(bf16[8,48,128]{2,1,0:T(8,128)(2,1)S(1)} %pad_maximum_fusion.1), channel_id=1, source_target_pairs={{0,8},{4,20},{8,0},{12,28},{16,24},{20,4},{24,16},{28,12},{1,9},{5... | collective-permute-start | bytes 294920 | tf_op jit(solution)/shard_map/ppermute | solution.py:41
  57.8 2.7 %collective-permute-done.17 = bf16[8,48,128]{2,1,0:T(8,128)(2,1)S(1)} collective-permute-done((bf16[8,48,128]{2,1,0:T(8,128)(2,1)S(1)}, bf16[8,48,128]{2,1,0:T(8,128)(2,1)S(1)}, u32[]{:S(2)}, u32[]{:S(2)}) %collective-permute-start.17) | collective-permute-done | bytes 98336 | tf_op jit(solution)/shard_map/ppermute | solution.py:41
  60.7 1.4 %collective-permute-done.18 = bf16[16,48,128]{2,1,0:T(8,128)(2,1)S(1)} collective-permute-done((bf16[16,48,128]{2,1,0:T(8,128)(2,1)S(1)}, bf16[16,48,128]{2,1,0:T(8,128)(2,1)S(1)}, u32[]{:S(2)}, u32[]{:S(2)}) %collective-permute-start.18) | collective-permute-done | bytes 196640 | tf_op jit(solution)/shard_map/ppermute | solution.py:41
  62.1 3.5 %shard_map.105 = f32[64,32,128]{2,1,0:T(8,128)} custom-call(s32[1]{0:T(128)} %bitcast.1.slab_number_ref, bf16[32,48,128]{2,1,0:T(8,128)(2,1)S(1)} %constant_dynamic-update-slice_fusion.5.boxes_ref), custom_call_target="tpu_custom_call" | custom-call | tf_op jit(solution)/shard_map/pallas_call | solution.py:436
  (32 shorter events, 0.3 us)
Async XLA Ops:
  0.6 28.2 %copy-start = (s32[4,32]{1,0:T(4,128)S(1)}, s32[4,32]{1,0:T(4,128)}, u32[]{:S(2)}) copy-start(s32[4,32]{1,0:T(4,128)} %members_ref.1) | copy-start | bytes 1540
  0.6 28.1 %copy-start.1 = (f32[4]{0:T(128)S(1)}, f32[4]{0:T(128)}, u32[]{:S(2)}) copy-start(f32[4]{0:T(128)} %shift_ref.1) | copy-start | bytes 52
  0.7 28.1 %copy-start.2 = (s32[4]{0:T(128)S(1)}, s32[4]{0:T(128)}, u32[]{:S(2)}) copy-start(s32[4]{0:T(128)} %start_ref.1) | copy-start | bytes 52
  0.7 28.1 %copy-start.3 = (s32[4]{0:T(128)S(1)}, s32[4]{0:T(128)}, u32[]{:S(2)}) copy-start(s32[4]{0:T(128)} %row_ref.1) | copy-start | bytes 52
  0.7 28.1 %copy-start.4 = (s32[4]{0:T(128)S(1)}, s32[4]{0:T(128)}, u32[]{:S(2)}) copy-start(s32[4]{0:T(128)} %col_ref.1) | copy-start | bytes 52
  0.7 6.2 %collective-permute-start.1 = (bf16[1024,256]{1,0:T(8,128)(2,1)}, bf16[1024,256]{1,0:T(8,128)(2,1)S(1)}, u32[]{:S(2)}, u32[]{:S(2)}) collective-permute-start(bf16[1024,256]{1,0:T(8,128)(2,1)} %bitcast.9), channel_id=1, source_target_pairs={{0,4},{4,0},{8,12},{12,8},{16,20},{20,16},{24,28},{28,24},{1,5},{5... | collective-permute-start | bytes 1572872 | tf_op jit(solution)/shard_map/ppermute | solution.py:83
  1.2 14.6 %collective-permute-start.7 = (bf16[1024,256]{1,0:T(8,128)(2,1)}, bf16[1024,256]{1,0:T(8,128)(2,1)S(1)}, u32[]{:S(2)}, u32[]{:S(2)}) collective-permute-start(bf16[1024,256]{1,0:T(8,128)(2,1)} %bitcast.10), channel_id=1, source_target_pairs={{0,16},{4,12},{8,24},{12,4},{16,0},{20,28},{24,8},{28,20},{1,17},{... | collective-permute-start | bytes 1572872 | tf_op jit(solution)/shard_map/ppermute | solution.py:74
  3.8 13.0 %collective-permute-start = (bf16[1024,256]{1,0:T(8,128)(2,1)}, bf16[1024,256]{1,0:T(8,128)(2,1)S(1)}, u32[]{:S(2)}, u32[]{:S(2)}) collective-permute-start(bf16[1024,256]{1,0:T(8,128)(2,1)} %bitcast.11), channel_id=1, source_target_pairs={{0,8},{4,20},{8,0},{12,28},{16,24},{20,4},{24,16},{28,12},{1,9},{5... | collective-permute-start | bytes 1572872 | tf_op jit(solution)/shard_map/ppermute | solution.py:74
  6.8 10.4 %collective-permute-start.2 = (bf16[32,512]{1,0:T(8,128)(2,1)S(1)}, bf16[32,512]{1,0:T(8,128)(2,1)S(1)}, u32[]{:S(2)}, u32[]{:S(2)}) collective-permute-start(bf16[32,512]{1,0:T(8,128)(2,1)S(1)} %pad_maximum_fusion.3.rest_8_), channel_id=1, source_target_pairs={{0,8},{4,20},{8,0},{12,28},{16,24},{20,4},{24,16},{28,12},{1,9},{5... | collective-permute-start | bytes 98312 | tf_op jit(solution)/shard_map/ppermute | solution.py:74
  7.4 9.8 %collective-permute-start.3 = (bf16[32,512]{1,0:T(8,128)(2,1)S(1)}, bf16[32,512]{1,0:T(8,128)(2,1)S(1)}, u32[]{:S(2)}, u32[]{:S(2)}) collective-permute-start(bf16[32,512]{1,0:T(8,128)(2,1)S(1)} %pad_maximum_fusion.3.rest_8_), channel_id=1, source_target_pairs={{0,16},{4,12},{8,24},{12,4},{16,0},{20,28},{24,8},{28,20},{1,17},{... | collective-permute-start | bytes 98312 | tf_op jit(solution)/shard_map/ppermute | solution.py:74
  15.8 10.9 %collective-permute-start.8 = (bf16[1024,256]{1,0:T(8,128)(2,1)S(1)}, bf16[1024,256]{1,0:T(8,128)(2,1)S(1)}, u32[]{:S(2)}, u32[]{:S(2)}) collective-permute-start(bf16[1024,256]{1,0:T(8,128)(2,1)S(1)} %collective-permute-done.7.rest_2_), channel_id=1, source_target_pairs={{0,4},{4,0},{8,12},{12,8},{16,20},{20,16},{24,28},{28,24},{1,5},{5... | collective-permute-start | bytes 1572872 | tf_op jit(solution)/shard_map/ppermute | solution.py:89
  17.2 9.5 %collective-permute-start.4 = (bf16[1024,256]{1,0:T(8,128)(2,1)S(1)}, bf16[1024,256]{1,0:T(8,128)(2,1)S(1)}, u32[]{:S(2)}, u32[]{:S(2)}) collective-permute-start(bf16[1024,256]{1,0:T(8,128)(2,1)S(1)} %collective-permute-done.rest_1_), channel_id=1, source_target_pairs={{0,16},{4,12},{8,24},{12,4},{16,0},{20,28},{24,8},{28,20},{1,17},{... | collective-permute-start | bytes 1572872 | tf_op jit(solution)/shard_map/ppermute | solution.py:79
  19.0 7.8 %collective-permute-start.6 = (bf16[1024,256]{1,0:T(8,128)(2,1)S(1)}, bf16[1024,256]{1,0:T(8,128)(2,1)S(1)}, u32[]{:S(2)}, u32[]{:S(2)}) collective-permute-start(bf16[1024,256]{1,0:T(8,128)(2,1)S(1)} %collective-permute-done.rest_1_), channel_id=1, source_target_pairs={{0,4},{4,0},{8,12},{12,8},{16,20},{20,16},{24,28},{28,24},{1,5},{5... | collective-permute-start | bytes 1572872 | tf_op jit(solution)/shard_map/ppermute | solution.py:89
  19.0 2.0 %collective-permute-start.9 = (bf16[32,512]{1,0:T(8,128)(2,1)S(1)}, bf16[32,512]{1,0:T(8,128)(2,1)S(1)}, u32[]{:S(2)}, u32[]{:S(2)}) collective-permute-start(bf16[32,512]{1,0:T(8,128)(2,1)S(1)} %pad_maximum_fusion.3.rest_8_), channel_id=1, source_target_pairs={{0,4},{4,0},{8,12},{12,8},{16,20},{20,16},{24,28},{28,24},{1,5},{5... | collective-permute-start | bytes 98312 | tf_op jit(solution)/shard_map/ppermute | solution.py:90
  19.5 2.7 %collective-permute-start.10 = (bf16[32,512]{1,0:T(8,128)(2,1)S(1)}, bf16[32,512]{1,0:T(8,128)(2,1)S(1)}, u32[]{:S(2)}, u32[]{:S(2)}) collective-permute-start(bf16[32,512]{1,0:T(8,128)(2,1)S(1)} %collective-permute-done.2.rest_9_), channel_id=1, source_target_pairs={{0,4},{4,0},{8,12},{12,8},{16,20},{20,16},{24,28},{28,24},{1,5},{5... | collective-permute-start | bytes 98312 | tf_op jit(solution)/shard_map/ppermute | solution.py:90
  20.9 5.8 %collective-permute-start.5 = (bf16[32,512]{1,0:T(8,128)(2,1)S(1)}, bf16[32,512]{1,0:T(8,128)(2,1)S(1)}, u32[]{:S(2)}, u32[]{:S(2)}) collective-permute-start(bf16[32,512]{1,0:T(8,128)(2,1)S(1)} %collective-permute-done.2.rest_9_), channel_id=1, source_target_pairs={{0,16},{4,12},{8,24},{12,4},{16,0},{20,28},{24,8},{28,20},{1,17},{... | collective-permute-start | bytes 98312 | tf_op jit(solution)/shard_map/ppermute | solution.py:79
  22.2 4.5 %collective-permute-start.11 = (bf16[32,512]{1,0:T(8,128)(2,1)S(1)}, bf16[32,512]{1,0:T(8,128)(2,1)S(1)}, u32[]{:S(2)}, u32[]{:S(2)}) collective-permute-start(bf16[32,512]{1,0:T(8,128)(2,1)S(1)} %collective-permute-done.3.rest_10_), channel_id=1, source_target_pairs={{0,4},{4,0},{8,12},{12,8},{16,20},{20,16},{24,28},{28,24},{1,5},{5... | collective-permute-start | bytes 98312 | tf_op jit(solution)/shard_map/ppermute | solution.py:90
  26.8 2.0 %collective-permute-start.12 = (bf16[1024,256]{1,0:T(8,128)(2,1)S(1)}, bf16[1024,256]{1,0:T(8,128)(2,1)S(1)}, u32[]{:S(2)}, u32[]{:S(2)}) collective-permute-start(bf16[1024,256]{1,0:T(8,128)(2,1)S(1)} %collective-permute-done.4.rest_3_), channel_id=1, source_target_pairs={{0,4},{4,0},{8,12},{12,8},{16,20},{20,16},{24,28},{28,24},{1,5},{5... | collective-permute-start | bytes 1572872 | tf_op jit(solution)/shard_map/ppermute | solution.py:96
  26.8 1.9 %collective-permute-start.13 = (bf16[32,512]{1,0:T(8,128)(2,1)S(1)}, bf16[32,512]{1,0:T(8,128)(2,1)S(1)}, u32[]{:S(2)}, u32[]{:S(2)}) collective-permute-start(bf16[32,512]{1,0:T(8,128)(2,1)S(1)} %collective-permute-done.5.rest_11_), channel_id=1, source_target_pairs={{0,4},{4,0},{8,12},{12,8},{16,20},{20,16},{24,28},{28,24},{1,5},{5... | collective-permute-start | bytes 98312 | tf_op jit(solution)/shard_map/ppermute | solution.py:97
  42.7 4.7 %collective-permute-start.14 = (bf16[1,48,128]{2,1,0:T(8,128)(2,1)S(1)}, bf16[1,48,128]{2,1,0:T(8,128)(2,1)S(1)}, u32[]{:S(2)}, u32[]{:S(2)}) collective-permute-start(bf16[1,48,128]{2,1,0:T(8,128)(2,1)S(1)} %bitcast.5), channel_id=1, source_target_pairs={{0,2},{1,3},{2,0},{3,1},{4,6},{5,7},{6,4},{7,5},{8,10},{9,11},{10,... | collective-permute-start | bytes 36872 | tf_op jit(solution)/shard_map/ppermute | solution.py:41
  47.4 3.8 %collective-permute-start.15 = (bf16[2,48,128]{2,1,0:T(8,128)(2,1)S(1)}, bf16[2,48,128]{2,1,0:T(8,128)(2,1)S(1)}, u32[]{:S(2)}, u32[]{:S(2)}) collective-permute-start(bf16[2,48,128]{2,1,0:T(8,128)(2,1)S(1)} %pad_maximum_fusion.4), channel_id=1, source_target_pairs={{0,1},{1,0},{2,3},{3,2},{4,5},{5,4},{6,7},{7,6},{8,9},{9,8},{10,11... | collective-permute-start | bytes 73736 | tf_op jit(solution)/shard_map/ppermute | solution.py:41
  51.2 4.6 %collective-permute-start.16 = (bf16[4,48,128]{2,1,0:T(8,128)(2,1)S(1)}, bf16[4,48,128]{2,1,0:T(8,128)(2,1)S(1)}, u32[]{:S(2)}, u32[]{:S(2)}) collective-permute-start(bf16[4,48,128]{2,1,0:T(8,128)(2,1)S(1)} %pad_maximum_fusion.2), channel_id=1, source_target_pairs={{0,16},{4,12},{8,24},{12,4},{16,0},{20,28},{24,8},{28,20},{1,17},{... | collective-permute-start | bytes 147464 | tf_op jit(solution)/shard_map/ppermute | solution.py:41
  55.8 4.7 %collective-permute-start.17 = (bf16[8,48,128]{2,1,0:T(8,128)(2,1)S(1)}, bf16[8,48,128]{2,1,0:T(8,128)(2,1)S(1)}, u32[]{:S(2)}, u32[]{:S(2)}) collective-permute-start(bf16[8,48,128]{2,1,0:T(8,128)(2,1)S(1)} %pad_maximum_fusion.1), channel_id=1, source_target_pairs={{0,8},{4,20},{8,0},{12,28},{16,24},{20,4},{24,16},{28,12},{1,9},{5... | collective-permute-start | bytes 294920 | tf_op jit(solution)/shard_map/ppermute | solution.py:41
  60.6 1.5 %collective-permute-start.18 = (bf16[16,48,128]{2,1,0:T(8,128)(2,1)S(1)}, bf16[16,48,128]{2,1,0:T(8,128)(2,1)S(1)}, u32[]{:S(2)}, u32[]{:S(2)}) collective-permute-start(bf16[16,48,128]{2,1,0:T(8,128)(2,1)S(1)} %get-tuple-element.38), channel_id=1, source_target_pairs={{0,4},{4,0},{8,12},{12,8},{16,20},{20,16},{24,28},{28,24},{1,5},{5... | collective-permute-start | bytes 589832 | tf_op jit(solution)/shard_map/ppermute | solution.py:41

commit v4 on v3

--- a/solution.py
+++ b/solution.py
@@ -70,8 +70,8 @@
     pairs = [[(i, i ^ bit_of(i, stage)) for i in range(holders)] for stage in range(stages)]
     swap = [(i, i ^ 1) for i in range(holders)]
 
-    def send(part):
-        return [lax.ppermute(part, "atoms", pair) for pair in pairs]
+    def send(part, ways):
+        return [lax.ppermute(part, "atoms", pair) for pair in ways]
 
     def forward(part, firsts):
         have = [part]
@@ -79,13 +79,16 @@
             have = have + [first] + [lax.ppermute(piece, "atoms", pair) for piece in have[1:]]
         return have
 
-    firsts = send(blocks)
+    firsts = send(blocks, pairs[:1])
     beside = lax.ppermute(blocks, "atoms", swap)
     beside, wanted = lax.optimization_barrier((beside, side()))
-    side_firsts = send(wanted)
+    later, wanted = lax.optimization_barrier((blocks, wanted))
+    firsts = firsts + send(later, pairs[1:])
+    side_firsts = send(wanted, pairs)
+    have = forward(blocks, firsts)
     if stages:
-        firsts[0], side_firsts = lax.optimization_barrier((firsts[0], side_firsts))
-    have, side_have = forward(blocks, firsts), forward(wanted, side_firsts)
+        have[1], side_firsts = lax.optimization_barrier((have[1], side_firsts))
+    side_have = forward(wanted, side_firsts)
     swapped = [beside] + [lax.ppermute(piece, "atoms", swap) for piece in have[1:-1]]
     side_swapped = [lax.ppermute(piece, "atoms", swap) for piece in side_have[:-1]]
     mine = jnp.concatenate([blocks, wanted[:, : blocks.shape[1]]], axis=0)
@@ -203,7 +206,8 @@
     source, target = iota((area, area), 0), iota((area, area), 1)
     wanted = ((target // LANES) * LOW + target % LOW) * BS + (target % LANES) // LOW
     reorder = (source == wanted).astype(jnp.float32).astype(half)
-    identity = (iota((order, order), 0) == iota((order, order), 1)).astype(jnp.float32).astype(half)
+    side = 2 * LANES if order % (2 * LANES) == 0 else LANES
+    identity = (iota((side, side), 0) == iota((side, side), 1)).astype(jnp.float32).astype(half)
     source, target = iota((LANES, LANES), 0), iota((LANES, LANES), 1)
     back = (source == (target % BS) * LOW + target // BS).astype(jnp.float32).astype(half)
     front = (target == (source % BS) * LOW + source // BS).astype(jnp.float32).astype(half)
@@ -258,7 +262,16 @@
         for group in range(groups):
             assemble(task, group)
             yield
-        mirrored = nt(identity, matrix[task].astype(half))
+        plain = matrix[task].astype(half)
+        mirrored = jnp.concatenate(
+            [
+                jnp.concatenate(
+                    [nt(identity, plain[low : low + side, at : at + side]) for low in range(0, order, side)], axis=1
+                )
+                for at in range(0, order, side)
+            ],
+            axis=0,
+        )
         yield
         whole = plus_diagonal(matrix[task] + mirrored, 0.5, -shift_ref[task])
         bound = jnp.max(jnp.sum(jnp.abs(whole), axis=0, keepdims=True), axis=1, keepdims=True) + 1e-06

time: 66 us -> 64.2 us (0.973)
  waiting for transfers between devices: 26.4 us -> 22.9 us
  starting transfers between devices: 18.3 us -> 20 us
    ppermute x4, waiting for transfers between devices: 9.74 us -> 6.26 us  [send(): return [lax.ppermute(part, 'atoms', pair) for pair in ways]]
    ppermute x2, starting transfers between devices: 3.03 us -> 4.87 us  [forward(): lax.ppermute(piece, 'atoms', pair)]
    ppermute x2, waiting for transfers between devices: 3.12 us -> 2.27 us  [forward(): lax.ppermute(piece, 'atoms', pair)]
    ppermute x5, starting transfers between devices: 8.58 us -> 7.88 us  [gather_everywhere(): value = jnp.concatenate([value, lax.ppermute(value, axis, pairs)], axis=0)]
  transfers between devices with their start and end apart: 19 -> 19, of which waited for: 11 -> 9; matrix products, arithmetic and copies ran while one was open for 4% -> 4% of each run, Pallas kernels for 0% -> 0%
where the time goes in v4:
time: 64.2 us; the launch traced here: 63.9 us
  waiting for transfers between devices  22.9 us (36%)
  starting transfers between devices  20 us (31%)
  Pallas kernels  17.4 us (27%)
  other arithmetic  2.64 us (4%)
  between operations  0.79 us (1%)
    pallas_call x1, Pallas kernels, on_device(): pl.pallas_call(functools.partial(density_kernel, holders, atoms_here, lin...  13.8 us
    ppermute x5, waiting for transfers between devices, gather_everywhere(): value = jnp.concatenate([value, lax.ppermute(value, axis, pairs)], axis=0)  11.2 us
    ppermute x5, starting transfers between devices, gather_everywhere(): value = jnp.concatenate([value, lax.ppermute(value, axis, pairs)], axis=0)  7.88 us
    ppermute x4, waiting for transfers between devices, send(): return [lax.ppermute(part, 'atoms', pair) for pair in ways]  6.26 us
    ppermute x4, starting transfers between devices, send(): return [lax.ppermute(part, 'atoms', pair) for pair in ways]  5.09 us
    ppermute x2, starting transfers between devices, forward(): lax.ppermute(piece, 'atoms', pair)  4.87 us
    pallas_call x1, Pallas kernels, on_device(): pl.pallas_call(functools.partial(slab_kernel, tasks), in_specs=[scalars,...  3.63 us
    ppermute x2, waiting for transfers between devices, forward(): lax.ppermute(piece, 'atoms', pair)  2.27 us
  transfers between devices with their start and end apart: 19, of which 9 were waited for; matrix products, arithmetic and copies ran while one was open for 4% of the time, Pallas kernels for 0%

profile of v4, /device:TPU:0, one launch (start us, length us, event | category | flops | bytes accessed | tf_op | source)
XLA Modules:
  0.0 63.9 jit_solution(11092676228317066175)
XLA Ops:
  0.7 0.5 collective-permute-start.2
  1.2 2.6 %collective-permute-start = (bf16[1024,256]{1,0:T(8,128)(2,1)}, bf16[1024,256]{1,0:T(8,128)(2,1)S(1)}, u32[]{:S(2)}, u32[]{:S(2)}) collective-permute-start(bf16[1024,256]{1,0:T(8,128)(2,1)} %bitcast.10), channel_id=1, source_target_pairs={{0,8},{4,20},{8,0},{12,28},{16,24},{20,4},{24,16},{28,12},{1,9},{5... | collective-permute-start | bytes 1572872 | tf_op jit(solution)/shard_map/ppermute | solution.py:74
  3.8 0.7 %fusion.2 = (bf16[32,32]{1,0:T(8,128)(2,1)S(1)}, bf16[32,32]{1,0:T(8,128)(2,1)S(1)}) fusion(s32[32,32]{1,0:T(8,128)} %param.11), kind=kLoop, calls=%fused_computation.24 | loop fusion | flops 21504 | bytes 8192 | tf_op jit(solution)/shard_map/convert
  4.5 0.1 fusion.4
  4.6 0.7 %pad_maximum_fusion.3.rest_8_ = bf16[32,512]{1,0:T(8,128)(2,1)S(1)} fusion(bf16[32,256]{1,0:T(8,128)(2,1)S(1)} %fusion.4, bf16[32,256]{1,0:T(8,128)(2,1)} %param.10), kind=kLoop, calls=%fused_computation.6 | loop fusion | flops 65536 | bytes 65536 | tf_op jit(solution)/shard_map/concatenate | solution.py:405
  5.3 1.5 %collective-permute-start.7 = (bf16[1024,256]{1,0:T(8,128)(2,1)}, bf16[1024,256]{1,0:T(8,128)(2,1)S(1)}, u32[]{:S(2)}, u32[]{:S(2)}) collective-permute-start(bf16[1024,256]{1,0:T(8,128)(2,1)} %bitcast.11), channel_id=1, source_target_pairs={{0,16},{4,12},{8,24},{12,4},{16,0},{20,28},{24,8},{28,20},{1,17},{... | collective-permute-start | bytes 1572872 | tf_op jit(solution)/shard_map/ppermute | solution.py:74
  6.8 0.5 collective-permute-start.3
  7.4 0.5 collective-permute-start.4
  7.8 6.3 %collective-permute-done.rest_1_ = bf16[1024,256]{1,0:T(8,128)(2,1)S(1)} collective-permute-done((bf16[1024,256]{1,0:T(8,128)(2,1)}, bf16[1024,256]{1,0:T(8,128)(2,1)S(1)}, u32[]{:S(2)}, u32[]{:S(2)}) %collective-permute-start) | collective-permute-done | bytes 524320 | tf_op jit(solution)/shard_map/ppermute | solution.py:74
  14.1 3.5 %collective-permute-start.1 = (bf16[1024,256]{1,0:T(8,128)(2,1)S(1)}, bf16[1024,256]{1,0:T(8,128)(2,1)S(1)}, u32[]{:S(2)}, u32[]{:S(2)}) collective-permute-start(bf16[1024,256]{1,0:T(8,128)(2,1)S(1)} %collective-permute-done.rest_1_), channel_id=1, source_target_pairs={{0,16},{4,12},{8,24},{12,4},{16,0},{20,28},{24,8},{28,20},{1,17},{... | collective-permute-start | bytes 1572872 | tf_op jit(solution)/shard_map/ppermute | solution.py:79
  17.6 0.5 collective-permute-start.8
  18.1 0.1 collective-permute-start.9
  18.2 0.4 collective-permute-start.10
  18.6 1.7 %collective-permute-done.9.rest_12_ = bf16[32,512]{1,0:T(8,128)(2,1)S(1)} collective-permute-done((bf16[32,512]{1,0:T(8,128)(2,1)S(1)}, bf16[32,512]{1,0:T(8,128)(2,1)S(1)}, u32[]{:S(2)}, u32[]{:S(2)}) %collective-permute-start.9) | collective-permute-done | bytes 32800 | tf_op jit(solution)/shard_map/ppermute | solution.py:93
  20.3 1.4 %collective-permute-start.5 = (bf16[32,512]{1,0:T(8,128)(2,1)S(1)}, bf16[32,512]{1,0:T(8,128)(2,1)S(1)}, u32[]{:S(2)}, u32[]{:S(2)}) collective-permute-start(bf16[32,512]{1,0:T(8,128)(2,1)S(1)} %collective-permute-done.3.rest_9_), channel_id=1, source_target_pairs={{0,16},{4,12},{8,24},{12,4},{16,0},{20,28},{24,8},{28,20},{1,17},{... | collective-permute-start | bytes 98312 | tf_op jit(solution)/shard_map/ppermute | solution.py:79
  21.7 1.1 %pad_maximum_fusion.rest_0_ = bf16[1056,256]{1,0:T(8,128)(2,1)S(1)} fusion(bf16[32,256]{1,0:T(8,128)(2,1)S(1)} %slice.3, bf16[1024,256]{1,0:T(8,128)(2,1)} %bitcast.12), kind=kLoop, calls=%fused_computation | loop fusion | flops 1081344 | bytes 1081344 | tf_op jit(solution)/shard_map/concatenate | solution.py:94
  22.8 2.3 %collective-permute-done.5.rest_11_ = bf16[32,512]{1,0:T(8,128)(2,1)S(1)} collective-permute-done((bf16[32,512]{1,0:T(8,128)(2,1)S(1)}, bf16[32,512]{1,0:T(8,128)(2,1)S(1)}, u32[]{:S(2)}, u32[]{:S(2)}) %collective-permute-start.5) | collective-permute-done | bytes 32800 | tf_op jit(solution)/shard_map/ppermute | solution.py:79
  25.1 0.1 collective-permute-start.12
  25.2 0.5 collective-permute-start.13
  25.7 1.4 %collective-permute-done.13.rest_15_ = bf16[32,512]{1,0:T(8,128)(2,1)S(1)} collective-permute-done((bf16[32,512]{1,0:T(8,128)(2,1)S(1)}, bf16[32,512]{1,0:T(8,128)(2,1)S(1)}, u32[]{:S(2)}, u32[]{:S(2)}) %collective-permute-start.13) | collective-permute-done | bytes 32800 | tf_op jit(solution)/shard_map/ppermute | solution.py:100
  27.2 13.8 %shard_map.104 = (bf16[4,512,128]{2,1,0:T(8,128)(2,1)}, bf16[48,128]{1,0:T(8,128)(2,1)S(1)}) custom-call(f32[4]{0:T(128)S(1)} %copy-done.1, s32[4]{0:T(128)S(1)} %copy-done.2, s32[4]{0:T(128)S(1)} %copy-done.3, s32[4]{0:T(128)S(1)} %copy-done.4, s32[4,32]{1,0:T(4,128)S(1)} %copy-done, bf16[4,512,1024]{2,1,0:T(8,128)(2,1)} %basis_hbm.1, ...), custom_call_target="tpu_custom_call" | custom-call | tf_op jit(solution)/shard_map/pallas_call | solution.py:412
  41.0 2.6 %collective-permute-start.14 = (bf16[1,48,128]{2,1,0:T(8,128)(2,1)S(1)}, bf16[1,48,128]{2,1,0:T(8,128)(2,1)S(1)}, u32[]{:S(2)}, u32[]{:S(2)}) collective-permute-start(bf16[1,48,128]{2,1,0:T(8,128)(2,1)S(1)} %bitcast.5), channel_id=1, source_target_pairs={{0,2},{1,3},{2,0},{3,1},{4,6},{5,7},{6,4},{7,5},{8,10},{9,11},{10,... | collective-permute-start | bytes 36872 | tf_op jit(solution)/shard_map/ppermute | solution.py:41
  43.6 2.0 %collective-permute-done.14 = bf16[1,48,128]{2,1,0:T(8,128)(2,1)S(1)} collective-permute-done((bf16[1,48,128]{2,1,0:T(8,128)(2,1)S(1)}, bf16[1,48,128]{2,1,0:T(8,128)(2,1)S(1)}, u32[]{:S(2)}, u32[]{:S(2)}) %collective-permute-start.14) | collective-permute-done | bytes 12320 | tf_op jit(solution)/shard_map/ppermute | solution.py:41
  45.6 1.6 %collective-permute-start.15 = (bf16[2,48,128]{2,1,0:T(8,128)(2,1)S(1)}, bf16[2,48,128]{2,1,0:T(8,128)(2,1)S(1)}, u32[]{:S(2)}, u32[]{:S(2)}) collective-permute-start(bf16[2,48,128]{2,1,0:T(8,128)(2,1)S(1)} %pad_maximum_fusion.4), channel_id=1, source_target_pairs={{0,1},{1,0},{2,3},{3,2},{4,5},{5,4},{6,7},{7,6},{8,9},{9,8},{10,11... | collective-permute-start | bytes 73736 | tf_op jit(solution)/shard_map/ppermute | solution.py:41
  47.2 2.3 %collective-permute-done.15 = bf16[2,48,128]{2,1,0:T(8,128)(2,1)S(1)} collective-permute-done((bf16[2,48,128]{2,1,0:T(8,128)(2,1)S(1)}, bf16[2,48,128]{2,1,0:T(8,128)(2,1)S(1)}, u32[]{:S(2)}, u32[]{:S(2)}) %collective-permute-start.15) | collective-permute-done | bytes 24608 | tf_op jit(solution)/shard_map/ppermute | solution.py:41
  49.5 2.1 %collective-permute-start.16 = (bf16[4,48,128]{2,1,0:T(8,128)(2,1)S(1)}, bf16[4,48,128]{2,1,0:T(8,128)(2,1)S(1)}, u32[]{:S(2)}, u32[]{:S(2)}) collective-permute-start(bf16[4,48,128]{2,1,0:T(8,128)(2,1)S(1)} %pad_maximum_fusion.2), channel_id=1, source_target_pairs={{0,16},{4,12},{8,24},{12,4},{16,0},{20,28},{24,8},{28,20},{1,17},{... | collective-permute-start | bytes 147464 | tf_op jit(solution)/shard_map/ppermute | solution.py:41
  51.6 2.4 %collective-permute-done.16 = bf16[4,48,128]{2,1,0:T(8,128)(2,1)S(1)} collective-permute-done((bf16[4,48,128]{2,1,0:T(8,128)(2,1)S(1)}, bf16[4,48,128]{2,1,0:T(8,128)(2,1)S(1)}, u32[]{:S(2)}, u32[]{:S(2)}) %collective-permute-start.16) | collective-permute-done | bytes 49184 | tf_op jit(solution)/shard_map/ppermute | solution.py:41
  54.0 1.5 %collective-permute-start.17 = (bf16[8,48,128]{2,1,0:T(8,128)(2,1)S(1)}, bf16[8,48,128]{2,1,0:T(8,128)(2,1)S(1)}, u32[]{:S(2)}, u32[]{:S(2)}) collective-permute-start(bf16[8,48,128]{2,1,0:T(8,128)(2,1)S(1)} %pad_maximum_fusion.1), channel_id=1, source_target_pairs={{0,8},{4,20},{8,0},{12,28},{16,24},{20,4},{24,16},{28,12},{1,9},{5... | collective-permute-start | bytes 294920 | tf_op jit(solution)/shard_map/ppermute | solution.py:41
  55.6 3.1 %collective-permute-done.17 = bf16[8,48,128]{2,1,0:T(8,128)(2,1)S(1)} collective-permute-done((bf16[8,48,128]{2,1,0:T(8,128)(2,1)S(1)}, bf16[8,48,128]{2,1,0:T(8,128)(2,1)S(1)}, u32[]{:S(2)}, u32[]{:S(2)}) %collective-permute-start.17) | collective-permute-done | bytes 98336 | tf_op jit(solution)/shard_map/ppermute | solution.py:41
  58.7 0.1 collective-permute-start.18
  58.8 1.4 %collective-permute-done.18 = bf16[16,48,128]{2,1,0:T(8,128)(2,1)S(1)} collective-permute-done((bf16[16,48,128]{2,1,0:T(8,128)(2,1)S(1)}, bf16[16,48,128]{2,1,0:T(8,128)(2,1)S(1)}, u32[]{:S(2)}, u32[]{:S(2)}) %collective-permute-start.18) | collective-permute-done | bytes 196640 | tf_op jit(solution)/shard_map/ppermute | solution.py:41
  60.3 3.6 %shard_map.105 = f32[64,32,128]{2,1,0:T(8,128)} custom-call(s32[1]{0:T(128)} %bitcast.1.slab_number_ref, bf16[32,48,128]{2,1,0:T(8,128)(2,1)S(1)} %constant_dynamic-update-slice_fusion.5.boxes_ref), custom_call_target="tpu_custom_call" | custom-call | tf_op jit(solution)/shard_map/pallas_call | solution.py:449
  (32 shorter events, 0.2 us)
Async XLA Ops:
  0.6 26.5 %copy-start = (s32[4,32]{1,0:T(4,128)S(1)}, s32[4,32]{1,0:T(4,128)}, u32[]{:S(2)}) copy-start(s32[4,32]{1,0:T(4,128)} %members_ref.1) | copy-start | bytes 1540
  0.6 26.5 %copy-start.1 = (f32[4]{0:T(128)S(1)}, f32[4]{0:T(128)}, u32[]{:S(2)}) copy-start(f32[4]{0:T(128)} %shift_ref.1) | copy-start | bytes 52
  0.7 26.5 %copy-start.2 = (s32[4]{0:T(128)S(1)}, s32[4]{0:T(128)}, u32[]{:S(2)}) copy-start(s32[4]{0:T(128)} %start_ref.1) | copy-start | bytes 52
  0.7 26.5 %copy-start.3 = (s32[4]{0:T(128)S(1)}, s32[4]{0:T(128)}, u32[]{:S(2)}) copy-start(s32[4]{0:T(128)} %row_ref.1) | copy-start | bytes 52
  0.7 26.5 %copy-start.4 = (s32[4]{0:T(128)S(1)}, s32[4]{0:T(128)}, u32[]{:S(2)}) copy-start(s32[4]{0:T(128)} %col_ref.1) | copy-start | bytes 52
  0.7 4.6 %collective-permute-start.2 = (bf16[1024,256]{1,0:T(8,128)(2,1)}, bf16[1024,256]{1,0:T(8,128)(2,1)S(1)}, u32[]{:S(2)}, u32[]{:S(2)}) collective-permute-start(bf16[1024,256]{1,0:T(8,128)(2,1)} %bitcast.9), channel_id=1, source_target_pairs={{0,4},{4,0},{8,12},{12,8},{16,20},{20,16},{24,28},{28,24},{1,5},{5... | collective-permute-start | bytes 1572872 | tf_op jit(solution)/shard_map/ppermute | solution.py:83
  1.2 12.9 %collective-permute-start = (bf16[1024,256]{1,0:T(8,128)(2,1)}, bf16[1024,256]{1,0:T(8,128)(2,1)S(1)}, u32[]{:S(2)}, u32[]{:S(2)}) collective-permute-start(bf16[1024,256]{1,0:T(8,128)(2,1)} %bitcast.10), channel_id=1, source_target_pairs={{0,8},{4,20},{8,0},{12,28},{16,24},{20,4},{24,16},{28,12},{1,9},{5... | collective-permute-start | bytes 1572872 | tf_op jit(solution)/shard_map/ppermute | solution.py:74
  5.3 12.3 %collective-permute-start.7 = (bf16[1024,256]{1,0:T(8,128)(2,1)}, bf16[1024,256]{1,0:T(8,128)(2,1)S(1)}, u32[]{:S(2)}, u32[]{:S(2)}) collective-permute-start(bf16[1024,256]{1,0:T(8,128)(2,1)} %bitcast.11), channel_id=1, source_target_pairs={{0,16},{4,12},{8,24},{12,4},{16,0},{20,28},{24,8},{28,20},{1,17},{... | collective-permute-start | bytes 1572872 | tf_op jit(solution)/shard_map/ppermute | solution.py:74
  6.8 10.7 %collective-permute-start.3 = (bf16[32,512]{1,0:T(8,128)(2,1)S(1)}, bf16[32,512]{1,0:T(8,128)(2,1)S(1)}, u32[]{:S(2)}, u32[]{:S(2)}) collective-permute-start(bf16[32,512]{1,0:T(8,128)(2,1)S(1)} %pad_maximum_fusion.3.rest_8_), channel_id=1, source_target_pairs={{0,8},{4,20},{8,0},{12,28},{16,24},{20,4},{24,16},{28,12},{1,9},{5... | collective-permute-start | bytes 98312 | tf_op jit(solution)/shard_map/ppermute | solution.py:74
  7.4 10.2 %collective-permute-start.4 = (bf16[32,512]{1,0:T(8,128)(2,1)S(1)}, bf16[32,512]{1,0:T(8,128)(2,1)S(1)}, u32[]{:S(2)}, u32[]{:S(2)}) collective-permute-start(bf16[32,512]{1,0:T(8,128)(2,1)S(1)} %pad_maximum_fusion.3.rest_8_), channel_id=1, source_target_pairs={{0,16},{4,12},{8,24},{12,4},{16,0},{20,28},{24,8},{28,20},{1,17},{... | collective-permute-start | bytes 98312 | tf_op jit(solution)/shard_map/ppermute | solution.py:74
  14.1 11.0 %collective-permute-start.1 = (bf16[1024,256]{1,0:T(8,128)(2,1)S(1)}, bf16[1024,256]{1,0:T(8,128)(2,1)S(1)}, u32[]{:S(2)}, u32[]{:S(2)}) collective-permute-start(bf16[1024,256]{1,0:T(8,128)(2,1)S(1)} %collective-permute-done.rest_1_), channel_id=1, source_target_pairs={{0,16},{4,12},{8,24},{12,4},{16,0},{20,28},{24,8},{28,20},{1,17},{... | collective-permute-start | bytes 1572872 | tf_op jit(solution)/shard_map/ppermute | solution.py:79
  17.6 7.5 %collective-permute-start.6 = (bf16[1024,256]{1,0:T(8,128)(2,1)S(1)}, bf16[1024,256]{1,0:T(8,128)(2,1)S(1)}, u32[]{:S(2)}, u32[]{:S(2)}) collective-permute-start(bf16[1024,256]{1,0:T(8,128)(2,1)S(1)} %collective-permute-done.rest_1_), channel_id=1, source_target_pairs={{0,4},{4,0},{8,12},{12,8},{16,20},{20,16},{24,28},{28,24},{1,5},{5... | collective-permute-start | bytes 1572872 | tf_op jit(solution)/shard_map/ppermute | solution.py:92
  17.6 7.5 %collective-permute-start.8 = (bf16[1024,256]{1,0:T(8,128)(2,1)S(1)}, bf16[1024,256]{1,0:T(8,128)(2,1)S(1)}, u32[]{:S(2)}, u32[]{:S(2)}) collective-permute-start(bf16[1024,256]{1,0:T(8,128)(2,1)S(1)} %collective-permute-done.7.rest_2_), channel_id=1, source_target_pairs={{0,4},{4,0},{8,12},{12,8},{16,20},{20,16},{24,28},{28,24},{1,5},{5... | collective-permute-start | bytes 1572872 | tf_op jit(solution)/shard_map/ppermute | solution.py:92
  18.1 2.2 %collective-permute-start.9 = (bf16[32,512]{1,0:T(8,128)(2,1)S(1)}, bf16[32,512]{1,0:T(8,128)(2,1)S(1)}, u32[]{:S(2)}, u32[]{:S(2)}) collective-permute-start(bf16[32,512]{1,0:T(8,128)(2,1)S(1)} %pad_maximum_fusion.3.rest_8_), channel_id=1, source_target_pairs={{0,4},{4,0},{8,12},{12,8},{16,20},{20,16},{24,28},{28,24},{1,5},{5... | collective-permute-start | bytes 98312 | tf_op jit(solution)/shard_map/ppermute | solution.py:93
  18.2 3.5 %collective-permute-start.10 = (bf16[32,512]{1,0:T(8,128)(2,1)S(1)}, bf16[32,512]{1,0:T(8,128)(2,1)S(1)}, u32[]{:S(2)}, u32[]{:S(2)}) collective-permute-start(bf16[32,512]{1,0:T(8,128)(2,1)S(1)} %collective-permute-done.3.rest_9_), channel_id=1, source_target_pairs={{0,4},{4,0},{8,12},{12,8},{16,20},{20,16},{24,28},{28,24},{1,5},{5... | collective-permute-start | bytes 98312 | tf_op jit(solution)/shard_map/ppermute | solution.py:93
  20.3 4.8 %collective-permute-start.5 = (bf16[32,512]{1,0:T(8,128)(2,1)S(1)}, bf16[32,512]{1,0:T(8,128)(2,1)S(1)}, u32[]{:S(2)}, u32[]{:S(2)}) collective-permute-start(bf16[32,512]{1,0:T(8,128)(2,1)S(1)} %collective-permute-done.3.rest_9_), channel_id=1, source_target_pairs={{0,16},{4,12},{8,24},{12,4},{16,0},{20,28},{24,8},{28,20},{1,17},{... | collective-permute-start | bytes 98312 | tf_op jit(solution)/shard_map/ppermute | solution.py:79
  21.7 3.4 %collective-permute-start.11 = (bf16[32,512]{1,0:T(8,128)(2,1)S(1)}, bf16[32,512]{1,0:T(8,128)(2,1)S(1)}, u32[]{:S(2)}, u32[]{:S(2)}) collective-permute-start(bf16[32,512]{1,0:T(8,128)(2,1)S(1)} %collective-permute-done.4.rest_10_), channel_id=1, source_target_pairs={{0,4},{4,0},{8,12},{12,8},{16,20},{20,16},{24,28},{28,24},{1,5},{5... | collective-permute-start | bytes 98312 | tf_op jit(solution)/shard_map/ppermute | solution.py:93
  25.1 2.0 %collective-permute-start.12 = (bf16[1024,256]{1,0:T(8,128)(2,1)S(1)}, bf16[1024,256]{1,0:T(8,128)(2,1)S(1)}, u32[]{:S(2)}, u32[]{:S(2)}) collective-permute-start(bf16[1024,256]{1,0:T(8,128)(2,1)S(1)} %collective-permute-done.1.rest_3_), channel_id=1, source_target_pairs={{0,4},{4,0},{8,12},{12,8},{16,20},{20,16},{24,28},{28,24},{1,5},{5... | collective-permute-start | bytes 1572872 | tf_op jit(solution)/shard_map/ppermute | solution.py:99
  25.2 1.9 %collective-permute-start.13 = (bf16[32,512]{1,0:T(8,128)(2,1)S(1)}, bf16[32,512]{1,0:T(8,128)(2,1)S(1)}, u32[]{:S(2)}, u32[]{:S(2)}) collective-permute-start(bf16[32,512]{1,0:T(8,128)(2,1)S(1)} %collective-permute-done.5.rest_11_), channel_id=1, source_target_pairs={{0,4},{4,0},{8,12},{12,8},{16,20},{20,16},{24,28},{28,24},{1,5},{5... | collective-permute-start | bytes 98312 | tf_op jit(solution)/shard_map/ppermute | solution.py:100
  41.0 4.7 %collective-permute-start.14 = (bf16[1,48,128]{2,1,0:T(8,128)(2,1)S(1)}, bf16[1,48,128]{2,1,0:T(8,128)(2,1)S(1)}, u32[]{:S(2)}, u32[]{:S(2)}) collective-permute-start(bf16[1,48,128]{2,1,0:T(8,128)(2,1)S(1)} %bitcast.5), channel_id=1, source_target_pairs={{0,2},{1,3},{2,0},{3,1},{4,6},{5,7},{6,4},{7,5},{8,10},{9,11},{10,... | collective-permute-start | bytes 36872 | tf_op jit(solution)/shard_map/ppermute | solution.py:41
  45.6 3.8 %collective-permute-start.15 = (bf16[2,48,128]{2,1,0:T(8,128)(2,1)S(1)}, bf16[2,48,128]{2,1,0:T(8,128)(2,1)S(1)}, u32[]{:S(2)}, u32[]{:S(2)}) collective-permute-start(bf16[2,48,128]{2,1,0:T(8,128)(2,1)S(1)} %pad_maximum_fusion.4), channel_id=1, source_target_pairs={{0,1},{1,0},{2,3},{3,2},{4,5},{5,4},{6,7},{7,6},{8,9},{9,8},{10,11... | collective-permute-start | bytes 73736 | tf_op jit(solution)/shard_map/ppermute | solution.py:41
  49.5 4.5 %collective-permute-start.16 = (bf16[4,48,128]{2,1,0:T(8,128)(2,1)S(1)}, bf16[4,48,128]{2,1,0:T(8,128)(2,1)S(1)}, u32[]{:S(2)}, u32[]{:S(2)}) collective-permute-start(bf16[4,48,128]{2,1,0:T(8,128)(2,1)S(1)} %pad_maximum_fusion.2), channel_id=1, source_target_pairs={{0,16},{4,12},{8,24},{12,4},{16,0},{20,28},{24,8},{28,20},{1,17},{... | collective-permute-start | bytes 147464 | tf_op jit(solution)/shard_map/ppermute | solution.py:41
  54.0 4.7 %collective-permute-start.17 = (bf16[8,48,128]{2,1,0:T(8,128)(2,1)S(1)}, bf16[8,48,128]{2,1,0:T(8,128)(2,1)S(1)}, u32[]{:S(2)}, u32[]{:S(2)}) collective-permute-start(bf16[8,48,128]{2,1,0:T(8,128)(2,1)S(1)} %pad_maximum_fusion.1), channel_id=1, source_target_pairs={{0,8},{4,20},{8,0},{12,28},{16,24},{20,4},{24,16},{28,12},{1,9},{5... | collective-permute-start | bytes 294920 | tf_op jit(solution)/shard_map/ppermute | solution.py:41
  58.7 1.5 %collective-permute-start.18 = (bf16[16,48,128]{2,1,0:T(8,128)(2,1)S(1)}, bf16[16,48,128]{2,1,0:T(8,128)(2,1)S(1)}, u32[]{:S(2)}, u32[]{:S(2)}) collective-permute-start(bf16[16,48,128]{2,1,0:T(8,128)(2,1)S(1)} %get-tuple-element.42), channel_id=1, source_target_pairs={{0,4},{4,0},{8,12},{12,8},{16,20},{20,16},{24,28},{28,24},{1,5},{5... | collective-permute-start | bytes 589832 | tf_op jit(solution)/shard_map/ppermute | solution.py:41

commit v5 on v4

--- a/solution.py
+++ b/solution.py
@@ -36,8 +36,6 @@
         steps = [1 << bit for bit in range(size.bit_length() - 1)][::-1]
         for stage, step in enumerate(steps):
             pairs = [(i, i ^ step) for i in range(size)]
-            if axis == "atoms" and step > 1:
-                pairs = [(i, i ^ (steps[len(steps) - 2 - stage] if i & 1 else step)) for i in range(size)]
             value = jnp.concatenate([value, lax.ppermute(value, axis, pairs)], axis=0)
     return value
 
@@ -141,12 +139,11 @@
 ):
     pieces, extras = rest[:holders], rest[holders : 2 * holders]
     (
-        density_hbm,
+        density,
         box_ref,
         cols,
         sides,
         basis,
-        density,
         ids_all,
         onsite_all,
         product,
@@ -156,7 +153,6 @@
         place_sem,
         sems,
         basis_sems,
-        density_sems,
     ) = rest[2 * holders :]
     half = jnp.bfloat16
     tasks, set_size = members_ref.shape
@@ -171,7 +167,6 @@
             target = whole.at[pl.ds(number * count, count)]
             copies.append(pltpu.make_async_copy(part.at[pl.ds(0, count)], target, sems.at[kind, number]))
     loads = [pltpu.make_async_copy(basis_hbm.at[t], basis.at[t], basis_sems.at[t]) for t in range(tasks)]
-    stores = [pltpu.make_async_copy(density.at[t], density_hbm.at[t], density_sems.at[t]) for t in range(tasks)]
     for copy in copies:
         copy.start()
     held_by, held_at = split(members_ref[...], atoms_here)
@@ -237,6 +232,7 @@
         for low in range(LOW):
             row = low * set_size + group * LOW + low
             spot[pl.ds(row, 1), :] = onsite_all[pl.ds(base + low, 1), :]
+        yield
         ordered = nn(spot[...].astype(half), reorder)
         for high in range(area // LANES):
             tiles = [
@@ -260,7 +256,7 @@
 
     def steps_of(task):
         for group in range(groups):
-            assemble(task, group)
+            yield from assemble(task, group)
             yield
         plain = matrix[task].astype(half)
         mirrored = jnp.concatenate(
@@ -293,10 +289,12 @@
             part = slice(upper * LANES, (upper + 1) * LANES)
             density[task, part, :] = nn(front, mid[part]).astype(half)
             wide.append(nn(tall[:, part], back).astype(half))
-        stores[task].start()
-        yield
-        loads[task].wait()
+        yield
+        if task == 0:
+            for load in loads:
+                load.wait()
         weights = nn(jnp.concatenate(wide, axis=1), basis[task])
+        yield
         values = jnp.sum(weights * basis[task, :CENTRAL, :].astype(jnp.float32), axis=0, keepdims=True)
         rows = values.shape[1] // LANES
         box = jnp.concatenate([values[:, row * LANES : (row + 1) * LANES] for row in range(rows)], axis=0)
@@ -325,8 +323,6 @@
     box_ref[...] = jnp.concatenate(
         box_rows + [corner, jnp.zeros((rest_rows, LANES), jnp.float32)], axis=0
     ).astype(half)
-    for store in stores:
-        store.wait()
 
 
 def slab_kernel(tasks, slab_number_ref, boxes_ref, slab_ref, work, wide, unfolded, corner_vmem, corners, chosen, sem):
@@ -352,7 +348,7 @@
             count += jnp.logical_and(first > -BOXP, first < planes).astype(jnp.int32)
         return count
 
-    count = lax.fori_loop(0, devices, look, 0)
+    count = lax.fori_loop(0, devices, look, 0, unroll=4 if devices % 4 == 0 else 1)
     for extra in range(BATCH):
         chosen[count + extra] = -1
 
@@ -412,7 +408,7 @@
     density, boxes = pl.pallas_call(
         functools.partial(density_kernel, holders, atoms_here, links),
         in_specs=[scalars] * 4 + [vectors, pl.BlockSpec(memory_space=pltpu.HBM)] + [everything] * (2 * holders),
-        out_specs=[everything, vectors],
+        out_specs=[vectors, vectors],
         out_shape=[
             jax.ShapeDtypeStruct((tasks, order, CENTRAL), half),
             jax.ShapeDtypeStruct((box_rows, LANES), half),
@@ -421,7 +417,6 @@
             pltpu.VMEM((holders * atoms_here * links, area), half),
             pltpu.VMEM((holders * atoms_here, 2 * area), half),
             pltpu.VMEM((tasks, order, points), half),
-            pltpu.VMEM((tasks, order, CENTRAL), half),
             pltpu.VMEM((tasks * set_size, LOW * links), jnp.float32),
             pltpu.VMEM((tasks * set_size, area), jnp.float32),
             pltpu.VMEM((tasks, 2, LOW * set_size, area), jnp.float32),
@@ -430,7 +425,6 @@
             pltpu.SMEM((tasks, set_size), jnp.int32),
             pltpu.SemaphoreType.DMA,
             pltpu.SemaphoreType.DMA((2, holders)),
-            pltpu.SemaphoreType.DMA((tasks,)),
             pltpu.SemaphoreType.DMA((tasks,)),
         ],
         compiler_params=pltpu.CompilerParams(vmem_limit_bytes=48 * 1024 * 1024),

time: 64.2 us -> 63.4 us (0.988)
  no operation moved by 1% of the time
where the time goes in v5:
time: 63.4 us; the launch traced here: 63.2 us
  waiting for transfers between devices  22.6 us (36%)
  starting transfers between devices  20 us (32%)
  Pallas kernels  17.1 us (27%)
  other arithmetic  2.64 us (4%)
  between operations  0.79 us (1%)
    pallas_call x1, Pallas kernels, on_device(): pl.pallas_call(functools.partial(density_kernel, holders, atoms_here, lin...  13.5 us
    ppermute x5, waiting for transfers between devices, gather_everywhere(): value = jnp.concatenate([value, lax.ppermute(value, axis, pairs)], axis=0)  10.9 us
    ppermute x5, starting transfers between devices, gather_everywhere(): value = jnp.concatenate([value, lax.ppermute(value, axis, pairs)], axis=0)  7.87 us
    ppermute x4, waiting for transfers between devices, send(): return [lax.ppermute(part, 'atoms', pair) for pair in ways]  6.26 us
    ppermute x4, starting transfers between devices, send(): return [lax.ppermute(part, 'atoms', pair) for pair in ways]  5.09 us
    ppermute x2, starting transfers between devices, forward(): lax.ppermute(piece, 'atoms', pair)  4.87 us
    pallas_call x1, Pallas kernels, on_device(): pl.pallas_call(functools.partial(slab_kernel, tasks), in_specs=[scalars,...  3.55 us
    ppermute x2, waiting for transfers between devices, forward(): lax.ppermute(piece, 'atoms', pair)  2.27 us
  transfers between devices with their start and end apart: 19, of which 9 were waited for; matrix products, arithmetic and copies ran while one was open for 4% of the time, Pallas kernels for 0%

profile of v5, /device:TPU:0, one launch (start us, length us, event | category | flops | bytes accessed | tf_op | source)
XLA Modules:
  0.0 63.2 jit_solution(4694885037557642782)
XLA Ops:
  0.7 0.5 collective-permute-start.2
  1.2 2.6 %collective-permute-start = (bf16[1024,256]{1,0:T(8,128)(2,1)}, bf16[1024,256]{1,0:T(8,128)(2,1)S(1)}, u32[]{:S(2)}, u32[]{:S(2)}) collective-permute-start(bf16[1024,256]{1,0:T(8,128)(2,1)} %bitcast.10), channel_id=1, source_target_pairs={{0,8},{4,20},{8,0},{12,28},{16,24},{20,4},{24,16},{28,12},{1,9},{5... | collective-permute-start | bytes 1572872 | tf_op jit(solution)/shard_map/ppermute | solution.py:72
  3.8 0.7 %fusion.2 = (bf16[32,32]{1,0:T(8,128)(2,1)S(1)}, bf16[32,32]{1,0:T(8,128)(2,1)S(1)}) fusion(s32[32,32]{1,0:T(8,128)} %param.11), kind=kLoop, calls=%fused_computation.24 | loop fusion | flops 21504 | bytes 8192 | tf_op jit(solution)/shard_map/convert
  4.5 0.1 fusion.4
  4.6 0.7 %pad_maximum_fusion.3.rest_8_ = bf16[32,512]{1,0:T(8,128)(2,1)S(1)} fusion(bf16[32,256]{1,0:T(8,128)(2,1)S(1)} %fusion.4, bf16[32,256]{1,0:T(8,128)(2,1)} %param.10), kind=kLoop, calls=%fused_computation.6 | loop fusion | flops 65536 | bytes 65536 | tf_op jit(solution)/shard_map/concatenate | solution.py:401
  5.3 1.5 %collective-permute-start.7 = (bf16[1024,256]{1,0:T(8,128)(2,1)}, bf16[1024,256]{1,0:T(8,128)(2,1)S(1)}, u32[]{:S(2)}, u32[]{:S(2)}) collective-permute-start(bf16[1024,256]{1,0:T(8,128)(2,1)} %bitcast.11), channel_id=1, source_target_pairs={{0,16},{4,12},{8,24},{12,4},{16,0},{20,28},{24,8},{28,20},{1,17},{... | collective-permute-start | bytes 1572872 | tf_op jit(solution)/shard_map/ppermute | solution.py:72
  6.8 0.5 collective-permute-start.3
  7.4 0.5 collective-permute-start.4
  7.8 6.3 %collective-permute-done.rest_1_ = bf16[1024,256]{1,0:T(8,128)(2,1)S(1)} collective-permute-done((bf16[1024,256]{1,0:T(8,128)(2,1)}, bf16[1024,256]{1,0:T(8,128)(2,1)S(1)}, u32[]{:S(2)}, u32[]{:S(2)}) %collective-permute-start) | collective-permute-done | bytes 524320 | tf_op jit(solution)/shard_map/ppermute | solution.py:72
  14.1 3.5 %collective-permute-start.1 = (bf16[1024,256]{1,0:T(8,128)(2,1)S(1)}, bf16[1024,256]{1,0:T(8,128)(2,1)S(1)}, u32[]{:S(2)}, u32[]{:S(2)}) collective-permute-start(bf16[1024,256]{1,0:T(8,128)(2,1)S(1)} %collective-permute-done.rest_1_), channel_id=1, source_target_pairs={{0,16},{4,12},{8,24},{12,4},{16,0},{20,28},{24,8},{28,20},{1,17},{... | collective-permute-start | bytes 1572872 | tf_op jit(solution)/shard_map/ppermute | solution.py:77
  17.6 0.5 collective-permute-start.8
  18.1 0.1 collective-permute-start.9
  18.2 0.4 collective-permute-start.10
  18.6 1.7 %collective-permute-done.9.rest_12_ = bf16[32,512]{1,0:T(8,128)(2,1)S(1)} collective-permute-done((bf16[32,512]{1,0:T(8,128)(2,1)S(1)}, bf16[32,512]{1,0:T(8,128)(2,1)S(1)}, u32[]{:S(2)}, u32[]{:S(2)}) %collective-permute-start.9) | collective-permute-done | bytes 32800 | tf_op jit(solution)/shard_map/ppermute | solution.py:91
  20.3 1.4 %collective-permute-start.5 = (bf16[32,512]{1,0:T(8,128)(2,1)S(1)}, bf16[32,512]{1,0:T(8,128)(2,1)S(1)}, u32[]{:S(2)}, u32[]{:S(2)}) collective-permute-start(bf16[32,512]{1,0:T(8,128)(2,1)S(1)} %collective-permute-done.3.rest_9_), channel_id=1, source_target_pairs={{0,16},{4,12},{8,24},{12,4},{16,0},{20,28},{24,8},{28,20},{1,17},{... | collective-permute-start | bytes 98312 | tf_op jit(solution)/shard_map/ppermute | solution.py:77
  21.7 1.1 %pad_maximum_fusion.rest_0_ = bf16[1056,256]{1,0:T(8,128)(2,1)S(1)} fusion(bf16[32,256]{1,0:T(8,128)(2,1)S(1)} %slice.3, bf16[1024,256]{1,0:T(8,128)(2,1)} %bitcast.12), kind=kLoop, calls=%fused_computation | loop fusion | flops 1081344 | bytes 1081344 | tf_op jit(solution)/shard_map/concatenate | solution.py:92
  22.8 2.3 %collective-permute-done.5.rest_11_ = bf16[32,512]{1,0:T(8,128)(2,1)S(1)} collective-permute-done((bf16[32,512]{1,0:T(8,128)(2,1)S(1)}, bf16[32,512]{1,0:T(8,128)(2,1)S(1)}, u32[]{:S(2)}, u32[]{:S(2)}) %collective-permute-start.5) | collective-permute-done | bytes 32800 | tf_op jit(solution)/shard_map/ppermute | solution.py:77
  25.1 0.1 collective-permute-start.12
  25.2 0.5 collective-permute-start.13
  25.7 1.4 %collective-permute-done.13.rest_15_ = bf16[32,512]{1,0:T(8,128)(2,1)S(1)} collective-permute-done((bf16[32,512]{1,0:T(8,128)(2,1)S(1)}, bf16[32,512]{1,0:T(8,128)(2,1)S(1)}, u32[]{:S(2)}, u32[]{:S(2)}) %collective-permute-start.13) | collective-permute-done | bytes 32800 | tf_op jit(solution)/shard_map/ppermute | solution.py:98
  27.2 13.5 %shard_map.104 = (bf16[4,512,128]{2,1,0:T(8,128)(2,1)}, bf16[48,128]{1,0:T(8,128)(2,1)S(1)}) custom-call(f32[4]{0:T(128)S(1)} %copy-done.1, s32[4]{0:T(128)S(1)} %copy-done.2, s32[4]{0:T(128)S(1)} %copy-done.3, s32[4]{0:T(128)S(1)} %copy-done.4, s32[4,32]{1,0:T(4,128)S(1)} %copy-done, bf16[4,512,1024]{2,1,0:T(8,128)(2,1)} %basis_hbm.1, ...), custom_call_target="tpu_custom_call" | custom-call | tf_op jit(solution)/shard_map/pallas_call | solution.py:408
  40.7 2.6 %collective-permute-start.14 = (bf16[1,48,128]{2,1,0:T(8,128)(2,1)S(1)}, bf16[1,48,128]{2,1,0:T(8,128)(2,1)S(1)}, u32[]{:S(2)}, u32[]{:S(2)}) collective-permute-start(bf16[1,48,128]{2,1,0:T(8,128)(2,1)S(1)} %bitcast.5), channel_id=1, source_target_pairs={{0,2},{1,3},{2,0},{3,1},{4,6},{5,7},{6,4},{7,5},{8,10},{9,11},{10,... | collective-permute-start | bytes 36872 | tf_op jit(solution)/shard_map/ppermute | solution.py:39
  43.3 2.0 %collective-permute-done.14 = bf16[1,48,128]{2,1,0:T(8,128)(2,1)S(1)} collective-permute-done((bf16[1,48,128]{2,1,0:T(8,128)(2,1)S(1)}, bf16[1,48,128]{2,1,0:T(8,128)(2,1)S(1)}, u32[]{:S(2)}, u32[]{:S(2)}) %collective-permute-start.14) | collective-permute-done | bytes 12320 | tf_op jit(solution)/shard_map/ppermute | solution.py:39
  45.4 1.5 %collective-permute-start.15 = (bf16[2,48,128]{2,1,0:T(8,128)(2,1)S(1)}, bf16[2,48,128]{2,1,0:T(8,128)(2,1)S(1)}, u32[]{:S(2)}, u32[]{:S(2)}) collective-permute-start(bf16[2,48,128]{2,1,0:T(8,128)(2,1)S(1)} %pad_maximum_fusion.4), channel_id=1, source_target_pairs={{0,1},{1,0},{2,3},{3,2},{4,5},{5,4},{6,7},{7,6},{8,9},{9,8},{10,11... | collective-permute-start | bytes 73736 | tf_op jit(solution)/shard_map/ppermute | solution.py:39
  46.9 2.3 %collective-permute-done.15 = bf16[2,48,128]{2,1,0:T(8,128)(2,1)S(1)} collective-permute-done((bf16[2,48,128]{2,1,0:T(8,128)(2,1)S(1)}, bf16[2,48,128]{2,1,0:T(8,128)(2,1)S(1)}, u32[]{:S(2)}, u32[]{:S(2)}) %collective-permute-start.15) | collective-permute-done | bytes 24608 | tf_op jit(solution)/shard_map/ppermute | solution.py:39
  49.2 2.1 %collective-permute-start.16 = (bf16[4,48,128]{2,1,0:T(8,128)(2,1)S(1)}, bf16[4,48,128]{2,1,0:T(8,128)(2,1)S(1)}, u32[]{:S(2)}, u32[]{:S(2)}) collective-permute-start(bf16[4,48,128]{2,1,0:T(8,128)(2,1)S(1)} %pad_maximum_fusion.2), channel_id=1, source_target_pairs={{0,16},{4,20},{8,24},{12,28},{16,0},{20,4},{24,8},{28,12},{1,17},{... | collective-permute-start | bytes 147464 | tf_op jit(solution)/shard_map/ppermute | solution.py:39
  51.3 2.1 %collective-permute-done.16 = bf16[4,48,128]{2,1,0:T(8,128)(2,1)S(1)} collective-permute-done((bf16[4,48,128]{2,1,0:T(8,128)(2,1)S(1)}, bf16[4,48,128]{2,1,0:T(8,128)(2,1)S(1)}, u32[]{:S(2)}, u32[]{:S(2)}) %collective-permute-start.16) | collective-permute-done | bytes 49184 | tf_op jit(solution)/shard_map/ppermute | solution.py:39
  53.4 1.5 %collective-permute-start.17 = (bf16[8,48,128]{2,1,0:T(8,128)(2,1)S(1)}, bf16[8,48,128]{2,1,0:T(8,128)(2,1)S(1)}, u32[]{:S(2)}, u32[]{:S(2)}) collective-permute-start(bf16[8,48,128]{2,1,0:T(8,128)(2,1)S(1)} %pad_maximum_fusion.1), channel_id=1, source_target_pairs={{0,8},{4,12},{8,0},{12,4},{16,24},{20,28},{24,16},{28,20},{1,9},{5... | collective-permute-start | bytes 294920 | tf_op jit(solution)/shard_map/ppermute | solution.py:39
  55.0 3.1 %collective-permute-done.17 = bf16[8,48,128]{2,1,0:T(8,128)(2,1)S(1)} collective-permute-done((bf16[8,48,128]{2,1,0:T(8,128)(2,1)S(1)}, bf16[8,48,128]{2,1,0:T(8,128)(2,1)S(1)}, u32[]{:S(2)}, u32[]{:S(2)}) %collective-permute-start.17) | collective-permute-done | bytes 98336 | tf_op jit(solution)/shard_map/ppermute | solution.py:39
  58.1 0.1 collective-permute-start.18
  58.2 1.4 %collective-permute-done.18 = bf16[16,48,128]{2,1,0:T(8,128)(2,1)S(1)} collective-permute-done((bf16[16,48,128]{2,1,0:T(8,128)(2,1)S(1)}, bf16[16,48,128]{2,1,0:T(8,128)(2,1)S(1)}, u32[]{:S(2)}, u32[]{:S(2)}) %collective-permute-start.18) | collective-permute-done | bytes 196640 | tf_op jit(solution)/shard_map/ppermute | solution.py:39
  59.7 3.6 %shard_map.105 = f32[64,32,128]{2,1,0:T(8,128)} custom-call(s32[1]{0:T(128)} %bitcast.1.slab_number_ref, bf16[32,48,128]{2,1,0:T(8,128)(2,1)S(1)} %constant_dynamic-update-slice_fusion.5.boxes_ref), custom_call_target="tpu_custom_call" | custom-call | tf_op jit(solution)/shard_map/pallas_call | solution.py:443
  (32 shorter events, 0.2 us)
Async XLA Ops:
  0.6 26.5 %copy-start = (s32[4,32]{1,0:T(4,128)S(1)}, s32[4,32]{1,0:T(4,128)}, u32[]{:S(2)}) copy-start(s32[4,32]{1,0:T(4,128)} %members_ref.1) | copy-start | bytes 1540
  0.6 26.5 %copy-start.1 = (f32[4]{0:T(128)S(1)}, f32[4]{0:T(128)}, u32[]{:S(2)}) copy-start(f32[4]{0:T(128)} %shift_ref.1) | copy-start | bytes 52
  0.7 26.5 %copy-start.2 = (s32[4]{0:T(128)S(1)}, s32[4]{0:T(128)}, u32[]{:S(2)}) copy-start(s32[4]{0:T(128)} %start_ref.1) | copy-start | bytes 52
  0.7 26.5 %copy-start.3 = (s32[4]{0:T(128)S(1)}, s32[4]{0:T(128)}, u32[]{:S(2)}) copy-start(s32[4]{0:T(128)} %row_ref.1) | copy-start | bytes 52
  0.7 26.5 %copy-start.4 = (s32[4]{0:T(128)S(1)}, s32[4]{0:T(128)}, u32[]{:S(2)}) copy-start(s32[4]{0:T(128)} %col_ref.1) | copy-start | bytes 52
  0.7 4.6 %collective-permute-start.2 = (bf16[1024,256]{1,0:T(8,128)(2,1)}, bf16[1024,256]{1,0:T(8,128)(2,1)S(1)}, u32[]{:S(2)}, u32[]{:S(2)}) collective-permute-start(bf16[1024,256]{1,0:T(8,128)(2,1)} %bitcast.9), channel_id=1, source_target_pairs={{0,4},{4,0},{8,12},{12,8},{16,20},{20,16},{24,28},{28,24},{1,5},{5... | collective-permute-start | bytes 1572872 | tf_op jit(solution)/shard_map/ppermute | solution.py:81
  1.2 12.9 %collective-permute-start = (bf16[1024,256]{1,0:T(8,128)(2,1)}, bf16[1024,256]{1,0:T(8,128)(2,1)S(1)}, u32[]{:S(2)}, u32[]{:S(2)}) collective-permute-start(bf16[1024,256]{1,0:T(8,128)(2,1)} %bitcast.10), channel_id=1, source_target_pairs={{0,8},{4,20},{8,0},{12,28},{16,24},{20,4},{24,16},{28,12},{1,9},{5... | collective-permute-start | bytes 1572872 | tf_op jit(solution)/shard_map/ppermute | solution.py:72
  5.3 12.3 %collective-permute-start.7 = (bf16[1024,256]{1,0:T(8,128)(2,1)}, bf16[1024,256]{1,0:T(8,128)(2,1)S(1)}, u32[]{:S(2)}, u32[]{:S(2)}) collective-permute-start(bf16[1024,256]{1,0:T(8,128)(2,1)} %bitcast.11), channel_id=1, source_target_pairs={{0,16},{4,12},{8,24},{12,4},{16,0},{20,28},{24,8},{28,20},{1,17},{... | collective-permute-start | bytes 1572872 | tf_op jit(solution)/shard_map/ppermute | solution.py:72
  6.8 10.7 %collective-permute-start.3 = (bf16[32,512]{1,0:T(8,128)(2,1)S(1)}, bf16[32,512]{1,0:T(8,128)(2,1)S(1)}, u32[]{:S(2)}, u32[]{:S(2)}) collective-permute-start(bf16[32,512]{1,0:T(8,128)(2,1)S(1)} %pad_maximum_fusion.3.rest_8_), channel_id=1, source_target_pairs={{0,8},{4,20},{8,0},{12,28},{16,24},{20,4},{24,16},{28,12},{1,9},{5... | collective-permute-start | bytes 98312 | tf_op jit(solution)/shard_map/ppermute | solution.py:72
  7.4 10.2 %collective-permute-start.4 = (bf16[32,512]{1,0:T(8,128)(2,1)S(1)}, bf16[32,512]{1,0:T(8,128)(2,1)S(1)}, u32[]{:S(2)}, u32[]{:S(2)}) collective-permute-start(bf16[32,512]{1,0:T(8,128)(2,1)S(1)} %pad_maximum_fusion.3.rest_8_), channel_id=1, source_target_pairs={{0,16},{4,12},{8,24},{12,4},{16,0},{20,28},{24,8},{28,20},{1,17},{... | collective-permute-start | bytes 98312 | tf_op jit(solution)/shard_map/ppermute | solution.py:72
  14.1 11.0 %collective-permute-start.1 = (bf16[1024,256]{1,0:T(8,128)(2,1)S(1)}, bf16[1024,256]{1,0:T(8,128)(2,1)S(1)}, u32[]{:S(2)}, u32[]{:S(2)}) collective-permute-start(bf16[1024,256]{1,0:T(8,128)(2,1)S(1)} %collective-permute-done.rest_1_), channel_id=1, source_target_pairs={{0,16},{4,12},{8,24},{12,4},{16,0},{20,28},{24,8},{28,20},{1,17},{... | collective-permute-start | bytes 1572872 | tf_op jit(solution)/shard_map/ppermute | solution.py:77
  17.6 7.5 %collective-permute-start.6 = (bf16[1024,256]{1,0:T(8,128)(2,1)S(1)}, bf16[1024,256]{1,0:T(8,128)(2,1)S(1)}, u32[]{:S(2)}, u32[]{:S(2)}) collective-permute-start(bf16[1024,256]{1,0:T(8,128)(2,1)S(1)} %collective-permute-done.rest_1_), channel_id=1, source_target_pairs={{0,4},{4,0},{8,12},{12,8},{16,20},{20,16},{24,28},{28,24},{1,5},{5... | collective-permute-start | bytes 1572872 | tf_op jit(solution)/shard_map/ppermute | solution.py:90
  17.6 7.5 %collective-permute-start.8 = (bf16[1024,256]{1,0:T(8,128)(2,1)S(1)}, bf16[1024,256]{1,0:T(8,128)(2,1)S(1)}, u32[]{:S(2)}, u32[]{:S(2)}) collective-permute-start(bf16[1024,256]{1,0:T(8,128)(2,1)S(1)} %collective-permute-done.7.rest_2_), channel_id=1, source_target_pairs={{0,4},{4,0},{8,12},{12,8},{16,20},{20,16},{24,28},{28,24},{1,5},{5... | collective-permute-start | bytes 1572872 | tf_op jit(solution)/shard_map/ppermute | solution.py:90
  18.1 2.2 %collective-permute-start.9 = (bf16[32,512]{1,0:T(8,128)(2,1)S(1)}, bf16[32,512]{1,0:T(8,128)(2,1)S(1)}, u32[]{:S(2)}, u32[]{:S(2)}) collective-permute-start(bf16[32,512]{1,0:T(8,128)(2,1)S(1)} %pad_maximum_fusion.3.rest_8_), channel_id=1, source_target_pairs={{0,4},{4,0},{8,12},{12,8},{16,20},{20,16},{24,28},{28,24},{1,5},{5... | collective-permute-start | bytes 98312 | tf_op jit(solution)/shard_map/ppermute | solution.py:91
  18.2 3.5 %collective-permute-start.10 = (bf16[32,512]{1,0:T(8,128)(2,1)S(1)}, bf16[32,512]{1,0:T(8,128)(2,1)S(1)}, u32[]{:S(2)}, u32[]{:S(2)}) collective-permute-start(bf16[32,512]{1,0:T(8,128)(2,1)S(1)} %collective-permute-done.3.rest_9_), channel_id=1, source_target_pairs={{0,4},{4,0},{8,12},{12,8},{16,20},{20,16},{24,28},{28,24},{1,5},{5... | collective-permute-start | bytes 98312 | tf_op jit(solution)/shard_map/ppermute | solution.py:91
  20.3 4.8 %collective-permute-start.5 = (bf16[32,512]{1,0:T(8,128)(2,1)S(1)}, bf16[32,512]{1,0:T(8,128)(2,1)S(1)}, u32[]{:S(2)}, u32[]{:S(2)}) collective-permute-start(bf16[32,512]{1,0:T(8,128)(2,1)S(1)} %collective-permute-done.3.rest_9_), channel_id=1, source_target_pairs={{0,16},{4,12},{8,24},{12,4},{16,0},{20,28},{24,8},{28,20},{1,17},{... | collective-permute-start | bytes 98312 | tf_op jit(solution)/shard_map/ppermute | solution.py:77
  21.7 3.4 %collective-permute-start.11 = (bf16[32,512]{1,0:T(8,128)(2,1)S(1)}, bf16[32,512]{1,0:T(8,128)(2,1)S(1)}, u32[]{:S(2)}, u32[]{:S(2)}) collective-permute-start(bf16[32,512]{1,0:T(8,128)(2,1)S(1)} %collective-permute-done.4.rest_10_), channel_id=1, source_target_pairs={{0,4},{4,0},{8,12},{12,8},{16,20},{20,16},{24,28},{28,24},{1,5},{5... | collective-permute-start | bytes 98312 | tf_op jit(solution)/shard_map/ppermute | solution.py:91
  25.1 2.0 %collective-permute-start.12 = (bf16[1024,256]{1,0:T(8,128)(2,1)S(1)}, bf16[1024,256]{1,0:T(8,128)(2,1)S(1)}, u32[]{:S(2)}, u32[]{:S(2)}) collective-permute-start(bf16[1024,256]{1,0:T(8,128)(2,1)S(1)} %collective-permute-done.1.rest_3_), channel_id=1, source_target_pairs={{0,4},{4,0},{8,12},{12,8},{16,20},{20,16},{24,28},{28,24},{1,5},{5... | collective-permute-start | bytes 1572872 | tf_op jit(solution)/shard_map/ppermute | solution.py:97
  25.2 1.9 %collective-permute-start.13 = (bf16[32,512]{1,0:T(8,128)(2,1)S(1)}, bf16[32,512]{1,0:T(8,128)(2,1)S(1)}, u32[]{:S(2)}, u32[]{:S(2)}) collective-permute-start(bf16[32,512]{1,0:T(8,128)(2,1)S(1)} %collective-permute-done.5.rest_11_), channel_id=1, source_target_pairs={{0,4},{4,0},{8,12},{12,8},{16,20},{20,16},{24,28},{28,24},{1,5},{5... | collective-permute-start | bytes 98312 | tf_op jit(solution)/shard_map/ppermute | solution.py:98
  40.7 4.7 %collective-permute-start.14 = (bf16[1,48,128]{2,1,0:T(8,128)(2,1)S(1)}, bf16[1,48,128]{2,1,0:T(8,128)(2,1)S(1)}, u32[]{:S(2)}, u32[]{:S(2)}) collective-permute-start(bf16[1,48,128]{2,1,0:T(8,128)(2,1)S(1)} %bitcast.5), channel_id=1, source_target_pairs={{0,2},{1,3},{2,0},{3,1},{4,6},{5,7},{6,4},{7,5},{8,10},{9,11},{10,... | collective-permute-start | bytes 36872 | tf_op jit(solution)/shard_map/ppermute | solution.py:39
  45.4 3.8 %collective-permute-start.15 = (bf16[2,48,128]{2,1,0:T(8,128)(2,1)S(1)}, bf16[2,48,128]{2,1,0:T(8,128)(2,1)S(1)}, u32[]{:S(2)}, u32[]{:S(2)}) collective-permute-start(bf16[2,48,128]{2,1,0:T(8,128)(2,1)S(1)} %pad_maximum_fusion.4), channel_id=1, source_target_pairs={{0,1},{1,0},{2,3},{3,2},{4,5},{5,4},{6,7},{7,6},{8,9},{9,8},{10,11... | collective-permute-start | bytes 73736 | tf_op jit(solution)/shard_map/ppermute | solution.py:39
  49.2 4.2 %collective-permute-start.16 = (bf16[4,48,128]{2,1,0:T(8,128)(2,1)S(1)}, bf16[4,48,128]{2,1,0:T(8,128)(2,1)S(1)}, u32[]{:S(2)}, u32[]{:S(2)}) collective-permute-start(bf16[4,48,128]{2,1,0:T(8,128)(2,1)S(1)} %pad_maximum_fusion.2), channel_id=1, source_target_pairs={{0,16},{4,20},{8,24},{12,28},{16,0},{20,4},{24,8},{28,12},{1,17},{... | collective-permute-start | bytes 147464 | tf_op jit(solution)/shard_map/ppermute | solution.py:39
  53.4 4.7 %collective-permute-start.17 = (bf16[8,48,128]{2,1,0:T(8,128)(2,1)S(1)}, bf16[8,48,128]{2,1,0:T(8,128)(2,1)S(1)}, u32[]{:S(2)}, u32[]{:S(2)}) collective-permute-start(bf16[8,48,128]{2,1,0:T(8,128)(2,1)S(1)} %pad_maximum_fusion.1), channel_id=1, source_target_pairs={{0,8},{4,12},{8,0},{12,4},{16,24},{20,28},{24,16},{28,20},{1,9},{5... | collective-permute-start | bytes 294920 | tf_op jit(solution)/shard_map/ppermute | solution.py:39
  58.1 1.5 %collective-permute-start.18 = (bf16[16,48,128]{2,1,0:T(8,128)(2,1)S(1)}, bf16[16,48,128]{2,1,0:T(8,128)(2,1)S(1)}, u32[]{:S(2)}, u32[]{:S(2)}) collective-permute-start(bf16[16,48,128]{2,1,0:T(8,128)(2,1)S(1)} %get-tuple-element.42), channel_id=1, source_target_pairs={{0,4},{4,0},{8,12},{12,8},{16,20},{20,16},{24,28},{28,24},{1,5},{5... | collective-permute-start | bytes 589832 | tf_op jit(solution)/shard_map/ppermute | solution.py:39

commit v6 on v5

--- a/solution.py
+++ b/solution.py
@@ -19,7 +19,7 @@
 
 LOW = 8
 LANES = 128
-BATCH = 4
+BATCH = 8
 STAGGER = 1
 
 
@@ -80,7 +80,8 @@
     firsts = send(blocks, pairs[:1])
     beside = lax.ppermute(blocks, "atoms", swap)
     beside, wanted = lax.optimization_barrier((beside, side()))
-    later, wanted = lax.optimization_barrier((blocks, wanted))
+    mine = jnp.concatenate([blocks, wanted[:, : blocks.shape[1]]], axis=0)
+    later, wanted, mine = lax.optimization_barrier((blocks, wanted, mine))
     firsts = firsts + send(later, pairs[1:])
     side_firsts = send(wanted, pairs)
     have = forward(blocks, firsts)
@@ -89,9 +90,8 @@
     side_have = forward(wanted, side_firsts)
     swapped = [beside] + [lax.ppermute(piece, "atoms", swap) for piece in have[1:-1]]
     side_swapped = [lax.ppermute(piece, "atoms", swap) for piece in side_have[:-1]]
-    mine = jnp.concatenate([blocks, wanted[:, : blocks.shape[1]]], axis=0)
-    have[-1], side_have[-1], swapped, side_swapped, mine = lax.optimization_barrier(
-        (have[-1], side_have[-1], swapped, side_swapped, mine)
+    have[-1], side_have[-1], swapped, side_swapped = lax.optimization_barrier(
+        (have[-1], side_have[-1], swapped, side_swapped)
     )
     if stages:
         swapped.append(lax.ppermute(have[-1], "atoms", swap))

time: 63.4 us -> 62.3 us (0.983)
  waiting for transfers between devices: 22.6 us -> 21.2 us
    ppermute x4, waiting for transfers between devices: 6.26 us -> 4.79 us  [send(): return [lax.ppermute(part, 'atoms', pair) for pair in ways]]
  transfers between devices with their start and end apart: 19 -> 19, of which waited for: 9 -> 10; matrix products, arithmetic and copies ran while one was open for 4% -> 4% of each run, Pallas kernels for 0% -> 0%
where the time goes in v6:
time: 62.3 us; the launch traced here: 61.8 us
  waiting for transfers between devices  21.2 us (34%)
  starting transfers between devices  20.3 us (33%)
  Pallas kernels  16.6 us (27%)
  other arithmetic  2.64 us (4%)
  between operations  0.8 us (1%)
    pallas_call x1, Pallas kernels, on_device(): pl.pallas_call(functools.partial(density_kernel, holders, atoms_here, lin...  13.6 us
    ppermute x5, waiting for transfers between devices, gather_everywhere(): value = jnp.concatenate([value, lax.ppermute(value, axis, pairs)], axis=0)  10.9 us
    ppermute x5, starting transfers between devices, gather_everywhere(): value = jnp.concatenate([value, lax.ppermute(value, axis, pairs)], axis=0)  7.85 us
    ppermute x2, starting transfers between devices, forward(): lax.ppermute(piece, 'atoms', pair)  5.18 us
    ppermute x4, starting transfers between devices, send(): return [lax.ppermute(part, 'atoms', pair) for pair in ways]  5.15 us
    ppermute x4, waiting for transfers between devices, send(): return [lax.ppermute(part, 'atoms', pair) for pair in ways]  4.79 us
    pallas_call x1, Pallas kernels, on_device(): pl.pallas_call(functools.partial(slab_kernel, tasks), in_specs=[scalars,...  3.09 us
    ppermute x2, waiting for transfers between devices, forward(): lax.ppermute(piece, 'atoms', pair)  2.36 us
  transfers between devices with their start and end apart: 19, of which 10 were waited for; matrix products, arithmetic and copies ran while one was open for 4% of the time, Pallas kernels for 0%

profile of v6, /device:TPU:0, one launch (start us, length us, event | category | flops | bytes accessed | tf_op | source)
XLA Modules:
  0.0 61.8 jit_solution(5735213942966592788)
XLA Ops:
  0.7 0.5 collective-permute-start
  1.2 2.6 %collective-permute-start.1 = (bf16[1024,256]{1,0:T(8,128)(2,1)}, bf16[1024,256]{1,0:T(8,128)(2,1)S(1)}, u32[]{:S(2)}, u32[]{:S(2)}) collective-permute-start(bf16[1024,256]{1,0:T(8,128)(2,1)} %bitcast.10), channel_id=1, source_target_pairs={{0,8},{4,20},{8,0},{12,28},{16,24},{20,4},{24,16},{28,12},{1,9},{5... | collective-permute-start | bytes 1572872 | tf_op jit(solution)/shard_map/ppermute | solution.py:72
  3.8 0.7 %fusion.2 = (bf16[32,32]{1,0:T(8,128)(2,1)S(1)}, bf16[32,32]{1,0:T(8,128)(2,1)S(1)}) fusion(s32[32,32]{1,0:T(8,128)} %param.11), kind=kLoop, calls=%fused_computation.24 | loop fusion | flops 21504 | bytes 8192 | tf_op jit(solution)/shard_map/convert
  4.5 0.1 fusion.4
  4.6 0.7 %pad_maximum_fusion.3.rest_8_ = bf16[32,512]{1,0:T(8,128)(2,1)S(1)} fusion(bf16[32,256]{1,0:T(8,128)(2,1)S(1)} %fusion.4, bf16[32,256]{1,0:T(8,128)(2,1)} %param.10), kind=kLoop, calls=%fused_computation.6 | loop fusion | flops 65536 | bytes 65536 | tf_op jit(solution)/shard_map/concatenate | solution.py:401
  5.3 1.1 %pad_maximum_fusion.rest_0_ = bf16[1056,256]{1,0:T(8,128)(2,1)S(1)} fusion(bf16[32,256]{1,0:T(8,128)(2,1)S(1)} %slice.3, bf16[1024,256]{1,0:T(8,128)(2,1)} %bitcast.11), kind=kLoop, calls=%fused_computation | loop fusion | flops 1081344 | bytes 1081344 | tf_op jit(solution)/shard_map/concatenate | solution.py:83
  6.4 1.6 %collective-permute-start.4 = (bf16[1024,256]{1,0:T(8,128)(2,1)S(1)}, bf16[1024,256]{1,0:T(8,128)(2,1)S(1)}, u32[]{:S(2)}, u32[]{:S(2)}) collective-permute-start(bf16[1024,256]{1,0:T(8,128)(2,1)S(1)} %bitcast.12), channel_id=1, source_target_pairs={{0,16},{4,12},{8,24},{12,4},{16,0},{20,28},{24,8},{28,20},{1,17},{... | collective-permute-start | bytes 1572872 | tf_op jit(solution)/shard_map/ppermute | solution.py:72
  8.0 0.5 collective-permute-start.2
  8.5 0.5 collective-permute-start.3
  9.0 4.1 %collective-permute-done.1.rest_1_ = bf16[1024,256]{1,0:T(8,128)(2,1)S(1)} collective-permute-done((bf16[1024,256]{1,0:T(8,128)(2,1)}, bf16[1024,256]{1,0:T(8,128)(2,1)S(1)}, u32[]{:S(2)}, u32[]{:S(2)}) %collective-permute-start.1) | collective-permute-done | bytes 524320 | tf_op jit(solution)/shard_map/ppermute | solution.py:72
  13.2 3.4 %collective-permute-start.5 = (bf16[1024,256]{1,0:T(8,128)(2,1)S(1)}, bf16[1024,256]{1,0:T(8,128)(2,1)S(1)}, u32[]{:S(2)}, u32[]{:S(2)}) collective-permute-start(bf16[1024,256]{1,0:T(8,128)(2,1)S(1)} %collective-permute-done.1.rest_1_), channel_id=1, source_target_pairs={{0,16},{4,12},{8,24},{12,4},{16,0},{20,28},{24,8},{28,20},{1,17},{... | collective-permute-start | bytes 1572872 | tf_op jit(solution)/shard_map/ppermute | solution.py:77
  16.6 0.6 %collective-permute-done.3.rest_10_ = bf16[32,512]{1,0:T(8,128)(2,1)S(1)} collective-permute-done((bf16[32,512]{1,0:T(8,128)(2,1)S(1)}, bf16[32,512]{1,0:T(8,128)(2,1)S(1)}, u32[]{:S(2)}, u32[]{:S(2)}) %collective-permute-start.3) | collective-permute-done | bytes 32800 | tf_op jit(solution)/shard_map/ppermute | solution.py:72
  17.2 0.1 collective-permute-start.7
  17.4 0.4 collective-permute-start.8
  17.8 0.1 collective-permute-start.9
  17.9 0.4 collective-permute-start.10
  18.3 1.7 %collective-permute-done.9.rest_12_ = bf16[32,512]{1,0:T(8,128)(2,1)S(1)} collective-permute-done((bf16[32,512]{1,0:T(8,128)(2,1)S(1)}, bf16[32,512]{1,0:T(8,128)(2,1)S(1)}, u32[]{:S(2)}, u32[]{:S(2)}) %collective-permute-start.9) | collective-permute-done | bytes 32800 | tf_op jit(solution)/shard_map/ppermute | solution.py:92
  19.9 1.7 %collective-permute-start.6 = (bf16[32,512]{1,0:T(8,128)(2,1)S(1)}, bf16[32,512]{1,0:T(8,128)(2,1)S(1)}, u32[]{:S(2)}, u32[]{:S(2)}) collective-permute-start(bf16[32,512]{1,0:T(8,128)(2,1)S(1)} %collective-permute-done.2.rest_9_), channel_id=1, source_target_pairs={{0,16},{4,12},{8,24},{12,4},{16,0},{20,28},{24,8},{28,20},{1,17},{... | collective-permute-start | bytes 98312 | tf_op jit(solution)/shard_map/ppermute | solution.py:77
  21.7 2.4 %collective-permute-done.6.rest_11_ = bf16[32,512]{1,0:T(8,128)(2,1)S(1)} collective-permute-done((bf16[32,512]{1,0:T(8,128)(2,1)S(1)}, bf16[32,512]{1,0:T(8,128)(2,1)S(1)}, u32[]{:S(2)}, u32[]{:S(2)}) %collective-permute-start.6) | collective-permute-done | bytes 32800 | tf_op jit(solution)/shard_map/ppermute | solution.py:77
  24.2 0.5 collective-permute-start.13
  24.7 1.4 %collective-permute-done.13.rest_15_ = bf16[32,512]{1,0:T(8,128)(2,1)S(1)} collective-permute-done((bf16[32,512]{1,0:T(8,128)(2,1)S(1)}, bf16[32,512]{1,0:T(8,128)(2,1)S(1)}, u32[]{:S(2)}, u32[]{:S(2)}) %collective-permute-start.13) | collective-permute-done | bytes 32800 | tf_op jit(solution)/shard_map/ppermute | solution.py:98
  26.2 13.6 %shard_map.104 = (bf16[4,512,128]{2,1,0:T(8,128)(2,1)}, bf16[48,128]{1,0:T(8,128)(2,1)S(1)}) custom-call(f32[4]{0:T(128)S(1)} %copy-done.1, s32[4]{0:T(128)S(1)} %copy-done.2, s32[4]{0:T(128)S(1)} %copy-done.3, s32[4]{0:T(128)S(1)} %copy-done.4, s32[4,32]{1,0:T(4,128)S(1)} %copy-done, bf16[4,512,1024]{2,1,0:T(8,128)(2,1)} %basis_hbm.1, ...), custom_call_target="tpu_custom_call" | custom-call | tf_op jit(solution)/shard_map/pallas_call | solution.py:408
  39.8 2.6 %collective-permute-start.14 = (bf16[1,48,128]{2,1,0:T(8,128)(2,1)S(1)}, bf16[1,48,128]{2,1,0:T(8,128)(2,1)S(1)}, u32[]{:S(2)}, u32[]{:S(2)}) collective-permute-start(bf16[1,48,128]{2,1,0:T(8,128)(2,1)S(1)} %bitcast.5), channel_id=1, source_target_pairs={{0,2},{1,3},{2,0},{3,1},{4,6},{5,7},{6,4},{7,5},{8,10},{9,11},{10,... | collective-permute-start | bytes 36872 | tf_op jit(solution)/shard_map/ppermute | solution.py:39
  42.4 2.0 %collective-permute-done.14 = bf16[1,48,128]{2,1,0:T(8,128)(2,1)S(1)} collective-permute-done((bf16[1,48,128]{2,1,0:T(8,128)(2,1)S(1)}, bf16[1,48,128]{2,1,0:T(8,128)(2,1)S(1)}, u32[]{:S(2)}, u32[]{:S(2)}) %collective-permute-start.14) | collective-permute-done | bytes 12320 | tf_op jit(solution)/shard_map/ppermute | solution.py:39
  44.4 1.5 %collective-permute-start.15 = (bf16[2,48,128]{2,1,0:T(8,128)(2,1)S(1)}, bf16[2,48,128]{2,1,0:T(8,128)(2,1)S(1)}, u32[]{:S(2)}, u32[]{:S(2)}) collective-permute-start(bf16[2,48,128]{2,1,0:T(8,128)(2,1)S(1)} %pad_maximum_fusion.4), channel_id=1, source_target_pairs={{0,1},{1,0},{2,3},{3,2},{4,5},{5,4},{6,7},{7,6},{8,9},{9,8},{10,11... | collective-permute-start | bytes 73736 | tf_op jit(solution)/shard_map/ppermute | solution.py:39
  46.0 2.3 %collective-permute-done.15 = bf16[2,48,128]{2,1,0:T(8,128)(2,1)S(1)} collective-permute-done((bf16[2,48,128]{2,1,0:T(8,128)(2,1)S(1)}, bf16[2,48,128]{2,1,0:T(8,128)(2,1)S(1)}, u32[]{:S(2)}, u32[]{:S(2)}) %collective-permute-start.15) | collective-permute-done | bytes 24608 | tf_op jit(solution)/shard_map/ppermute | solution.py:39
  48.3 2.1 %collective-permute-start.16 = (bf16[4,48,128]{2,1,0:T(8,128)(2,1)S(1)}, bf16[4,48,128]{2,1,0:T(8,128)(2,1)S(1)}, u32[]{:S(2)}, u32[]{:S(2)}) collective-permute-start(bf16[4,48,128]{2,1,0:T(8,128)(2,1)S(1)} %pad_maximum_fusion.2), channel_id=1, source_target_pairs={{0,16},{4,20},{8,24},{12,28},{16,0},{20,4},{24,8},{28,12},{1,17},{... | collective-permute-start | bytes 147464 | tf_op jit(solution)/shard_map/ppermute | solution.py:39
  50.4 2.1 %collective-permute-done.16 = bf16[4,48,128]{2,1,0:T(8,128)(2,1)S(1)} collective-permute-done((bf16[4,48,128]{2,1,0:T(8,128)(2,1)S(1)}, bf16[4,48,128]{2,1,0:T(8,128)(2,1)S(1)}, u32[]{:S(2)}, u32[]{:S(2)}) %collective-permute-start.16) | collective-permute-done | bytes 49184 | tf_op jit(solution)/shard_map/ppermute | solution.py:39
  52.4 1.5 %collective-permute-start.17 = (bf16[8,48,128]{2,1,0:T(8,128)(2,1)S(1)}, bf16[8,48,128]{2,1,0:T(8,128)(2,1)S(1)}, u32[]{:S(2)}, u32[]{:S(2)}) collective-permute-start(bf16[8,48,128]{2,1,0:T(8,128)(2,1)S(1)} %pad_maximum_fusion.1), channel_id=1, source_target_pairs={{0,8},{4,12},{8,0},{12,4},{16,24},{20,28},{24,16},{28,20},{1,9},{5... | collective-permute-start | bytes 294920 | tf_op jit(solution)/shard_map/ppermute | solution.py:39
  54.0 3.1 %collective-permute-done.17 = bf16[8,48,128]{2,1,0:T(8,128)(2,1)S(1)} collective-permute-done((bf16[8,48,128]{2,1,0:T(8,128)(2,1)S(1)}, bf16[8,48,128]{2,1,0:T(8,128)(2,1)S(1)}, u32[]{:S(2)}, u32[]{:S(2)}) %collective-permute-start.17) | collective-permute-done | bytes 98336 | tf_op jit(solution)/shard_map/ppermute | solution.py:39
  57.2 1.4 %collective-permute-done.18 = bf16[16,48,128]{2,1,0:T(8,128)(2,1)S(1)} collective-permute-done((bf16[16,48,128]{2,1,0:T(8,128)(2,1)S(1)}, bf16[16,48,128]{2,1,0:T(8,128)(2,1)S(1)}, u32[]{:S(2)}, u32[]{:S(2)}) %collective-permute-start.18) | collective-permute-done | bytes 196640 | tf_op jit(solution)/shard_map/ppermute | solution.py:39
  58.7 3.1 %shard_map.105 = f32[64,32,128]{2,1,0:T(8,128)} custom-call(s32[1]{0:T(128)} %bitcast.1.slab_number_ref, bf16[32,48,128]{2,1,0:T(8,128)(2,1)S(1)} %constant_dynamic-update-slice_fusion.5.boxes_ref), custom_call_target="tpu_custom_call" | custom-call | tf_op jit(solution)/shard_map/pallas_call | solution.py:443
  (34 shorter events, 0.4 us)
Async XLA Ops:
  0.6 5.8 %copy-start.5 = (bf16[32,32,256]{2,1,0:T(8,128)(2,1)S(1)}, bf16[32,32,256]{2,1,0:T(8,128)(2,1)}, u32[]{:S(2)}) copy-start(bf16[32,32,256]{2,1,0:T(8,128)(2,1)} %param.9) | copy-start | bytes 1572868
  0.6 25.5 %copy-start = (s32[4,32]{1,0:T(4,128)S(1)}, s32[4,32]{1,0:T(4,128)}, u32[]{:S(2)}) copy-start(s32[4,32]{1,0:T(4,128)} %members_ref.1) | copy-start | bytes 1540
  0.7 25.5 %copy-start.1 = (f32[4]{0:T(128)S(1)}, f32[4]{0:T(128)}, u32[]{:S(2)}) copy-start(f32[4]{0:T(128)} %shift_ref.1) | copy-start | bytes 52
  0.7 25.5 %copy-start.2 = (s32[4]{0:T(128)S(1)}, s32[4]{0:T(128)}, u32[]{:S(2)}) copy-start(s32[4]{0:T(128)} %start_ref.1) | copy-start | bytes 52
  0.7 25.5 %copy-start.3 = (s32[4]{0:T(128)S(1)}, s32[4]{0:T(128)}, u32[]{:S(2)}) copy-start(s32[4]{0:T(128)} %row_ref.1) | copy-start | bytes 52
  0.7 25.5 %copy-start.4 = (s32[4]{0:T(128)S(1)}, s32[4]{0:T(128)}, u32[]{:S(2)}) copy-start(s32[4]{0:T(128)} %col_ref.1) | copy-start | bytes 52
  0.7 4.6 %collective-permute-start = (bf16[1024,256]{1,0:T(8,128)(2,1)}, bf16[1024,256]{1,0:T(8,128)(2,1)S(1)}, u32[]{:S(2)}, u32[]{:S(2)}) collective-permute-start(bf16[1024,256]{1,0:T(8,128)(2,1)} %bitcast.9), channel_id=1, source_target_pairs={{0,4},{4,0},{8,12},{12,8},{16,20},{20,16},{24,28},{28,24},{1,5},{5... | collective-permute-start | bytes 1572872 | tf_op jit(solution)/shard_map/ppermute | solution.py:81
  1.2 11.9 %collective-permute-start.1 = (bf16[1024,256]{1,0:T(8,128)(2,1)}, bf16[1024,256]{1,0:T(8,128)(2,1)S(1)}, u32[]{:S(2)}, u32[]{:S(2)}) collective-permute-start(bf16[1024,256]{1,0:T(8,128)(2,1)} %bitcast.10), channel_id=1, source_target_pairs={{0,8},{4,20},{8,0},{12,28},{16,24},{20,4},{24,16},{28,12},{1,9},{5... | collective-permute-start | bytes 1572872 | tf_op jit(solution)/shard_map/ppermute | solution.py:72
  6.4 10.9 %collective-permute-start.4 = (bf16[1024,256]{1,0:T(8,128)(2,1)S(1)}, bf16[1024,256]{1,0:T(8,128)(2,1)S(1)}, u32[]{:S(2)}, u32[]{:S(2)}) collective-permute-start(bf16[1024,256]{1,0:T(8,128)(2,1)S(1)} %bitcast.12), channel_id=1, source_target_pairs={{0,16},{4,12},{8,24},{12,4},{16,0},{20,28},{24,8},{28,20},{1,17},{... | collective-permute-start | bytes 1572872 | tf_op jit(solution)/shard_map/ppermute | solution.py:72
  8.0 8.6 %collective-permute-start.2 = (bf16[32,512]{1,0:T(8,128)(2,1)S(1)}, bf16[32,512]{1,0:T(8,128)(2,1)S(1)}, u32[]{:S(2)}, u32[]{:S(2)}) collective-permute-start(bf16[32,512]{1,0:T(8,128)(2,1)S(1)} %pad_maximum_fusion.3.rest_8_), channel_id=1, source_target_pairs={{0,8},{4,20},{8,0},{12,28},{16,24},{20,4},{24,16},{28,12},{1,9},{5... | collective-permute-start | bytes 98312 | tf_op jit(solution)/shard_map/ppermute | solution.py:72
  8.5 8.7 %collective-permute-start.3 = (bf16[32,512]{1,0:T(8,128)(2,1)S(1)}, bf16[32,512]{1,0:T(8,128)(2,1)S(1)}, u32[]{:S(2)}, u32[]{:S(2)}) collective-permute-start(bf16[32,512]{1,0:T(8,128)(2,1)S(1)} %pad_maximum_fusion.3.rest_8_), channel_id=1, source_target_pairs={{0,16},{4,12},{8,24},{12,4},{16,0},{20,28},{24,8},{28,20},{1,17},{... | collective-permute-start | bytes 98312 | tf_op jit(solution)/shard_map/ppermute | solution.py:72
  13.2 11.0 %collective-permute-start.5 = (bf16[1024,256]{1,0:T(8,128)(2,1)S(1)}, bf16[1024,256]{1,0:T(8,128)(2,1)S(1)}, u32[]{:S(2)}, u32[]{:S(2)}) collective-permute-start(bf16[1024,256]{1,0:T(8,128)(2,1)S(1)} %collective-permute-done.1.rest_1_), channel_id=1, source_target_pairs={{0,16},{4,12},{8,24},{12,4},{16,0},{20,28},{24,8},{28,20},{1,17},{... | collective-permute-start | bytes 1572872 | tf_op jit(solution)/shard_map/ppermute | solution.py:77
  17.2 6.9 %collective-permute-start.7 = (bf16[1024,256]{1,0:T(8,128)(2,1)S(1)}, bf16[1024,256]{1,0:T(8,128)(2,1)S(1)}, u32[]{:S(2)}, u32[]{:S(2)}) collective-permute-start(bf16[1024,256]{1,0:T(8,128)(2,1)S(1)} %collective-permute-done.1.rest_1_), channel_id=1, source_target_pairs={{0,4},{4,0},{8,12},{12,8},{16,20},{20,16},{24,28},{28,24},{1,5},{5... | collective-permute-start | bytes 1572872 | tf_op jit(solution)/shard_map/ppermute | solution.py:91
  17.4 6.8 %collective-permute-start.8 = (bf16[1024,256]{1,0:T(8,128)(2,1)S(1)}, bf16[1024,256]{1,0:T(8,128)(2,1)S(1)}, u32[]{:S(2)}, u32[]{:S(2)}) collective-permute-start(bf16[1024,256]{1,0:T(8,128)(2,1)S(1)} %collective-permute-done.4.rest_2_), channel_id=1, source_target_pairs={{0,4},{4,0},{8,12},{12,8},{16,20},{20,16},{24,28},{28,24},{1,5},{5... | collective-permute-start | bytes 1572872 | tf_op jit(solution)/shard_map/ppermute | solution.py:91
  17.8 2.2 %collective-permute-start.9 = (bf16[32,512]{1,0:T(8,128)(2,1)S(1)}, bf16[32,512]{1,0:T(8,128)(2,1)S(1)}, u32[]{:S(2)}, u32[]{:S(2)}) collective-permute-start(bf16[32,512]{1,0:T(8,128)(2,1)S(1)} %pad_maximum_fusion.3.rest_8_), channel_id=1, source_target_pairs={{0,4},{4,0},{8,12},{12,8},{16,20},{20,16},{24,28},{28,24},{1,5},{5... | collective-permute-start | bytes 98312 | tf_op jit(solution)/shard_map/ppermute | solution.py:92
  17.9 3.8 %collective-permute-start.10 = (bf16[32,512]{1,0:T(8,128)(2,1)S(1)}, bf16[32,512]{1,0:T(8,128)(2,1)S(1)}, u32[]{:S(2)}, u32[]{:S(2)}) collective-permute-start(bf16[32,512]{1,0:T(8,128)(2,1)S(1)} %collective-permute-done.2.rest_9_), channel_id=1, source_target_pairs={{0,4},{4,0},{8,12},{12,8},{16,20},{20,16},{24,28},{28,24},{1,5},{5... | collective-permute-start | bytes 98312 | tf_op jit(solution)/shard_map/ppermute | solution.py:92
  19.9 4.2 %collective-permute-start.6 = (bf16[32,512]{1,0:T(8,128)(2,1)S(1)}, bf16[32,512]{1,0:T(8,128)(2,1)S(1)}, u32[]{:S(2)}, u32[]{:S(2)}) collective-permute-start(bf16[32,512]{1,0:T(8,128)(2,1)S(1)} %collective-permute-done.2.rest_9_), channel_id=1, source_target_pairs={{0,16},{4,12},{8,24},{12,4},{16,0},{20,28},{24,8},{28,20},{1,17},{... | collective-permute-start | bytes 98312 | tf_op jit(solution)/shard_map/ppermute | solution.py:77
  21.7 2.4 %collective-permute-start.11 = (bf16[32,512]{1,0:T(8,128)(2,1)S(1)}, bf16[32,512]{1,0:T(8,128)(2,1)S(1)}, u32[]{:S(2)}, u32[]{:S(2)}) collective-permute-start(bf16[32,512]{1,0:T(8,128)(2,1)S(1)} %collective-permute-done.3.rest_10_), channel_id=1, source_target_pairs={{0,4},{4,0},{8,12},{12,8},{16,20},{20,16},{24,28},{28,24},{1,5},{5... | collective-permute-start | bytes 98312 | tf_op jit(solution)/shard_map/ppermute | solution.py:92
  24.1 2.0 %collective-permute-start.12 = (bf16[1024,256]{1,0:T(8,128)(2,1)S(1)}, bf16[1024,256]{1,0:T(8,128)(2,1)S(1)}, u32[]{:S(2)}, u32[]{:S(2)}) collective-permute-start(bf16[1024,256]{1,0:T(8,128)(2,1)S(1)} %collective-permute-done.5.rest_3_), channel_id=1, source_target_pairs={{0,4},{4,0},{8,12},{12,8},{16,20},{20,16},{24,28},{28,24},{1,5},{5... | collective-permute-start | bytes 1572872 | tf_op jit(solution)/shard_map/ppermute | solution.py:97
  24.2 1.9 %collective-permute-start.13 = (bf16[32,512]{1,0:T(8,128)(2,1)S(1)}, bf16[32,512]{1,0:T(8,128)(2,1)S(1)}, u32[]{:S(2)}, u32[]{:S(2)}) collective-permute-start(bf16[32,512]{1,0:T(8,128)(2,1)S(1)} %collective-permute-done.6.rest_11_), channel_id=1, source_target_pairs={{0,4},{4,0},{8,12},{12,8},{16,20},{20,16},{24,28},{28,24},{1,5},{5... | collective-permute-start | bytes 98312 | tf_op jit(solution)/shard_map/ppermute | solution.py:98
  39.8 4.7 %collective-permute-start.14 = (bf16[1,48,128]{2,1,0:T(8,128)(2,1)S(1)}, bf16[1,48,128]{2,1,0:T(8,128)(2,1)S(1)}, u32[]{:S(2)}, u32[]{:S(2)}) collective-permute-start(bf16[1,48,128]{2,1,0:T(8,128)(2,1)S(1)} %bitcast.5), channel_id=1, source_target_pairs={{0,2},{1,3},{2,0},{3,1},{4,6},{5,7},{6,4},{7,5},{8,10},{9,11},{10,... | collective-permute-start | bytes 36872 | tf_op jit(solution)/shard_map/ppermute | solution.py:39
  44.4 3.8 %collective-permute-start.15 = (bf16[2,48,128]{2,1,0:T(8,128)(2,1)S(1)}, bf16[2,48,128]{2,1,0:T(8,128)(2,1)S(1)}, u32[]{:S(2)}, u32[]{:S(2)}) collective-permute-start(bf16[2,48,128]{2,1,0:T(8,128)(2,1)S(1)} %pad_maximum_fusion.4), channel_id=1, source_target_pairs={{0,1},{1,0},{2,3},{3,2},{4,5},{5,4},{6,7},{7,6},{8,9},{9,8},{10,11... | collective-permute-start | bytes 73736 | tf_op jit(solution)/shard_map/ppermute | solution.py:39
  48.3 4.2 %collective-permute-start.16 = (bf16[4,48,128]{2,1,0:T(8,128)(2,1)S(1)}, bf16[4,48,128]{2,1,0:T(8,128)(2,1)S(1)}, u32[]{:S(2)}, u32[]{:S(2)}) collective-permute-start(bf16[4,48,128]{2,1,0:T(8,128)(2,1)S(1)} %pad_maximum_fusion.2), channel_id=1, source_target_pairs={{0,16},{4,20},{8,24},{12,28},{16,0},{20,4},{24,8},{28,12},{1,17},{... | collective-permute-start | bytes 147464 | tf_op jit(solution)/shard_map/ppermute | solution.py:39
  52.4 4.7 %collective-permute-start.17 = (bf16[8,48,128]{2,1,0:T(8,128)(2,1)S(1)}, bf16[8,48,128]{2,1,0:T(8,128)(2,1)S(1)}, u32[]{:S(2)}, u32[]{:S(2)}) collective-permute-start(bf16[8,48,128]{2,1,0:T(8,128)(2,1)S(1)} %pad_maximum_fusion.1), channel_id=1, source_target_pairs={{0,8},{4,12},{8,0},{12,4},{16,24},{20,28},{24,16},{28,20},{1,9},{5... | collective-permute-start | bytes 294920 | tf_op jit(solution)/shard_map/ppermute | solution.py:39
  57.2 1.5 %collective-permute-start.18 = (bf16[16,48,128]{2,1,0:T(8,128)(2,1)S(1)}, bf16[16,48,128]{2,1,0:T(8,128)(2,1)S(1)}, u32[]{:S(2)}, u32[]{:S(2)}) collective-permute-start(bf16[16,48,128]{2,1,0:T(8,128)(2,1)S(1)} %get-tuple-element.42), channel_id=1, source_target_pairs={{0,4},{4,0},{8,12},{12,8},{16,20},{20,16},{24,28},{28,24},{1,5},{5... | collective-permute-start | bytes 589832 | tf_op jit(solution)/shard_map/ppermute | solution.py:39

commit v7 on v6

--- a/solution.py
+++ b/solution.py
@@ -189,7 +189,8 @@
     ).astype(half)
     onsite_all[...] = nn(chosen, sides[:, :area])
     raw = nn(chosen, sides[:, area:]).astype(half)
-    source, target = iota((area, LOW * links), 0), iota((area, LOW * links), 1) % links
+    wide = (raw.shape[1], LOW * links)
+    source, target = iota(wide, 0), iota(wide, 1) % links
     spread = jnp.where(source == target, 1.0, jnp.where(source == links + target, 256.0, 0.0)).astype(half)
     ids_all[...] = nn(raw, spread)
     place_copy.wait()
@@ -398,13 +399,13 @@
     def side():
         ids, diagonal = lax.optimization_barrier((neighbor_ids, onsite))
         idents = jnp.concatenate([ids % 256, ids // 256], axis=1).astype(half)
-        return jnp.concatenate([diagonal, jnp.pad(idents, ((0, 0), (0, area - 2 * links)))], axis=1)
+        return jnp.concatenate([diagonal, jnp.pad(idents, ((0, 0), (0, -2 * links % LANES)))], axis=1)
 
     pieces, extras = gather_columns(blocks, side, holders)
     everything = pl.BlockSpec(memory_space=pl.ANY)
     scalars = pl.BlockSpec(memory_space=pltpu.SMEM)
     vectors = pl.BlockSpec(memory_space=pltpu.VMEM)
-    box_rows = (tasks * points // LANES + 1 + 15) // 16 * 16
+    box_rows = tasks * points // LANES + LOW
     density, boxes = pl.pallas_call(
         functools.partial(density_kernel, holders, atoms_here, links),
         in_specs=[scalars] * 4 + [vectors, pl.BlockSpec(memory_space=pltpu.HBM)] + [everything] * (2 * holders),
@@ -415,7 +416,7 @@
         ],
         scratch_shapes=[
             pltpu.VMEM((holders * atoms_here * links, area), half),
-            pltpu.VMEM((holders * atoms_here, 2 * area), half),
+            pltpu.VMEM((holders * atoms_here, area + (2 * links + LANES - 1) // LANES * LANES), half),
             pltpu.VMEM((tasks, order, points), half),
             pltpu.VMEM((tasks * set_size, LOW * links), jnp.float32),
             pltpu.VMEM((tasks * set_size, area), jnp.float32),

time: 62.3 us -> 61.7 us (level)
  no operation moved by 1% of the time
where the time goes in v7:
time: 61.7 us; the launch traced here: 61.2 us
  waiting for transfers between devices  20.7 us (34%)
  starting transfers between devices  20.3 us (33%)
  Pallas kernels  16.6 us (27%)
  other arithmetic  2.64 us (4%)
  between operations  0.79 us (1%)
    pallas_call x1, Pallas kernels, on_device(): pl.pallas_call(functools.partial(density_kernel, holders, atoms_here, lin...  13.5 us
    ppermute x5, waiting for transfers between devices, gather_everywhere(): value = jnp.concatenate([value, lax.ppermute(value, axis, pairs)], axis=0)  10.6 us
    ppermute x5, starting transfers between devices, gather_everywhere(): value = jnp.concatenate([value, lax.ppermute(value, axis, pairs)], axis=0)  7.84 us
    ppermute x2, starting transfers between devices, forward(): lax.ppermute(piece, 'atoms', pair)  5.2 us
    ppermute x4, starting transfers between devices, send(): return [lax.ppermute(part, 'atoms', pair) for pair in ways]  5.15 us
    ppermute x4, waiting for transfers between devices, send(): return [lax.ppermute(part, 'atoms', pair) for pair in ways]  4.6 us
    pallas_call x1, Pallas kernels, on_device(): pl.pallas_call(functools.partial(slab_kernel, tasks), in_specs=[scalars,...  3.09 us
    ppermute x2, waiting for transfers between devices, forward(): lax.ppermute(piece, 'atoms', pair)  2.46 us
  transfers between devices with their start and end apart: 19, of which 10 were waited for; matrix products, arithmetic and copies ran while one was open for 4% of the time, Pallas kernels for 0%

profile of v7, /device:TPU:0, one launch (start us, length us, event | category | flops | bytes accessed | tf_op | source)
XLA Modules:
  0.0 61.2 jit_solution(17487417688571555650)
XLA Ops:
  0.7 0.5 collective-permute-start
  1.2 2.6 %collective-permute-start.1 = (bf16[1024,256]{1,0:T(8,128)(2,1)}, bf16[1024,256]{1,0:T(8,128)(2,1)S(1)}, u32[]{:S(2)}, u32[]{:S(2)}) collective-permute-start(bf16[1024,256]{1,0:T(8,128)(2,1)} %bitcast.10), channel_id=1, source_target_pairs={{0,8},{4,20},{8,0},{12,28},{16,24},{20,4},{24,16},{28,12},{1,9},{5... | collective-permute-start | bytes 1572872 | tf_op jit(solution)/shard_map/ppermute | solution.py:72
  3.8 0.7 %fusion = (bf16[32,32]{1,0:T(8,128)(2,1)S(1)}, bf16[32,32]{1,0:T(8,128)(2,1)S(1)}) fusion(s32[32,32]{1,0:T(8,128)} %param.11), kind=kLoop, calls=%fused_computation.21 | loop fusion | flops 21504 | bytes 8192 | tf_op jit(solution)/shard_map/convert
  4.5 0.1 fusion.6
  4.6 0.7 %pad_maximum_fusion.3.rest_8_ = bf16[32,384]{1,0:T(8,128)(2,1)S(1)} fusion(bf16[32,128]{1,0:T(8,128)(2,1)S(1)} %fusion.6, bf16[32,256]{1,0:T(8,128)(2,1)} %param.10), kind=kLoop, calls=%fused_computation.3 | loop fusion | flops 49152 | bytes 49152 | tf_op jit(solution)/shard_map/concatenate | solution.py:402
  5.3 1.1 %pad_maximum_fusion.rest_0_ = bf16[1056,256]{1,0:T(8,128)(2,1)S(1)} fusion(bf16[32,256]{1,0:T(8,128)(2,1)S(1)} %slice.3, bf16[1024,256]{1,0:T(8,128)(2,1)} %bitcast.11), kind=kLoop, calls=%fused_computation | loop fusion | flops 1081344 | bytes 1081344 | tf_op jit(solution)/shard_map/concatenate | solution.py:83
  6.4 1.6 %collective-permute-start.4 = (bf16[1024,256]{1,0:T(8,128)(2,1)S(1)}, bf16[1024,256]{1,0:T(8,128)(2,1)S(1)}, u32[]{:S(2)}, u32[]{:S(2)}) collective-permute-start(bf16[1024,256]{1,0:T(8,128)(2,1)S(1)} %bitcast.12), channel_id=1, source_target_pairs={{0,16},{4,12},{8,24},{12,4},{16,0},{20,28},{24,8},{28,20},{1,17},{... | collective-permute-start | bytes 1572872 | tf_op jit(solution)/shard_map/ppermute | solution.py:72
  8.0 0.5 collective-permute-start.2
  8.5 0.5 collective-permute-start.3
  9.0 4.1 %collective-permute-done.1.rest_1_ = bf16[1024,256]{1,0:T(8,128)(2,1)S(1)} collective-permute-done((bf16[1024,256]{1,0:T(8,128)(2,1)}, bf16[1024,256]{1,0:T(8,128)(2,1)S(1)}, u32[]{:S(2)}, u32[]{:S(2)}) %collective-permute-start.1) | collective-permute-done | bytes 524320 | tf_op jit(solution)/shard_map/ppermute | solution.py:72
  13.1 3.5 %collective-permute-start.5 = (bf16[1024,256]{1,0:T(8,128)(2,1)S(1)}, bf16[1024,256]{1,0:T(8,128)(2,1)S(1)}, u32[]{:S(2)}, u32[]{:S(2)}) collective-permute-start(bf16[1024,256]{1,0:T(8,128)(2,1)S(1)} %collective-permute-done.1.rest_1_), channel_id=1, source_target_pairs={{0,16},{4,12},{8,24},{12,4},{16,0},{20,28},{24,8},{28,20},{1,17},{... | collective-permute-start | bytes 1572872 | tf_op jit(solution)/shard_map/ppermute | solution.py:77
  16.6 0.5 collective-permute-done.3.rest_10_
  17.1 0.1 collective-permute-start.7
  17.2 0.4 collective-permute-start.8
  17.6 0.1 collective-permute-start.9
  17.7 0.4 collective-permute-start.10
  18.1 1.7 %collective-permute-done.9.rest_12_ = bf16[32,384]{1,0:T(8,128)(2,1)S(1)} collective-permute-done((bf16[32,384]{1,0:T(8,128)(2,1)S(1)}, bf16[32,384]{1,0:T(8,128)(2,1)S(1)}, u32[]{:S(2)}, u32[]{:S(2)}) %collective-permute-start.9) | collective-permute-done | bytes 24608 | tf_op jit(solution)/shard_map/ppermute | solution.py:92
  19.8 1.7 %collective-permute-start.6 = (bf16[32,384]{1,0:T(8,128)(2,1)S(1)}, bf16[32,384]{1,0:T(8,128)(2,1)S(1)}, u32[]{:S(2)}, u32[]{:S(2)}) collective-permute-start(bf16[32,384]{1,0:T(8,128)(2,1)S(1)} %collective-permute-done.2.rest_9_), channel_id=1, source_target_pairs={{0,16},{4,12},{8,24},{12,4},{16,0},{20,28},{24,8},{28,20},{1,17},{... | collective-permute-start | bytes 73736 | tf_op jit(solution)/shard_map/ppermute | solution.py:77
  21.6 2.5 %collective-permute-done.6.rest_11_ = bf16[32,384]{1,0:T(8,128)(2,1)S(1)} collective-permute-done((bf16[32,384]{1,0:T(8,128)(2,1)S(1)}, bf16[32,384]{1,0:T(8,128)(2,1)S(1)}, u32[]{:S(2)}, u32[]{:S(2)}) %collective-permute-start.6) | collective-permute-done | bytes 24608 | tf_op jit(solution)/shard_map/ppermute | solution.py:77
  24.1 0.5 collective-permute-start.13
  24.6 1.4 %collective-permute-done.13.rest_15_ = bf16[32,384]{1,0:T(8,128)(2,1)S(1)} collective-permute-done((bf16[32,384]{1,0:T(8,128)(2,1)S(1)}, bf16[32,384]{1,0:T(8,128)(2,1)S(1)}, u32[]{:S(2)}, u32[]{:S(2)}) %collective-permute-start.13) | collective-permute-done | bytes 24608 | tf_op jit(solution)/shard_map/ppermute | solution.py:98
  26.1 13.5 %shard_map.104 = (bf16[4,512,128]{2,1,0:T(8,128)(2,1)}, bf16[40,128]{1,0:T(8,128)(2,1)S(1)}) custom-call(f32[4]{0:T(128)S(1)} %copy-done.1, s32[4]{0:T(128)S(1)} %copy-done.2, s32[4]{0:T(128)S(1)} %copy-done.3, s32[4]{0:T(128)S(1)} %copy-done.4, s32[4,32]{1,0:T(4,128)S(1)} %copy-done, bf16[4,512,1024]{2,1,0:T(8,128)(2,1)} %basis_hbm.1, ...), custom_call_target="tpu_custom_call" | custom-call | tf_op jit(solution)/shard_map/pallas_call | solution.py:409
  39.6 2.6 %collective-permute-start.14 = (bf16[1,40,128]{2,1,0:T(8,128)(2,1)S(1)}, bf16[1,40,128]{2,1,0:T(8,128)(2,1)S(1)}, u32[]{:S(2)}, u32[]{:S(2)}) collective-permute-start(bf16[1,40,128]{2,1,0:T(8,128)(2,1)S(1)} %bitcast.5), channel_id=1, source_target_pairs={{0,2},{1,3},{2,0},{3,1},{4,6},{5,7},{6,4},{7,5},{8,10},{9,11},{10,... | collective-permute-start | bytes 30728 | tf_op jit(solution)/shard_map/ppermute | solution.py:39
  42.2 2.0 %collective-permute-done.14 = bf16[1,40,128]{2,1,0:T(8,128)(2,1)S(1)} collective-permute-done((bf16[1,40,128]{2,1,0:T(8,128)(2,1)S(1)}, bf16[1,40,128]{2,1,0:T(8,128)(2,1)S(1)}, u32[]{:S(2)}, u32[]{:S(2)}) %collective-permute-start.14) | collective-permute-done | bytes 10272 | tf_op jit(solution)/shard_map/ppermute | solution.py:39
  44.2 1.5 %collective-permute-start.15 = (bf16[2,40,128]{2,1,0:T(8,128)(2,1)S(1)}, bf16[2,40,128]{2,1,0:T(8,128)(2,1)S(1)}, u32[]{:S(2)}, u32[]{:S(2)}) collective-permute-start(bf16[2,40,128]{2,1,0:T(8,128)(2,1)S(1)} %pad_maximum_fusion.4), channel_id=1, source_target_pairs={{0,1},{1,0},{2,3},{3,2},{4,5},{5,4},{6,7},{7,6},{8,9},{9,8},{10,11... | collective-permute-start | bytes 61448 | tf_op jit(solution)/shard_map/ppermute | solution.py:39
  45.8 2.2 %collective-permute-done.15 = bf16[2,40,128]{2,1,0:T(8,128)(2,1)S(1)} collective-permute-done((bf16[2,40,128]{2,1,0:T(8,128)(2,1)S(1)}, bf16[2,40,128]{2,1,0:T(8,128)(2,1)S(1)}, u32[]{:S(2)}, u32[]{:S(2)}) %collective-permute-start.15) | collective-permute-done | bytes 20512 | tf_op jit(solution)/shard_map/ppermute | solution.py:39
  48.0 2.1 %collective-permute-start.16 = (bf16[4,40,128]{2,1,0:T(8,128)(2,1)S(1)}, bf16[4,40,128]{2,1,0:T(8,128)(2,1)S(1)}, u32[]{:S(2)}, u32[]{:S(2)}) collective-permute-start(bf16[4,40,128]{2,1,0:T(8,128)(2,1)S(1)} %pad_maximum_fusion.2), channel_id=1, source_target_pairs={{0,16},{4,20},{8,24},{12,28},{16,0},{20,4},{24,8},{28,12},{1,17},{... | collective-permute-start | bytes 122888 | tf_op jit(solution)/shard_map/ppermute | solution.py:39
  50.1 2.0 %collective-permute-done.16 = bf16[4,40,128]{2,1,0:T(8,128)(2,1)S(1)} collective-permute-done((bf16[4,40,128]{2,1,0:T(8,128)(2,1)S(1)}, bf16[4,40,128]{2,1,0:T(8,128)(2,1)S(1)}, u32[]{:S(2)}, u32[]{:S(2)}) %collective-permute-start.16) | collective-permute-done | bytes 40992 | tf_op jit(solution)/shard_map/ppermute | solution.py:39
  52.1 1.5 %collective-permute-start.17 = (bf16[8,40,128]{2,1,0:T(8,128)(2,1)S(1)}, bf16[8,40,128]{2,1,0:T(8,128)(2,1)S(1)}, u32[]{:S(2)}, u32[]{:S(2)}) collective-permute-start(bf16[8,40,128]{2,1,0:T(8,128)(2,1)S(1)} %pad_maximum_fusion.1), channel_id=1, source_target_pairs={{0,8},{4,12},{8,0},{12,4},{16,24},{20,28},{24,16},{28,20},{1,9},{5... | collective-permute-start | bytes 245768 | tf_op jit(solution)/shard_map/ppermute | solution.py:39
  53.6 3.0 %collective-permute-done.17 = bf16[8,40,128]{2,1,0:T(8,128)(2,1)S(1)} collective-permute-done((bf16[8,40,128]{2,1,0:T(8,128)(2,1)S(1)}, bf16[8,40,128]{2,1,0:T(8,128)(2,1)S(1)}, u32[]{:S(2)}, u32[]{:S(2)}) %collective-permute-start.17) | collective-permute-done | bytes 81952 | tf_op jit(solution)/shard_map/ppermute | solution.py:39
  56.7 1.4 %collective-permute-done.18 = bf16[16,40,128]{2,1,0:T(8,128)(2,1)S(1)} collective-permute-done((bf16[16,40,128]{2,1,0:T(8,128)(2,1)S(1)}, bf16[16,40,128]{2,1,0:T(8,128)(2,1)S(1)}, u32[]{:S(2)}, u32[]{:S(2)}) %collective-permute-start.18) | collective-permute-done | bytes 163872 | tf_op jit(solution)/shard_map/ppermute | solution.py:39
  58.1 3.1 %shard_map.105 = f32[64,32,128]{2,1,0:T(8,128)} custom-call(s32[1]{0:T(128)} %bitcast.1.slab_number_ref, bf16[32,40,128]{2,1,0:T(8,128)(2,1)S(1)} %constant_dynamic-update-slice_fusion.5.boxes_ref), custom_call_target="tpu_custom_call" | custom-call | tf_op jit(solution)/shard_map/pallas_call | solution.py:444
  (34 shorter events, 0.4 us)
Async XLA Ops:
  0.6 5.8 %copy-start.5 = (bf16[32,32,256]{2,1,0:T(8,128)(2,1)S(1)}, bf16[32,32,256]{2,1,0:T(8,128)(2,1)}, u32[]{:S(2)}) copy-start(bf16[32,32,256]{2,1,0:T(8,128)(2,1)} %param.9) | copy-start | bytes 1572868
  0.6 25.4 %copy-start = (s32[4,32]{1,0:T(4,128)S(1)}, s32[4,32]{1,0:T(4,128)}, u32[]{:S(2)}) copy-start(s32[4,32]{1,0:T(4,128)} %members_ref.1) | copy-start | bytes 1540
  0.7 25.4 %copy-start.1 = (f32[4]{0:T(128)S(1)}, f32[4]{0:T(128)}, u32[]{:S(2)}) copy-start(f32[4]{0:T(128)} %shift_ref.1) | copy-start | bytes 52
  0.7 25.4 %copy-start.2 = (s32[4]{0:T(128)S(1)}, s32[4]{0:T(128)}, u32[]{:S(2)}) copy-start(s32[4]{0:T(128)} %start_ref.1) | copy-start | bytes 52
  0.7 25.4 %copy-start.3 = (s32[4]{0:T(128)S(1)}, s32[4]{0:T(128)}, u32[]{:S(2)}) copy-start(s32[4]{0:T(128)} %row_ref.1) | copy-start | bytes 52
  0.7 25.4 %copy-start.4 = (s32[4]{0:T(128)S(1)}, s32[4]{0:T(128)}, u32[]{:S(2)}) copy-start(s32[4]{0:T(128)} %col_ref.1) | copy-start | bytes 52
  0.7 4.6 %collective-permute-start = (bf16[1024,256]{1,0:T(8,128)(2,1)}, bf16[1024,256]{1,0:T(8,128)(2,1)S(1)}, u32[]{:S(2)}, u32[]{:S(2)}) collective-permute-start(bf16[1024,256]{1,0:T(8,128)(2,1)} %bitcast.9), channel_id=1, source_target_pairs={{0,4},{4,0},{8,12},{12,8},{16,20},{20,16},{24,28},{28,24},{1,5},{5... | collective-permute-start | bytes 1572872 | tf_op jit(solution)/shard_map/ppermute | solution.py:81
  1.2 11.9 %collective-permute-start.1 = (bf16[1024,256]{1,0:T(8,128)(2,1)}, bf16[1024,256]{1,0:T(8,128)(2,1)S(1)}, u32[]{:S(2)}, u32[]{:S(2)}) collective-permute-start(bf16[1024,256]{1,0:T(8,128)(2,1)} %bitcast.10), channel_id=1, source_target_pairs={{0,8},{4,20},{8,0},{12,28},{16,24},{20,4},{24,16},{28,12},{1,9},{5... | collective-permute-start | bytes 1572872 | tf_op jit(solution)/shard_map/ppermute | solution.py:72
  6.4 10.8 %collective-permute-start.4 = (bf16[1024,256]{1,0:T(8,128)(2,1)S(1)}, bf16[1024,256]{1,0:T(8,128)(2,1)S(1)}, u32[]{:S(2)}, u32[]{:S(2)}) collective-permute-start(bf16[1024,256]{1,0:T(8,128)(2,1)S(1)} %bitcast.12), channel_id=1, source_target_pairs={{0,16},{4,12},{8,24},{12,4},{16,0},{20,28},{24,8},{28,20},{1,17},{... | collective-permute-start | bytes 1572872 | tf_op jit(solution)/shard_map/ppermute | solution.py:72
  8.0 8.6 %collective-permute-start.2 = (bf16[32,384]{1,0:T(8,128)(2,1)S(1)}, bf16[32,384]{1,0:T(8,128)(2,1)S(1)}, u32[]{:S(2)}, u32[]{:S(2)}) collective-permute-start(bf16[32,384]{1,0:T(8,128)(2,1)S(1)} %pad_maximum_fusion.3.rest_8_), channel_id=1, source_target_pairs={{0,8},{4,20},{8,0},{12,28},{16,24},{20,4},{24,16},{28,12},{1,9},{5... | collective-permute-start | bytes 73736 | tf_op jit(solution)/shard_map/ppermute | solution.py:72
  8.5 8.5 %collective-permute-start.3 = (bf16[32,384]{1,0:T(8,128)(2,1)S(1)}, bf16[32,384]{1,0:T(8,128)(2,1)S(1)}, u32[]{:S(2)}, u32[]{:S(2)}) collective-permute-start(bf16[32,384]{1,0:T(8,128)(2,1)S(1)} %pad_maximum_fusion.3.rest_8_), channel_id=1, source_target_pairs={{0,16},{4,12},{8,24},{12,4},{16,0},{20,28},{24,8},{28,20},{1,17},{... | collective-permute-start | bytes 73736 | tf_op jit(solution)/shard_map/ppermute | solution.py:72
  13.1 10.9 %collective-permute-start.5 = (bf16[1024,256]{1,0:T(8,128)(2,1)S(1)}, bf16[1024,256]{1,0:T(8,128)(2,1)S(1)}, u32[]{:S(2)}, u32[]{:S(2)}) collective-permute-start(bf16[1024,256]{1,0:T(8,128)(2,1)S(1)} %collective-permute-done.1.rest_1_), channel_id=1, source_target_pairs={{0,16},{4,12},{8,24},{12,4},{16,0},{20,28},{24,8},{28,20},{1,17},{... | collective-permute-start | bytes 1572872 | tf_op jit(solution)/shard_map/ppermute | solution.py:77
  17.1 7.0 %collective-permute-start.7 = (bf16[1024,256]{1,0:T(8,128)(2,1)S(1)}, bf16[1024,256]{1,0:T(8,128)(2,1)S(1)}, u32[]{:S(2)}, u32[]{:S(2)}) collective-permute-start(bf16[1024,256]{1,0:T(8,128)(2,1)S(1)} %collective-permute-done.1.rest_1_), channel_id=1, source_target_pairs={{0,4},{4,0},{8,12},{12,8},{16,20},{20,16},{24,28},{28,24},{1,5},{5... | collective-permute-start | bytes 1572872 | tf_op jit(solution)/shard_map/ppermute | solution.py:91
  17.2 6.9 %collective-permute-start.8 = (bf16[1024,256]{1,0:T(8,128)(2,1)S(1)}, bf16[1024,256]{1,0:T(8,128)(2,1)S(1)}, u32[]{:S(2)}, u32[]{:S(2)}) collective-permute-start(bf16[1024,256]{1,0:T(8,128)(2,1)S(1)} %collective-permute-done.4.rest_2_), channel_id=1, source_target_pairs={{0,4},{4,0},{8,12},{12,8},{16,20},{20,16},{24,28},{28,24},{1,5},{5... | collective-permute-start | bytes 1572872 | tf_op jit(solution)/shard_map/ppermute | solution.py:91
  17.6 2.2 %collective-permute-start.9 = (bf16[32,384]{1,0:T(8,128)(2,1)S(1)}, bf16[32,384]{1,0:T(8,128)(2,1)S(1)}, u32[]{:S(2)}, u32[]{:S(2)}) collective-permute-start(bf16[32,384]{1,0:T(8,128)(2,1)S(1)} %pad_maximum_fusion.3.rest_8_), channel_id=1, source_target_pairs={{0,4},{4,0},{8,12},{12,8},{16,20},{20,16},{24,28},{28,24},{1,5},{5... | collective-permute-start | bytes 73736 | tf_op jit(solution)/shard_map/ppermute | solution.py:92
  17.7 3.8 %collective-permute-start.10 = (bf16[32,384]{1,0:T(8,128)(2,1)S(1)}, bf16[32,384]{1,0:T(8,128)(2,1)S(1)}, u32[]{:S(2)}, u32[]{:S(2)}) collective-permute-start(bf16[32,384]{1,0:T(8,128)(2,1)S(1)} %collective-permute-done.2.rest_9_), channel_id=1, source_target_pairs={{0,4},{4,0},{8,12},{12,8},{16,20},{20,16},{24,28},{28,24},{1,5},{5... | collective-permute-start | bytes 73736 | tf_op jit(solution)/shard_map/ppermute | solution.py:92
  19.8 4.3 %collective-permute-start.6 = (bf16[32,384]{1,0:T(8,128)(2,1)S(1)}, bf16[32,384]{1,0:T(8,128)(2,1)S(1)}, u32[]{:S(2)}, u32[]{:S(2)}) collective-permute-start(bf16[32,384]{1,0:T(8,128)(2,1)S(1)} %collective-permute-done.2.rest_9_), channel_id=1, source_target_pairs={{0,16},{4,12},{8,24},{12,4},{16,0},{20,28},{24,8},{28,20},{1,17},{... | collective-permute-start | bytes 73736 | tf_op jit(solution)/shard_map/ppermute | solution.py:77
  21.5 2.5 %collective-permute-start.11 = (bf16[32,384]{1,0:T(8,128)(2,1)S(1)}, bf16[32,384]{1,0:T(8,128)(2,1)S(1)}, u32[]{:S(2)}, u32[]{:S(2)}) collective-permute-start(bf16[32,384]{1,0:T(8,128)(2,1)S(1)} %collective-permute-done.3.rest_10_), channel_id=1, source_target_pairs={{0,4},{4,0},{8,12},{12,8},{16,20},{20,16},{24,28},{28,24},{1,5},{5... | collective-permute-start | bytes 73736 | tf_op jit(solution)/shard_map/ppermute | solution.py:92
  24.0 2.0 %collective-permute-start.12 = (bf16[1024,256]{1,0:T(8,128)(2,1)S(1)}, bf16[1024,256]{1,0:T(8,128)(2,1)S(1)}, u32[]{:S(2)}, u32[]{:S(2)}) collective-permute-start(bf16[1024,256]{1,0:T(8,128)(2,1)S(1)} %collective-permute-done.5.rest_3_), channel_id=1, source_target_pairs={{0,4},{4,0},{8,12},{12,8},{16,20},{20,16},{24,28},{28,24},{1,5},{5... | collective-permute-start | bytes 1572872 | tf_op jit(solution)/shard_map/ppermute | solution.py:97
  24.1 1.9 %collective-permute-start.13 = (bf16[32,384]{1,0:T(8,128)(2,1)S(1)}, bf16[32,384]{1,0:T(8,128)(2,1)S(1)}, u32[]{:S(2)}, u32[]{:S(2)}) collective-permute-start(bf16[32,384]{1,0:T(8,128)(2,1)S(1)} %collective-permute-done.6.rest_11_), channel_id=1, source_target_pairs={{0,4},{4,0},{8,12},{12,8},{16,20},{20,16},{24,28},{28,24},{1,5},{5... | collective-permute-start | bytes 73736 | tf_op jit(solution)/shard_map/ppermute | solution.py:98
  39.6 4.6 %collective-permute-start.14 = (bf16[1,40,128]{2,1,0:T(8,128)(2,1)S(1)}, bf16[1,40,128]{2,1,0:T(8,128)(2,1)S(1)}, u32[]{:S(2)}, u32[]{:S(2)}) collective-permute-start(bf16[1,40,128]{2,1,0:T(8,128)(2,1)S(1)} %bitcast.5), channel_id=1, source_target_pairs={{0,2},{1,3},{2,0},{3,1},{4,6},{5,7},{6,4},{7,5},{8,10},{9,11},{10,... | collective-permute-start | bytes 30728 | tf_op jit(solution)/shard_map/ppermute | solution.py:39
  44.2 3.8 %collective-permute-start.15 = (bf16[2,40,128]{2,1,0:T(8,128)(2,1)S(1)}, bf16[2,40,128]{2,1,0:T(8,128)(2,1)S(1)}, u32[]{:S(2)}, u32[]{:S(2)}) collective-permute-start(bf16[2,40,128]{2,1,0:T(8,128)(2,1)S(1)} %pad_maximum_fusion.4), channel_id=1, source_target_pairs={{0,1},{1,0},{2,3},{3,2},{4,5},{5,4},{6,7},{7,6},{8,9},{9,8},{10,11... | collective-permute-start | bytes 61448 | tf_op jit(solution)/shard_map/ppermute | solution.py:39
  48.0 4.1 %collective-permute-start.16 = (bf16[4,40,128]{2,1,0:T(8,128)(2,1)S(1)}, bf16[4,40,128]{2,1,0:T(8,128)(2,1)S(1)}, u32[]{:S(2)}, u32[]{:S(2)}) collective-permute-start(bf16[4,40,128]{2,1,0:T(8,128)(2,1)S(1)} %pad_maximum_fusion.2), channel_id=1, source_target_pairs={{0,16},{4,20},{8,24},{12,28},{16,0},{20,4},{24,8},{28,12},{1,17},{... | collective-permute-start | bytes 122888 | tf_op jit(solution)/shard_map/ppermute | solution.py:39
  52.1 4.5 %collective-permute-start.17 = (bf16[8,40,128]{2,1,0:T(8,128)(2,1)S(1)}, bf16[8,40,128]{2,1,0:T(8,128)(2,1)S(1)}, u32[]{:S(2)}, u32[]{:S(2)}) collective-permute-start(bf16[8,40,128]{2,1,0:T(8,128)(2,1)S(1)} %pad_maximum_fusion.1), channel_id=1, source_target_pairs={{0,8},{4,12},{8,0},{12,4},{16,24},{20,28},{24,16},{28,20},{1,9},{5... | collective-permute-start | bytes 245768 | tf_op jit(solution)/shard_map/ppermute | solution.py:39
  56.6 1.5 %collective-permute-start.18 = (bf16[16,40,128]{2,1,0:T(8,128)(2,1)S(1)}, bf16[16,40,128]{2,1,0:T(8,128)(2,1)S(1)}, u32[]{:S(2)}, u32[]{:S(2)}) collective-permute-start(bf16[16,40,128]{2,1,0:T(8,128)(2,1)S(1)} %get-tuple-element.42), channel_id=1, source_target_pairs={{0,4},{4,0},{8,12},{12,8},{16,20},{20,16},{24,28},{28,24},{1,5},{5... | collective-permute-start | bytes 491528 | tf_op jit(solution)/shard_map/ppermute | solution.py:39
